TPU v7x, 32 devices: a whole 2x2x4 slice. The times are simulated.
32 devices in a mesh: dp: 2 (over x), depth: 4 (over y, core), wide: 4 (over z).
Axes of the slice: x: 2, y: 2, z: 4, core: 2. Of those that a mesh axis runs over, the one named last changes fastest.
Arguments:
- voxels: bfloat16 [16, 16, 64, 32, 192], P('dp', 'depth', None, 'wide'), may hold values from -6 to 6
- cotangent: bfloat16 [16, 16, 64, 32, 192], P('dp', 'depth', None, 'wide'), may hold values from -45 to 45
- project_in: float32 [192, 576], replicated, may hold values from -0.4375 to 0.4375
- project_out: float32 [192, 192], replicated, may hold values from -1.25 to 1.25
- expand: float32 [192, 768], replicated, may hold values from -0.4375 to 0.4375
- contract: float32 [768, 192], replicated, may hold values from -0.21875 to 0.21875
- bias_table: float32 [6, 343], replicated, may hold values from -4 to 4
- vectors: float32 [2304], replicated, may hold values from -0.8 to 1.3
- project_in_first: float32 [192, 576], replicated, may hold values from -1 to 1
- project_out_first: float32 [192, 192], replicated, may hold values from -1 to 1
- expand_first: float32 [192, 768], replicated, may hold values from -1 to 1
- contract_first: float32 [768, 192], replicated, may hold values from -1 to 1
- bias_table_first: float32 [6, 343], replicated, may hold values from -1 to 1
- vectors_first: float32 [2304], replicated, may hold values from -4 to 4
- project_in_second: float32 [192, 576], replicated, may hold values from 0.0022384885 to 0.008953954
- project_out_second: float32 [192, 192], replicated, may hold values from 0.0022384885 to 0.008953954
- expand_second: float32 [192, 768], replicated, may hold values from 0.0022384885 to 0.008953954
- contract_second: float32 [768, 192], replicated, may hold values from 0.0022384885 to 0.008953954
- bias_table_second: float32 [6, 343], replicated, may hold values from 0.0022384885 to 0.008953954
- vectors_second: float32 [2304], replicated, may hold values from 0.035815816 to 0.14326327
Outputs:
- layer_out: bfloat16 [16, 16, 64, 32, 192], P('dp', 'depth', None, 'wide')
- voxel_grad: bfloat16 [16, 16, 64, 32, 192], P('dp', 'depth', None, 'wide')
- project_in_grad: float32 [192, 576], replicated
- project_in_first_new: float32 [192, 576], replicated
- project_in_second_new: float32 [192, 576], replicated
- project_in_next: float32 [192, 576], replicated
- project_out_grad: float32 [192, 192], replicated
- project_out_first_new: float32 [192, 192], replicated
- project_out_second_new: float32 [192, 192], replicated
- project_out_next: float32 [192, 192], replicated
- expand_grad: float32 [192, 768], replicated
- expand_first_new: float32 [192, 768], replicated
- expand_second_new: float32 [192, 768], replicated
- expand_next: float32 [192, 768], replicated
- contract_grad: float32 [768, 192], replicated
- contract_first_new: float32 [768, 192], replicated
- contract_second_new: float32 [768, 192], replicated
- contract_next: float32 [768, 192], replicated
- bias_table_grad: float32 [6, 343], replicated
- bias_table_first_new: float32 [6, 343], replicated
- bias_table_second_new: float32 [6, 343], replicated
- bias_table_next: float32 [6, 343], replicated
- vectors_grad: float32 [2304], replicated
- vectors_first_new: float32 [2304], replicated
- vectors_second_new: float32 [2304], replicated
- vectors_next: float32 [2304], replicated
- project_in_copy: bfloat16 [192, 576], replicated
- project_out_copy: bfloat16 [192, 192], replicated
- expand_copy: bfloat16 [192, 768], replicated
- contract_copy: bfloat16 [768, 192], replicated
- grad_norm: float32 [], replicated
All inputs are finite; a program needn't handle non-finite values.
Results may differ from a plain program's by a relative error of at most 0.012.
The roundings to bfloat16 on the way count: a program that leaves them out, or rounds other values in their place, can miss the bound.
Values may be sent and summed in bfloat16 or wider, within the bound.
A program may use at most 512 MiB of HBM per device.

v0:
```python
from functools import partial

import jax
import jax.numpy as jnp
import numpy as np
from jax import lax
from jax.sharding import PartitionSpec as P

HEADS = 6
WIN = 4
SHIFT = 2
STEP = 10


norm_eps = 1e-05
mask_fill = -100.0
clip_bound = 1000.0
rate_matrix = 0.1
rate_vector = 0.6
weight_decay = 0.01
beta_first = 0.9
beta_second = 0.999
adam_eps = 1e-08


def from_behind(value, axis, by):
    peers = lax.axis_size(axis)
    return lax.ppermute(value, axis, [(i, (i + by) % peers) for i in range(peers)])


def relative_index():
    extent = 2 * WIN - 1
    corner = np.arange(WIN)
    places = np.stack(np.meshgrid(corner, corner, corner, indexing="ij"), -1).reshape(-1, 3)
    offsets = places[:, None, :] - places[None, :, :] + WIN - 1
    return (offsets[..., 0] * extent + offsets[..., 1]) * extent + offsets[..., 2]


def region_labels(count, start, length):
    places = start + jnp.arange(count, dtype=jnp.int32)
    return (places >= length - WIN).astype(jnp.int32) + (places >= length - SHIFT).astype(jnp.int32)


def window_split(tensor):
    batches, planes, height, breadth, feature = tensor.shape
    tensor = tensor.reshape(
        batches, planes // WIN, WIN, height // WIN, WIN, breadth // WIN, WIN, feature
    )
    tensor = tensor.transpose(0, 1, 3, 5, 2, 4, 6, 7)
    return tensor.reshape(-1, WIN**3, feature)


def window_join(tensor, batches, planes, height, breadth):
    feature = tensor.shape[-1]
    tensor = tensor.reshape(
        batches, planes // WIN, height // WIN, breadth // WIN, WIN, WIN, WIN, feature
    )
    tensor = tensor.transpose(0, 1, 4, 2, 5, 3, 6, 7)
    return tensor.reshape(batches, planes, height, breadth, feature)


def layer_norm(tensor, gain, offset):
    centred = tensor - jnp.mean(tensor, -1, keepdims=True)
    inverse = lax.rsqrt(jnp.mean(centred * centred, -1, keepdims=True) + norm_eps)
    unit_vals = centred * inverse
    return (unit_vals * gain + offset, unit_vals, inverse)


def norm_back(grad_out, unit_vals, inverse, gain):
    scaled = grad_out * gain
    inner = jnp.mean(scaled, -1, keepdims=True)
    along = jnp.mean(scaled * unit_vals, -1, keepdims=True)
    grad_in = inverse * (scaled - inner - unit_vals * along)
    return (grad_in, jnp.sum(grad_out * unit_vals, (0, 1)), jnp.sum(grad_out, (0, 1)))


def adam_update(weight, first, second, gradient, rate, decay):
    first_new = beta_first * first + (1.0 - beta_first) * gradient
    second_new = beta_second * second + (1.0 - beta_second) * gradient * gradient
    first_hat = first_new / (1.0 - beta_first**STEP)
    second_hat = second_new / (1.0 - beta_second**STEP)
    weight_new = weight - rate * (first_hat / (jnp.sqrt(second_hat) + adam_eps) + decay * weight)
    return (first_new, second_new, weight_new)


def whole_update(totals, weights, firsts, seconds, rates, decays):
    squares = jnp.float32(0.0)
    for member in totals:
        squares = squares + jnp.sum(member * member)
    norm_value = jnp.sqrt(squares)
    factor = jnp.minimum(1.0, clip_bound / (norm_value + 1e-06))
    outputs = []
    for member in range(6):
        clipped = totals[member] * factor
        outputs.append(
            (clipped,)
            + adam_update(
                weights[member],
                firsts[member],
                seconds[member],
                clipped,
                rates[member],
                decays[member],
            )
        )
    return (outputs, norm_value)


def local(
    voxels,
    cotangent,
    project_in,
    project_out,
    expand,
    contract,
    bias_table,
    vectors,
    project_in_first,
    project_out_first,
    expand_first,
    contract_first,
    bias_table_first,
    vectors_first,
    project_in_second,
    project_out_second,
    expand_second,
    contract_second,
    bias_table_second,
    vectors_second,
):
    batches, planes, height, breadth, width = voxels.shape
    heads = HEADS
    head_width = width // heads
    window_size = WIN**3
    scale = head_width ** (-0.5)
    bf = jnp.bfloat16
    fl = jnp.float32
    paired = jnp.stack([voxels, cotangent])
    arrived = from_behind(paired[:, :, :SHIFT], "depth", -1)
    paired = jnp.concatenate([paired[:, :, SHIFT:], arrived], 2)
    arrived = from_behind(paired[:, :, :, :, :SHIFT], "wide", -1)
    paired = jnp.concatenate([paired[:, :, :, :, SHIFT:], arrived], 4)
    paired = jnp.roll(paired, -SHIFT, 3)
    tokens = window_split(paired[0]).astype(fl)
    upstream_low = window_split(paired[1])
    upstream = upstream_low.astype(fl)
    windows = tokens.shape[0]
    plane_labels = region_labels(
        planes, lax.axis_index("depth") * planes, planes * lax.axis_size("depth")
    )
    height_labels = region_labels(height, 0, height)
    column_labels = region_labels(
        breadth, lax.axis_index("wide") * breadth, breadth * lax.axis_size("wide")
    )
    labels = (
        plane_labels[:, None, None] * 9
        + height_labels[None, :, None] * 3
        + column_labels[None, None, :]
    )
    labels = jnp.broadcast_to(labels[None, :, :, :, None], (batches, planes, height, breadth, 1))
    labels = window_split(labels)[..., 0]
    masks = jnp.where(labels[:, :, None] == labels[:, None, :], 0.0, mask_fill).astype(fl)
    extent = (2 * WIN - 1) ** 3
    selector = (
        jnp.asarray(relative_index().reshape(-1), jnp.int32)[:, None]
        == jnp.arange(extent, dtype=jnp.int32)[None, :]
    ).astype(fl)
    pair_bias = jnp.einsum("hr,pr->hp", bias_table, selector, precision=lax.Precision.HIGHEST)
    pair_bias = pair_bias.reshape(heads, window_size, window_size)
    members = [vectors[member * width : (member + 1) * width] for member in range(8)]
    gain_one, shift_one, query_bias, value_bias, out_bias, gain_two, shift_two, contract_bias = (
        members
    )
    expand_bias = vectors[8 * width :]
    in_low = project_in.astype(bf)
    out_low = project_out.astype(bf)
    expand_low = expand.astype(bf)
    contract_low = contract.astype(bf)
    normed_one, unit_one, inverse_one = layer_norm(tokens, gain_one, shift_one)
    entry_one = normed_one.astype(bf)
    in_bias = jnp.concatenate([query_bias, jnp.zeros((width,), fl), value_bias])
    triple = (
        jnp.einsum("wtc,cf->wtf", entry_one, in_low, preferred_element_type=fl) + in_bias
    ).astype(bf)
    query = triple[..., :width].reshape(windows, window_size, heads, head_width)
    keys = triple[..., width : 2 * width].reshape(windows, window_size, heads, head_width)
    values = triple[..., 2 * width :].reshape(windows, window_size, heads, head_width)

    def attend_scores():
        raw_scores = jnp.einsum("wihd,wjhd->whij", query, keys, preferred_element_type=fl) * scale
        return raw_scores + pair_bias[None] + masks[:, None]

    scores = attend_scores()
    peak = jnp.max(scores, -1, keepdims=True)
    expo = jnp.exp(scores - peak)
    totals_row = jnp.sum(expo, -1, keepdims=True)
    probs = expo / totals_row
    logsum = peak + jnp.log(totals_row)
    mixed = jnp.einsum("whij,wjhd->wihd", probs.astype(bf), values, preferred_element_type=fl)
    mixed = mixed.reshape(windows, window_size, width).astype(bf)
    middle = (
        tokens + jnp.einsum("wtc,cf->wtf", mixed, out_low, preferred_element_type=fl) + out_bias
    )
    normed_two, unit_two, inverse_two = layer_norm(middle, gain_two, shift_two)
    entry_two = normed_two.astype(bf)
    hidden = (
        jnp.einsum("wtc,cf->wtf", entry_two, expand_low, preferred_element_type=fl) + expand_bias
    )
    active, gelu_pull = jax.vjp(partial(jax.nn.gelu, approximate=False), hidden)
    active_low = active.astype(bf)
    result = (
        middle
        + jnp.einsum("wtf,fc->wtc", active_low, contract_low, preferred_element_type=fl)
        + contract_bias
    )
    contract_grad = jnp.einsum("wtf,wtc->fc", active_low, upstream_low, preferred_element_type=fl)
    contract_bias_grad = jnp.sum(upstream, (0, 1))
    active_grad = jnp.einsum("wtc,fc->wtf", upstream_low, contract_low, preferred_element_type=fl)
    hidden_low = gelu_pull(active_grad)[0].astype(bf)
    expand_bias_grad = jnp.sum(hidden_low.astype(fl), (0, 1))
    expand_grad = jnp.einsum("wtc,wtf->cf", entry_two, hidden_low, preferred_element_type=fl)
    normed_two_grad = jnp.einsum("wtf,cf->wtc", hidden_low, expand_low, preferred_element_type=fl)
    middle_grad, gain_two_grad, shift_two_grad = norm_back(
        normed_two_grad, unit_two, inverse_two, gain_two
    )
    middle_grad = middle_grad + upstream
    branch_low = middle_grad.astype(bf)
    out_bias_grad = jnp.sum(branch_low.astype(fl), (0, 1))
    project_out_grad = jnp.einsum("wtc,wtf->cf", mixed, branch_low, preferred_element_type=fl)
    mixed_low = jnp.einsum("wtf,cf->wtc", branch_low, out_low, preferred_element_type=fl).astype(bf)
    mixed_low = mixed_low.reshape(windows, window_size, heads, head_width)
    probs_again = jnp.exp(attend_scores() - logsum)
    prob_grad = jnp.einsum("wihd,wjhd->whij", mixed_low, values, preferred_element_type=fl)
    score_low = (
        probs_again * (prob_grad - jnp.sum(prob_grad * probs_again, -1, keepdims=True))
    ).astype(bf)
    table_grad = jnp.einsum(
        "hp,pr->hr",
        jnp.sum(score_low.astype(fl), 0).reshape(heads, -1),
        selector,
        precision=lax.Precision.HIGHEST,
    )
    query_grad = jnp.einsum("whij,wjhd->wihd", score_low, keys, preferred_element_type=fl) * scale
    keys_grad = jnp.einsum("whij,wihd->wjhd", score_low, query, preferred_element_type=fl) * scale
    values_grad = jnp.einsum(
        "whij,wihd->wjhd", probs_again.astype(bf), mixed_low, preferred_element_type=fl
    )
    triple_low = jnp.concatenate(
        [
            query_grad.reshape(windows, window_size, width),
            keys_grad.reshape(windows, window_size, width),
            values_grad.reshape(windows, window_size, width),
        ],
        -1,
    ).astype(bf)
    triple_round = triple_low.astype(fl)
    query_bias_grad = jnp.sum(triple_round[..., :width], (0, 1))
    value_bias_grad = jnp.sum(triple_round[..., 2 * width :], (0, 1))
    project_in_grad = jnp.einsum("wtc,wtf->cf", entry_one, triple_low, preferred_element_type=fl)
    normed_one_grad = jnp.einsum("wtf,cf->wtc", triple_low, in_low, preferred_element_type=fl)
    token_grad, gain_one_grad, shift_one_grad = norm_back(
        normed_one_grad, unit_one, inverse_one, gain_one
    )
    token_grad = token_grad + middle_grad
    vector_grad = jnp.concatenate(
        [
            gain_one_grad,
            shift_one_grad,
            query_bias_grad,
            value_bias_grad,
            out_bias_grad,
            gain_two_grad,
            shift_two_grad,
            contract_bias_grad,
            expand_bias_grad,
        ]
    )
    layer_grid = window_join(result.astype(bf), batches, planes, height, breadth)
    grad_grid = window_join(token_grad.astype(bf), batches, planes, height, breadth)
    leaving = jnp.roll(jnp.stack([layer_grid, grad_grid]), SHIFT, 3)
    arrived = from_behind(leaving[:, :, planes - SHIFT :], "depth", 1)
    leaving = jnp.concatenate([arrived, leaving[:, :, : planes - SHIFT]], 2)
    arrived = from_behind(leaving[:, :, :, :, breadth - SHIFT :], "wide", 1)
    leaving = jnp.concatenate([arrived, leaving[:, :, :, :, : breadth - SHIFT]], 4)
    weights = [project_in, project_out, expand, contract, bias_table, vectors]
    firsts = [
        project_in_first,
        project_out_first,
        expand_first,
        contract_first,
        bias_table_first,
        vectors_first,
    ]
    seconds = [
        project_in_second,
        project_out_second,
        expand_second,
        contract_second,
        bias_table_second,
        vectors_second,
    ]
    rates = [rate_matrix] * 4 + [rate_vector] * 2
    decays = [weight_decay] * 4 + [0.0, 0.0]
    totals = list(
        lax.psum(
            (
                project_in_grad,
                project_out_grad,
                expand_grad,
                contract_grad,
                table_grad,
                vector_grad,
            ),
            ("dp", "depth", "wide"),
        )
    )
    outputs, norm_value = whole_update(totals, weights, firsts, seconds, rates, decays)
    flat_out = [leaving[0], leaving[1]]
    for member in range(6):
        flat_out = flat_out + list(outputs[member])
    for member in range(4):
        flat_out = flat_out + [outputs[member][3].astype(bf)]
    flat_out = flat_out + [norm_value]
    return tuple(flat_out)


def solution(mesh):
    return jax.shard_map(
        local,
        mesh=mesh,
        in_specs=(
            P("dp", "depth", None, "wide", None),
            P("dp", "depth", None, "wide", None),
            P(),
            P(),
            P(),
            P(),
            P(),
            P(),
            P(),
            P(),
            P(),
            P(),
            P(),
            P(),
            P(),
            P(),
            P(),
            P(),
            P(),
            P(),
        ),
        out_specs=(
            P("dp", "depth", None, "wide", None),
            P("dp", "depth", None, "wide", None),
            P(),
            P(),
            P(),
            P(),
            P(),
            P(),
            P(),
            P(),
            P(),
            P(),
            P(),
            P(),
            P(),
            P(),
            P(),
            P(),
            P(),
            P(),
            P(),
            P(),
            P(),
            P(),
            P(),
            P(),
            P(),
            P(),
            P(),
            P(),
            P(),
        ),
        check_vma=False,
    )
```

profile of v0, /device:TPU:1, one launch (start us, length us, event | category | flops | bytes accessed | tf_op | source)
XLA Modules:
  0.0 1560.6 jit_solution(13735855954302178827)
XLA Ops:
  24.7 89.0 %collective-permute-done = bf16[2,8,2,64,8,192]{5,4,3,2,1,0:T(8,128)(2,1)} collective-permute-done((bf16[2,8,2,64,8,192]{5,4,3,2,1,0:T(8,128)(2,1)}, bf16[2,8,2,64,8,192]{5,4,3,2,1,0:T(8,128)(2,1)}, u32[]{:S(2)}, u32[]{:S(2)}) %collective-permute-start) | collective-permute-done | bytes 6291488 | tf_op jit(solution)/shard_map/ppermute | solution.py:28
  144.8 71.3 %collective-permute-done.1 = bf16[2,8,4,64,2,192]{5,4,3,2,1,0:T(2,128)(2,1)} collective-permute-done((bf16[2,8,4,64,2,192]{5,4,3,2,1,0:T(2,128)(2,1)}, bf16[2,8,4,64,2,192]{5,4,3,2,1,0:T(2,128)(2,1)}, u32[]{:S(2)}, u32[]{:S(2)}) %collective-permute-start.1) | collective-permute-done | bytes 3145760 | tf_op jit(solution)/shard_map/ppermute | solution.py:28
  303.9 19.4 %reshape.288 = f32[256,64,192]{2,1,0:T(8,128)} reshape(f32[8,1,16,2,4,4,4,192]{7,6,5,4,3,2,0,1:T(4,128)} %bitcast.116) | data formatting | bytes 25165824 | tf_op jit(solution)/shard_map/convert_element_type | solution.py:144
  421.2 22.5 %copy.177 = bf16[256,64,6,32]{1,3,2,0:T(8,128)(2,1)} copy(bf16[256,64,6,32]{0,3,2,1:T(8,128)(2,1)} %bitcast.125) | data formatting | bytes 12582912 | tf_op jit(solution)/shard_map/reshape | solution.py:185
  443.7 22.4 %copy.178 = bf16[256,64,6,32]{1,3,2,0:T(8,128)(2,1)} copy(bf16[256,64,6,32]{0,3,2,1:T(8,128)(2,1)} %bitcast.124) | data formatting | bytes 12582912 | tf_op jit(solution)/shard_map/reshape | solution.py:186
  466.1 22.5 %copy.180 = bf16[256,64,6,32]{1,3,2,0:T(8,128)(2,1)} copy(bf16[256,64,6,32]{0,3,2,1:T(8,128)(2,1)} %bitcast.123) | data formatting | bytes 12582912 | tf_op jit(solution)/shard_map/reshape | solution.py:187
  488.6 31.7 %fusion.75 = (f32[256,6,64]{2,1,0:T(8,128)S(1)}, f32[256,6,64,64]{2,3,1,0:T(8,128)}) fusion(f32[256,64,64]{1,2,0:T(8,128)} %compare_select_fusion, f32[6,64,64]{1,2,0:T(8,128)S(1)} %copy-done.6, bf16[256,64,6,32]{1,3,2,0:T(8,128)(2,1)} %copy.177, bf16[256,64,6,32]{1,3,2,0:T(8,128)(2,1)} %copy.178), kind=kOutput, calls=%fused_computation.181 | convolution fusion | flops 427720704 | bytes 42434560 | tf_op jit(solution)/shard_map/wihd,wjhd->whij/dot_general | solution.py:190
  520.2 20.6 %fusion.6 = f32[256,6,64]{2,1,0:T(8,128)S(1)} fusion(f32[256,6,64,64]{2,3,1,0:T(8,128)} %get-tuple-element.195, f32[256,6,64]{2,1,0:T(8,128)S(1)} %get-tuple-element.194), kind=kLoop, calls=%fused_computation.25 | loop fusion | flops 12484608 | bytes 25952256 | tf_op jit(solution)/shard_map/reduce_sum | solution.py:196
  542.0 26.3 %fusion.20 = bf16[256,6,32,64]{3,2,1,0:T(8,128)(2,1)} fusion(bf16[256,64,6,32]{1,3,2,0:T(8,128)(2,1)} %copy.180, f32[256,6,64,64]{2,3,1,0:T(8,128)} %get-tuple-element.195, f32[256,6,64]{2,1,0:T(8,128)S(1)} %fusion.6, f32[256,6,64]{2,1,0:T(8,128)S(1)} %get-tuple-element.194), kind=kOutput, calls=%fused_computation.76 | convolution fusion | flops 424673280 | bytes 38535168 | tf_op jit(solution)/shard_map/whij,wjhd->wihd/dot_general | solution.py:199
  568.3 19.5 %copy.182 = bf16[256,64,192]{0,2,1:T(8,128)(2,1)} copy(bf16[256,64,192]{1,2,0:T(8,128)(2,1)} %bitcast.127) | data formatting | bytes 12582912 | tf_op jit(solution)/shard_map/convert_element_type | solution.py:200
  603.3 23.1 %fusion.34 = f32[256,64,768]{2,0,1:T(8,128)} fusion(f32[192,768]{1,0:T(8,128)S(1)} %copy-done.7, f32[256,64,192]{0,2,1:T(8,128)} %copy-done, f32[192]{0:T(256)S(1)} %copy-done.39, f32[192]{0:T(256)S(1)} %copy-done.35, f32[256,64]{0,1:T(8,128)S(1)} %add_rsqrt_fusion.1, f32[256,64]{0,1:T(8,128)S(1)} %broadcast_multiply_fusion.9), kind=kOutput, calls=%fused_computation.115 | convolution fusion | flops 4847714304 | bytes 63636992 | tf_op jit(solution)/shard_map/wtc,cf->wtf/dot_general | solution.py:207
  626.5 130.3 %convert_reduce_fusion = (f32[768]{0:T(1024)}, bf16[256,64,768]{2,0,1:T(8,128)(2,1)}, f32[256,64,768]{2,0,1:T(8,128)}) fusion(f32[256,64,768]{2,0,1:T(8,128)} %fusion.34, f32[768]{0:T(1024)S(1)} %copy-done.33, bf16[256,64,192]{0,2,1:T(8,128)(2,1)} %copy.188, f32[768,192]{0,1:T(8,128)S(1)} %copy-done.11), kind=kOutput, calls=%fused_computation.2 | convolution fusion | flops 5775703040 | bytes 132716544 | tf_op jit(solution)/shard_map/wtc,fc->wtf/dot_general | solution.py:218
  818.4 22.5 %copy.190 = bf16[256,64,6,32]{1,3,2,0:T(8,128)(2,1)} copy(bf16[256,64,6,32]{0,3,2,1:T(8,128)(2,1)} %bitcast.126) | data formatting | bytes 12582912 | tf_op jit(solution)/shard_map/reshape | solution.py:231
  840.9 26.5 %fusion.17 = bf16[256,6,32,64]{3,2,1,0:T(8,128)(2,1)} fusion(bf16[256,64,6,32]{1,3,2,0:T(8,128)(2,1)} %copy.190, f32[256,6,64,64]{2,3,1,0:T(8,128)} %get-tuple-element.195, f32[256,6,64]{2,1,0:T(8,128)S(1)} %copy-done.4), kind=kOutput, calls=%fused_computation.75 | convolution fusion | flops 418381824 | bytes 38141952 | tf_op jit(solution)/shard_map/whij,wihd->wjhd/dot_general | solution.py:245
  867.4 40.8 %multiply_reduce_fusion = (f32[256,6,64]{2,1,0:T(8,128)S(1)}, f32[256,6,64,64]{2,3,1,0:T(8,128)}) fusion(f32[256,6,64,64]{2,3,1,0:T(8,128)} %get-tuple-element.195, f32[256,6,64]{2,1,0:T(8,128)S(1)} %copy-done.4, bf16[256,64,6,32]{1,3,2,0:T(8,128)(2,1)} %copy.190, bf16[256,64,6,32]{1,3,2,0:T(8,128)(2,1)} %copy.180), kind=kOutput, calls=%fused_computation.5 | convolution fusion | flops 421429248 | bytes 63700992 | tf_op jit(solution)/shard_map/wihd,wjhd->whij/dot_general | solution.py:233
  908.2 41.3 %convert_reduce_fusion.1 = (f32[6,64,64]{1,2,0:T(8,128)S(1)}, bf16[256,6,64,64]{2,3,1,0:T(8,128)(2,1)}) fusion(f32[256,6,64,64]{2,3,1,0:T(8,128)} %get-tuple-element.200, f32[256,6,64]{2,1,0:T(8,128)S(1)} %get-tuple-element.199, f32[256,6,64,64]{2,3,1,0:T(8,128)} %get-tuple-element.195, f32[256,6,64]{2,1,0:T(8,128)S(1)} %copy-done.4), kind=kLoop, calls=%fused_computation.3 | loop fusion | flops 37724160 | bytes 63799296 | tf_op jit(solution)/shard_map/reduce_sum | solution.py:239
  949.5 21.7 %multiply_convert_fusion.2 = bf16[256,6,32,64]{3,2,1,0:T(8,128)(2,1)} fusion(bf16[256,64,6,32]{1,3,2,0:T(8,128)(2,1)} %copy.177, bf16[256,6,64,64]{2,3,1,0:T(8,128)(2,1)} %get-tuple-element.174), kind=kOutput, calls=%fused_computation.29 | convolution fusion | flops 408944640 | bytes 25165824 | tf_op jit(solution)/shard_map/whij,wihd->wjhd/dot_general | solution.py:244
  971.2 19.6 %multiply_convert_fusion.3 = bf16[256,6,32,64]{3,2,1,0:T(8,128)(2,1)} fusion(bf16[256,64,6,32]{1,3,2,0:T(8,128)(2,1)} %copy.178, bf16[256,6,64,64]{2,3,1,0:T(8,128)(2,1)} %get-tuple-element.174), kind=kOutput, calls=%fused_computation.30 | convolution fusion | flops 408944640 | bytes 25165824 | tf_op jit(solution)/shard_map/whij,wjhd->wihd/dot_general | solution.py:243
  990.7 40.8 %multiply_convert_fusion.1 = bf16[256,64,768]{2,0,1:T(8,128)(2,1)} fusion(f32[256,64,768]{2,0,1:T(8,128)} %get-tuple-element.170, f32[256,64,768]{2,0,1:T(8,128)} %fusion.34, f32[768]{0:T(1024)S(1)} %copy-done.34), kind=kLoop, calls=%fused_computation.8 | loop fusion | flops 50331648 | bytes 125832192 | tf_op jit(solution)/shard_map/convert_element_type | solution.py:210
  1045.7 26.9 %add_convert_fusion.3 = bf16[256,64,192]{0,2,1:T(8,128)(2,1)} fusion(f32[256,64,192]{0,2,1:T(8,128)} %copy-done, f32[192]{0:T(256)S(1)} %copy-done.38, bf16[256,64,768]{2,0,1:T(8,128)(2,1)} %multiply_convert_fusion.1, f32[768,192]{0,1:T(8,128)S(1)} %copy-done.12), kind=kOutput, calls=%fused_computation.59 | convolution fusion | flops 4841422848 | bytes 44630784 | tf_op jit(solution)/shard_map/wtf,fc->wtc/dot_general | solution.py:213
  1133.2 19.7 %copy.198 = bf16[256,64,192]{0,2,1:T(8,128)(2,1)} copy(bf16[256,64,192]{1,2,0:T(8,128)(2,1)} %bitcast.117) | data formatting | bytes 12582912 | tf_op jit(solution)/shard_map/reshape | solution.py:250
  1287.1 21.5 %fusion.59 = f32[256,64,576]{0,2,1:T(8,128)} fusion(bf16[256,64,192]{0,2,1:T(8,128)(2,1)} %copy.200, bf16[256,64,192]{0,2,1:T(8,128)(2,1)} %copy.199, bf16[256,64,192]{0,2,1:T(8,128)(2,1)} %copy.198), kind=kLoop, calls=%fused_computation.172 | loop fusion | flops 56623104 | bytes 56623104 | tf_op jit(solution)/shard_map/convert_element_type | solution.py:256
  1308.6 53.6 %collective-permute-done.2 = bf16[2,8,2,64,8,192]{5,1,4,3,2,0:T(8,128)(2,1)} collective-permute-done((bf16[2,8,2,64,8,192]{5,1,4,3,2,0:T(8,128)(2,1)}, bf16[2,8,2,64,8,192]{5,1,4,3,2,0:T(8,128)(2,1)}, u32[]{:S(2)}, u32[]{:S(2)}) %collective-permute-start.2) | collective-permute-done | bytes 6291488 | tf_op jit(solution)/shard_map/ppermute | solution.py:28
  1378.6 106.6 %all-reduce = (f32[6,343]{1,0:T(8,128)S(1)}, f32[2304]{0:T(1024)S(1)}) all-reduce(f32[6,343]{1,0:T(8,128)S(1)} %fusion.21, f32[2304]{0:T(1024)S(1)} %concatenate.38), channel_id=1, replica_groups=mesh['dp'=2,'depth'=4,'wide'=4] {'dp','depth','wide'}, use_global_device_ids=true, to_apply=%region_20.21 | all-reduce | flops 4362 | bytes 34896 | tf_op jit(solution)/shard_map/psum | solution.py:305
  (205 shorter events, 600.5 us)
Async XLA Ops:
  7.2 1488.3 %all-reduce.4.cloned.1.call-start = ((), (), s32[]{:S(2)}) async-start(), calls=%async_computation | async-start | bytes 3735552 | tf_op jit(solution)/shard_map/psum | solution.py:305
  19.6 94.1 %collective-permute-start = (bf16[2,8,2,64,8,192]{5,4,3,2,1,0:T(8,128)(2,1)}, bf16[2,8,2,64,8,192]{5,4,3,2,1,0:T(8,128)(2,1)}, u32[]{:S(2)}, u32[]{:S(2)}) collective-permute-start(bf16[2,8,2,64,8,192]{5,4,3,2,1,0:T(8,128)(2,1)} %get-tuple-element.185), channel_id=1, source_target_pairs={{0,12},{4,0},{8,4},{12,8},{1,13},{5,1},{9,5},{13,9},{2,14},{6,2},{... | collective-permute-start | bytes 18874376 | tf_op jit(solution)/shard_map/ppermute | solution.py:28
  122.2 93.9 %collective-permute-start.1 = (bf16[2,8,4,64,2,192]{5,4,3,2,1,0:T(2,128)(2,1)}, bf16[2,8,4,64,2,192]{5,4,3,2,1,0:T(2,128)(2,1)}, u32[]{:S(2)}, u32[]{:S(2)}) collective-permute-start(bf16[2,8,4,64,2,192]{5,4,3,2,1,0:T(2,128)(2,1)} %pad_maximum_fusion.7), channel_id=1, source_target_pairs={{0,3},{1,0},{2,1},{3,2},{4,7},{5,4},{6,5},{7,6},{8,11},{9,8},{10,9... | collective-permute-start | bytes 9437192 | tf_op jit(solution)/shard_map/ppermute | solution.py:28
  129.1 264.6 %copy-start.41 = (f32[192]{0:T(256)}, f32[192]{0:T(256)S(1)}, u32[]{:S(2)}) copy-start(f32[192]{0:T(256)S(1)} %get-tuple-element.193) | copy-start | bytes 2308
  129.1 264.6 %copy-start.46 = (f32[192]{0:T(256)}, f32[192]{0:T(256)S(1)}, u32[]{:S(2)}) copy-start(f32[192]{0:T(256)S(1)} %get-tuple-element.192) | copy-start | bytes 2308
  303.8 89.8 %copy-start.25 = (f32[256,64]{0,1:T(8,128)}, f32[256,64]{0,1:T(8,128)S(1)}, u32[]{:S(2)}) copy-start(f32[256,64]{0,1:T(8,128)S(1)} %copy.174) | copy-start | bytes 196612
  346.5 47.1 %copy-start.27 = (f32[256,64]{0,1:T(8,128)}, f32[256,64]{0,1:T(8,128)S(1)}, u32[]{:S(2)}) copy-start(f32[256,64]{0,1:T(8,128)S(1)} %copy.176) | copy-start | bytes 196612
  367.7 25.9 %copy-start.23 = (f32[192,576]{1,0:T(8,128)S(1)}, f32[192,576]{1,0:T(8,128)}, u32[]{:S(2)}) copy-start(f32[192,576]{1,0:T(8,128)} %param.23) | copy-start | bytes 1327108
  596.3 30.2 %copy-start.17 = (f32[256,64]{0,1:T(8,128)}, f32[256,64]{0,1:T(8,128)S(1)}, u32[]{:S(2)}) copy-start(f32[256,64]{0,1:T(8,128)S(1)} %broadcast_multiply_fusion.9) | copy-start | bytes 196612
  603.2 23.2 %copy-start.19 = (f32[256,64]{0,1:T(8,128)}, f32[256,64]{0,1:T(8,128)S(1)}, u32[]{:S(2)}) copy-start(f32[256,64]{0,1:T(8,128)S(1)} %add_rsqrt_fusion.1) | copy-start | bytes 196612
  603.3 23.2 %copy-start.11 = (f32[768,192]{0,1:T(8,128)S(1)}, f32[768,192]{0,1:T(8,128)}, u32[]{:S(2)}) copy-start(f32[768,192]{0,1:T(8,128)} %param.26) | copy-start | bytes 1769476
  626.4 130.3 %copy-start.36 = (f32[192]{0:T(256)S(1)}, f32[192]{0:T(256)}, u32[]{:S(2)}) copy-start(f32[192]{0:T(256)} %get-tuple-element.188) | copy-start | bytes 2308
  626.5 130.3 %copy-start.40 = (f32[192]{0:T(256)S(1)}, f32[192]{0:T(256)}, u32[]{:S(2)}) copy-start(f32[192]{0:T(256)} %get-tuple-element.187) | copy-start | bytes 2308
  1264.8 97.4 %collective-permute-start.2 = (bf16[2,8,2,64,8,192]{5,1,4,3,2,0:T(8,128)(2,1)}, bf16[2,8,2,64,8,192]{5,1,4,3,2,0:T(8,128)(2,1)}, u32[]{:S(2)}, u32[]{:S(2)}) collective-permute-start(bf16[2,8,2,64,8,192]{5,1,4,3,2,0:T(8,128)(2,1)} %get-tuple-element.180), channel_id=1, source_target_pairs={{0,4},{4,8},{8,12},{12,0},{1,5},{5,9},{9,13},{13,1},{2,6},{6,10},{... | collective-permute-start | bytes 18874376 | tf_op jit(solution)/shard_map/ppermute | solution.py:28
  1279.2 83.1 %slice-start = ((s8[8388608]{0:T(1024)(128)(4,1)}), s8[4194304]{0:T(1024)(128)(4,1)S(1)}, s32[]{:S(2)}) async-start(s8[8388608]{0:T(1024)(128)(4,1)} %bitcast.113), calls=%async_computation.1 | async-start | bytes 8388608
  1287.1 75.2 %slice-start.1 = ((s8[8388608]{0:T(1024)(128)(4,1)}), s8[4194304]{0:T(1024)(128)(4,1)S(1)}, s32[]{:S(2)}) async-start(s8[8388608]{0:T(1024)(128)(4,1)} %bitcast.113), calls=%async_computation.2 | async-start | bytes 8388608
  1366.6 142.7 %copy-start.16 = (f32[192,192]{1,0:T(8,128)S(1)}, f32[192,192]{1,0:T(8,128)}, u32[]{:S(2)}) copy-start(f32[192,192]{1,0:T(8,128)} %param.24) | copy-start | bytes 442372
  1366.6 142.7 %copy-start.29 = (f32[192,192]{1,0:T(8,128)S(1)}, f32[192,192]{1,0:T(8,128)}, u32[]{:S(2)}) copy-start(f32[192,192]{1,0:T(8,128)} %param.36) | copy-start | bytes 442372
  1366.6 142.7 %copy-start.30 = (f32[192,192]{1,0:T(8,128)S(1)}, f32[192,192]{1,0:T(8,128)}, u32[]{:S(2)}) copy-start(f32[192,192]{1,0:T(8,128)} %param.30) | copy-start | bytes 442372
  1366.6 147.5 %copy-start.13 = (f32[768,192]{0,1:T(8,128)S(1)}, f32[768,192]{0,1:T(8,128)}, u32[]{:S(2)}) copy-start(f32[768,192]{0,1:T(8,128)} %param.26) | copy-start | bytes 1769476
  1366.6 147.5 %copy-start.21 = (f32[768,192]{0,1:T(8,128)S(1)}, f32[768,192]{0,1:T(8,128)}, u32[]{:S(2)}) copy-start(f32[768,192]{0,1:T(8,128)} %param.38) | copy-start | bytes 1769476
  1366.6 147.5 %copy-start.22 = (f32[768,192]{0,1:T(8,128)S(1)}, f32[768,192]{0,1:T(8,128)}, u32[]{:S(2)}) copy-start(f32[768,192]{0,1:T(8,128)} %param.32) | copy-start | bytes 1769476
  1366.6 153.0 %collective-permute-start.3 = (bf16[2,8,4,64,2,192]{5,1,4,3,2,0:T(8,128)(2,1)}, bf16[2,8,4,64,2,192]{5,1,4,3,2,0:T(8,128)(2,1)}, u32[]{:S(2)}, u32[]{:S(2)}) collective-permute-start(bf16[2,8,4,64,2,192]{5,1,4,3,2,0:T(8,128)(2,1)} %pad_maximum_fusion.6), channel_id=1, source_target_pairs={{0,1},{1,2},{2,3},{3,0},{4,5},{5,6},{6,7},{7,4},{8,9},{9,10},{10,1... | collective-permute-start | bytes 9437192 | tf_op jit(solution)/shard_map/ppermute | solution.py:28
  1376.3 140.5 %copy-start.9 = (f32[192,768]{1,0:T(8,128)S(1)}, f32[192,768]{1,0:T(8,128)}, u32[]{:S(2)}) copy-start(f32[192,768]{1,0:T(8,128)} %param.25) | copy-start | bytes 1769476
  (35 other events, 489.1 us)
Sparse Core Ops, SparseCore 0:
  1279.3 216.1 all-reduce.3
where the time goes:
time: 1570 us; the launch traced here: 1560 us
  matrix products  465 us (30%)
  local copies, waits for them, and re-layouts  422 us (27%)
  other arithmetic  320 us (20%)
  waiting for transfers between devices  223 us (14%)
  blocking collectives  107 us (7%)
  between operations  20.1 us (1%)
    ppermute x4, waiting for transfers between devices, from_behind(): lax.ppermute(value, axis, [(i, (i + by) % peers) for i in range(peers)])  214 us
    dot_general x1, matrix products, local(): jnp.einsum('wtc,fc->wtf', upstream_low, contract_low, preferred_element_t...  130 us
    psum x1, blocking collectives, local(): lax.psum((project_in_grad, project_out_grad, expand_grad, contract_grad,...  107 us
    convert_element_type x4, local copies, waits for them, and re-layouts, local(): tokens = window_split(paired[0]).astype(fl)  63.7 us
    reduce_sum x1, other arithmetic, local(): jnp.sum(score_low.astype(fl), 0).reshape(heads, -1)  41.3 us
    dot_general x1, matrix products, local(): jnp.einsum('wihd,wjhd->whij', mixed_low, values, preferred_element_type=fl)  40.8 us
    convert_element_type x1, other arithmetic, local(): active_low = active.astype(bf)  40.8 us
    transpose x2, local copies, waits for them, and re-layouts, window_join(): tensor = tensor.transpose(0, 1, 4, 2, 5, 3, 6, 7)  31.8 us
  transfers between devices with their start and end apart: 5, of which 4 were waited for; matrix products, arithmetic and copies ran while one was open for 7% of the time, Pallas kernels for 0%

commit v1 on v0

v1 whole, which is shorter than its diff:
```python
from functools import partial

import jax
import jax.numpy as jnp
import numpy as np
from jax import lax
from jax.experimental import pallas as pl
from jax.experimental.pallas import tpu as pltpu
from jax.sharding import PartitionSpec as P

HEADS = 6
WIN = 4
SHIFT = 2
STEP = 10
TOK = WIN**3
GROUP = 4
LANES = GROUP * TOK

norm_eps = 1e-05
mask_fill = -100.0
clip_bound = 1000.0
rate_matrix = 0.1
rate_vector = 0.6
weight_decay = 0.01
beta_first = 0.9
beta_second = 0.999
adam_eps = 1e-08
LOG2E = 1.4426950408889634
INV_SQRT2 = 0.7071067811865476
INV_SQRT2PI = 0.3989422804014327


def relative_index():
    extent = 2 * WIN - 1
    corner = np.arange(WIN)
    places = np.stack(np.meshgrid(corner, corner, corner, indexing="ij"), -1).reshape(-1, 3)
    offsets = places[:, None, :] - places[None, :, :] + WIN - 1
    return (offsets[..., 0] * extent + offsets[..., 1]) * extent + offsets[..., 2]


def region_labels(count, start, length):
    places = start + jnp.arange(count, dtype=jnp.int32)
    return (places >= length - WIN).astype(jnp.int32) + (places >= length - SHIFT).astype(jnp.int32)


def window_split(tensor):
    batches, planes, height, breadth, feature = tensor.shape
    tensor = tensor.reshape(
        batches, planes // WIN, WIN, height // WIN, WIN, breadth // WIN, WIN, feature
    )
    tensor = tensor.transpose(0, 1, 3, 5, 2, 4, 6, 7)
    return tensor.reshape(-1, WIN**3, feature)


def adam_update(weight, first, second, gradient, rate, decay):
    first_new = beta_first * first + (1.0 - beta_first) * gradient
    second_new = beta_second * second + (1.0 - beta_second) * gradient * gradient
    first_hat = first_new / (1.0 - beta_first**STEP)
    second_hat = second_new / (1.0 - beta_second**STEP)
    weight_new = weight - rate * (first_hat / (jnp.sqrt(second_hat) + adam_eps) + decay * weight)
    return (first_new, second_new, weight_new)


def whole_update(totals, weights, firsts, seconds, rates, decays):
    squares = jnp.float32(0.0)
    for member in totals:
        squares = squares + jnp.sum(member * member)
    norm_value = jnp.sqrt(squares)
    factor = jnp.minimum(1.0, clip_bound / (norm_value + 1e-06))
    outputs = []
    for member in range(6):
        clipped = totals[member] * factor
        outputs.append(
            (clipped,)
            + adam_update(
                weights[member],
                firsts[member],
                seconds[member],
                clipped,
                rates[member],
                decays[member],
            )
        )
    return (outputs, norm_value)


fl = jnp.float32
bf = jnp.bfloat16


def dot(a, b):
    return jnp.dot(a, b, preferred_element_type=fl)


def dot_nt(a, b):
    return lax.dot_general(a, b, (((1,), (1,)), ((), ())), preferred_element_type=fl)


def wide(v, lanes):
    return jnp.concatenate([v] * (lanes // v.shape[1]), axis=1)


def unit_norm(v):
    width = v.shape[0]
    mean = jnp.sum(v, 0, keepdims=True) * (1.0 / width)
    centred = v - mean
    inverse = lax.rsqrt(jnp.sum(centred * centred, 0, keepdims=True) * (1.0 / width) + norm_eps)
    return centred * inverse, inverse


def unit_back(grad, unit, inverse, gain):
    width = grad.shape[0]
    scaled = grad * gain
    inner = jnp.sum(scaled, 0, keepdims=True) * (1.0 / width)
    along = jnp.sum(scaled * unit, 0, keepdims=True) * (1.0 / width)
    return inverse * (scaled - inner - unit * along)


def fold(v):
    total = v[:, :128]
    for lane in range(128, v.shape[1], 128):
        total = total + v[:, lane : lane + 128]
    return total


def pair_blocks(low, c0, rows, lane0):
    count = rows // 32
    zero = jnp.zeros((32, 128), bf)
    out = []
    for a in range(count):
        out.append(
            jnp.concatenate(
                [
                    low[c0 + 32 * a : c0 + 32 * a + 32, lane0 : lane0 + 128] if a == b else zero
                    for b in range(count)
                ],
                axis=1,
            )
        )
    return jnp.concatenate(out, axis=0)


def cross(token_major, low, lane0, first_half):
    pieces = []
    for c0, rows in ((0, 128), (128, 64)):
        full = dot(
            token_major[lane0 : lane0 + 128, c0 : c0 + rows], pair_blocks(low, c0, rows, lane0)
        )
        for b in range(rows // 32):
            block = full[:, 128 * b : 128 * b + 128]
            pieces.append(jnp.where(first_half, block[:TOK], block[TOK:]))
    return pieces


def two_windows(compact, first_half):
    zero = jnp.zeros_like(compact)
    return jnp.concatenate(
        [jnp.where(first_half, compact, zero), jnp.where(first_half, zero, compact)], axis=0
    )


def placement():
    take = np.zeros((LANES, LANES + TOK), np.float32)
    give = np.zeros((LANES + TOK, LANES), np.float32)
    pick = np.zeros((TOK, LANES), np.float32)
    fill = np.zeros((LANES, TOK), np.float32)
    for hw in range(2):
        for ww in range(2):
            for d in range(WIN):
                for hh in range(WIN):
                    for wl in range(WIN):
                        t = ((hw * 2 + ww) * WIN + d) * 16 + hh * 4 + wl
                        h, w = 4 * hw + hh, 4 * ww + wl
                        if w < 2 * WIN - SHIFT:
                            row = d * 64 + h * 8 + w + SHIFT
                        else:
                            row = LANES + d * 16 + h * 2 + w - (2 * WIN - SHIFT)
                        take[t, row] = 1.0
                        give[row, t] = 1.0
    for d in range(WIN):
        for h in range(2 * WIN):
            for w in range(SHIFT):
                pick[d * 16 + h * 2 + w, d * 64 + h * 8 + w] = 1.0
                fill[d * 64 + h * 8 + w, d * 16 + h * 2 + w] = 1.0
    return [jnp.asarray(m, bf) for m in (take, give, pick, fill)]


def block_kernel(
    vox,
    cot,
    table_ref,
    vec_ref,
    w_in_t,
    w_in,
    w_out_t,
    w_out,
    w_exp_t,
    w_exp,
    w_con,
    w_con_t,
    take,
    give,
    pick,
    fill,
    out_res,
    out_tok,
    d_in,
    d_out,
    d_exp,
    d_con,
    d_vec,
    d_tab,
    own,
    halo_d,
    halo_w,
    send_w,
    back_send,
    back_recv,
    grid_out,
    own_sem,
    d_send,
    d_recv,
    w_send,
    w_recv,
    b_send,
    b_recv,
    o_sem,
    r_send,
    r_recv,
):
    crops = vox.shape[0]
    rows = vox.shape[2]
    width = vox.shape[3]
    units = rows // TOK
    n = LANES
    depth, peers_d = lax.axis_index("depth"), lax.axis_size("depth")
    column, peers_w = lax.axis_index("wide"), lax.axis_size("wide")
    d_prev = {"depth": lax.rem(depth + peers_d - 1, peers_d)}
    d_next = {"depth": lax.rem(depth + 1, peers_d)}
    w_prev = {"wide": lax.rem(column + peers_w - 1, peers_w)}
    w_next = {"wide": lax.rem(column + 1, peers_w)}
    mesh_id = pl.DeviceIdType.MESH
    sources = (vox, cot)
    results = (out_res, out_tok)

    def own_copy(c, a):
        slot = lax.rem(c, 2)
        return pltpu.make_async_copy(
            sources[a].at[c, pl.ds(SHIFT, 2)], own.at[slot, a], own_sem.at[slot, a]
        )

    def depth_copy(c, a):
        return pltpu.make_async_remote_copy(
            src_ref=sources[a].at[c, pl.ds(0, SHIFT)],
            dst_ref=halo_d.at[c, a],
            send_sem=d_send.at[c, a],
            recv_sem=d_recv.at[c, a],
            device_id=d_prev,
            device_id_type=mesh_id,
        )

    def wide_copy(c):
        return pltpu.make_async_remote_copy(
            src_ref=send_w.at[c],
            dst_ref=halo_w.at[c],
            send_sem=w_send.at[c],
            recv_sem=w_recv.at[c],
            device_id=w_prev,
            device_id_type=mesh_id,
        )

    def back_copy(c):
        return pltpu.make_async_remote_copy(
            src_ref=back_send.at[c],
            dst_ref=back_recv.at[c],
            send_sem=b_send.at[c],
            recv_sem=b_recv.at[c],
            device_id=w_next,
            device_id_type=mesh_id,
        )

    def keep_copy(c, a):
        slot = lax.rem(c, 2)
        return pltpu.make_async_copy(
            grid_out.at[slot, a, pl.ds(0, 2)], results[a].at[c, pl.ds(SHIFT, 2)], o_sem.at[slot, a]
        )

    def return_copy(c, a):
        slot = lax.rem(c, 2)
        return pltpu.make_async_remote_copy(
            src_ref=grid_out.at[slot, a, pl.ds(2, 2)],
            dst_ref=results[a].at[c, pl.ds(0, SHIFT)],
            send_sem=r_send.at[slot, a],
            recv_sem=r_recv.at[c, a],
            device_id=d_next,
            device_id_type=mesh_id,
        )

    barrier = pltpu.get_barrier_semaphore()
    for peer in (d_prev, d_next, w_prev, w_next):
        pl.semaphore_signal(barrier, inc=1, device_id=peer, device_id_type=mesh_id)
    pl.semaphore_wait(barrier, 4)

    for a in range(2):
        own_copy(0, a).start()

    def send_depth(c, carry):
        for a in range(2):
            depth_copy(c, a).start()
        return carry

    lax.fori_loop(0, crops, send_depth, 0)
    for ref in (d_in, d_out, d_exp, d_con, d_vec, d_tab):
        ref[...] = jnp.zeros_like(ref)

    def starts(u):
        first = pl.multiple_of(u * TOK + 16, 16)
        second = pl.multiple_of(lax.rem(u * TOK + TOK, rows), 16)
        return first, second

    def natural(c, a, u):
        first, second = starts(u)
        slot = lax.rem(c, 2)
        parts = []
        for d in range(2):
            parts.append(own[slot, a, d, pl.ds(first, 48), :])
            parts.append(own[slot, a, d, pl.ds(second, 16), :])
        for d in range(2):
            parts.append(halo_d[c, a, d, pl.ds(first, 48), :])
            parts.append(halo_d[c, a, d, pl.ds(second, 16), :])
        return jnp.concatenate(parts, axis=0)

    def pack(c):
        for a in range(2):
            own_copy(c, a).wait()
            depth_copy(c, a).wait_recv()

        def one(u, carry):
            for a in range(2):
                send_w[c, a, pl.ds(pl.multiple_of(u * TOK, TOK), TOK), :] = dot(
                    pick[...], natural(c, a, u)
                ).astype(bf)
            return carry

        lax.fori_loop(0, units, one, 0)
        wide_copy(c).start()

    def merge(c):
        slot = lax.rem(c, 2)
        back_copy(c).wait_recv()

        def one(u, carry):
            first, second = starts(u)
            for a in range(2):
                extra = dot(fill[...], back_recv[c, a, pl.ds(pl.multiple_of(u * TOK, TOK), TOK), :])
                for d in range(WIN):
                    for start, size, at in ((first, 48, 64 * d), (second, 16, 64 * d + 48)):
                        place = pl.ds(start, size)
                        grid_out[slot, a, d, place, :] = (
                            grid_out[slot, a, d, place, :].astype(fl) + extra[at : at + size]
                        ).astype(bf)
            return carry

        lax.fori_loop(0, units, one, 0)
        for a in range(2):
            keep_copy(c, a).start()
            return_copy(c, a).start()

    eye_c = (
        lax.broadcasted_iota(jnp.int32, (width, width), 0)
        == lax.broadcasted_iota(jnp.int32, (width, width), 1)
    ).astype(bf)
    eye_t = (
        lax.broadcasted_iota(jnp.int32, (n, n), 0) == lax.broadcasted_iota(jnp.int32, (n, n), 1)
    ).astype(bf)
    first_half = lax.broadcasted_iota(jnp.int32, (TOK, 128), 1) < TOK
    ones = jnp.ones((16, n), bf)
    scale = 32 ** (-0.5)

    def vec(index, size=width):
        return wide(vec_ref[index : index + size, :], n)

    def unit(c, u):
        here = pl.ds(pl.multiple_of(u * TOK, TOK), TOK)

        def tokens(a):
            low = dot(
                take[...], jnp.concatenate([natural(c, a, u), halo_w[c, a, here, :]], axis=0)
            ).astype(bf)
            return dot_nt(eye_c, low)

        def put(a, low):
            first, second = starts(u)
            slot = lax.rem(c, 2)
            placed = dot_nt(give[...], low).astype(bf)
            for d in range(WIN):
                grid_out[slot, a, d, pl.ds(first, 48), :] = placed[64 * d : 64 * d + 48]
                grid_out[slot, a, d, pl.ds(second, 16), :] = placed[64 * d + 48 : 64 * d + 64]
            back_send[c, a, here, :] = placed[n:]

        x = tokens(0)
        up = tokens(1)
        up_low = up.astype(bf)
        unit_one, inverse_one = unit_norm(x)
        entry_one = (unit_one * vec(0) + vec(width)).astype(bf)
        triple = dot(w_in_t[...], entry_one)
        query = (triple[:width] + vec(2 * width)).astype(bf)
        keys = triple[width : 2 * width].astype(bf)
        values = (triple[2 * width :] + vec(3 * width)).astype(bf)
        turned = dot_nt(eye_t, jnp.concatenate([keys, values], axis=0)).astype(bf)
        keys_t = turned[:, :width]
        values_t = turned[:, width:]
        probs = []
        probs_wide = []
        mixed = []
        edge = (u == units - 1).astype(jnp.int32)
        for half in range(2):
            lane0 = 128 * half
            pieces = cross(keys_t, query, lane0, first_half)
            which = edge if half == 1 else 0
            cols = []
            for head in range(HEADS):
                s = (
                    pieces[head] * (scale * LOG2E)
                    + table_ref[which, :, 128 * head : 128 * head + 128]
                )
                e = jnp.exp2(s - jnp.max(s, 0, keepdims=True))
                p = e * (1.0 / jnp.sum(e, 0, keepdims=True))
                p_wide = two_windows(p.astype(bf), first_half)
                probs.append(p)
                probs_wide.append(p_wide)
                cols.append(dot(values[32 * head : 32 * head + 32, lane0 : lane0 + 128], p_wide))
            mixed.append(jnp.concatenate(cols, axis=0))
        mixed = jnp.concatenate(mixed, axis=1).astype(bf)
        middle = x + dot(w_out_t[...], mixed) + vec(4 * width)
        unit_two, inverse_two = unit_norm(middle)
        entry_two = (unit_two * vec(5 * width) + vec(6 * width)).astype(bf)
        hidden = dot(w_exp_t[...], entry_two) + vec(8 * width, 4 * width)
        phi = 0.5 + 0.5 * lax.erf(hidden * INV_SQRT2)
        slope = phi + hidden * (INV_SQRT2PI * jnp.exp2(hidden * hidden * (-0.5 * LOG2E)))
        active = (hidden * phi).astype(bf)
        result = middle + dot(w_con_t[...], active) + vec(7 * width)
        put(0, result.astype(bf))
        hidden_low = (dot(w_con[...], up_low) * slope).astype(bf)
        grad_two = dot(w_exp[...], hidden_low)
        middle_grad = up + unit_back(grad_two, unit_two, inverse_two, vec(5 * width))
        branch_low = middle_grad.astype(bf)
        mixed_low = dot(w_out[...], branch_low).astype(bf)
        d_cols = [[], [], []]
        for half in range(2):
            lane0 = 128 * half
            pieces = cross(values_t, mixed_low, lane0, first_half)
            dq, dk, dv = [], [], []
            for head in range(HEADS):
                p = probs[half * HEADS + head]
                pg = pieces[head]
                sg = (p * (pg - jnp.sum(pg * p, 0, keepdims=True))).astype(bf)
                d_tab[:, 128 * head : 128 * head + 128] += sg.astype(fl)
                s_wide = two_windows(sg, first_half)
                at = slice(32 * head, 32 * head + 32)
                dq.append(dot(keys[at, lane0 : lane0 + 128], s_wide))
                dk.append(dot_nt(query[at, lane0 : lane0 + 128], s_wide))
                dv.append(
                    dot_nt(mixed_low[at, lane0 : lane0 + 128], probs_wide[half * HEADS + head])
                )
            for member, part in enumerate((dq, dk, dv)):
                d_cols[member].append(jnp.concatenate(part, axis=0))
        dq, dk, dv = [jnp.concatenate(part, axis=1) for part in d_cols]
        triple_low = jnp.concatenate([dq * scale, dk * scale, dv], axis=0).astype(bf)
        grad_one = dot(w_in[...], triple_low)
        token_grad = middle_grad + unit_back(grad_one, unit_one, inverse_one, vec(0))
        put(1, token_grad.astype(bf))
        d_in[...] += dot_nt(triple_low, jnp.concatenate([entry_one, ones], axis=0))
        d_out[...] += dot_nt(branch_low, jnp.concatenate([mixed, ones], axis=0))
        d_exp[...] += dot_nt(hidden_low, jnp.concatenate([entry_two, ones], axis=0))
        d_con[...] += dot_nt(active, up_low)
        d_vec[0:width, :] += fold(grad_one * unit_one)
        d_vec[width : 2 * width, :] += fold(grad_one)
        d_vec[2 * width : 3 * width, :] += fold(grad_two * unit_two)
        d_vec[3 * width : 4 * width, :] += fold(grad_two)
        d_vec[4 * width : 5 * width, :] += fold(up)

    pack(0)

    def crop(c, carry):
        wide_copy(c).wait_recv()

        @pl.when(c + 1 < crops)
        def _():
            for a in range(2):
                own_copy(c + 1, a).start()

        @pl.when(c >= 2)
        def _():
            for a in range(2):
                keep_copy(c - 2, a).wait()
                return_copy(c - 2, a).wait_send()

        def one(u, inner):
            unit(c, u)

            @pl.when((u == 1) & (c + 1 < crops))
            def _():
                pack(c + 1)

            @pl.when((u == units - 2) & (c > 0))
            def _():
                merge(c - 1)

            return inner

        lax.fori_loop(0, units, one, 0)
        back_copy(c).start()
        return carry

    lax.fori_loop(0, crops, crop, 0)
    merge(crops - 1)

    def finish(c, carry):
        for a in range(2):
            depth_copy(c, a).wait_send()
            return_copy(c, a).wait_recv()
        wide_copy(c).wait_send()
        back_copy(c).wait_send()
        return carry

    lax.fori_loop(0, crops, finish, 0)

    def close(c, carry):
        for a in range(2):
            keep_copy(c, a).wait()
            return_copy(c, a).wait_send()
        return carry

    lax.fori_loop(crops - 2, crops, close, 0)


def block_call(voxels, cotangent, table, vec_wide, mats):
    crops, planes, rows, width = voxels.shape
    hid = 4 * width
    whole = pl.BlockSpec(memory_space=pltpu.VMEM)
    far = pl.BlockSpec(memory_space=pl.ANY)
    consts = [table, vec_wide] + mats + placement()
    sem = pltpu.SemaphoreType.DMA
    return pl.pallas_call(
        block_kernel,
        in_specs=[far, far] + [whole] * len(consts),
        out_specs=[far, far] + [whole] * 6,
        out_shape=[
            jax.ShapeDtypeStruct(voxels.shape, bf),
            jax.ShapeDtypeStruct(voxels.shape, bf),
            jax.ShapeDtypeStruct((3 * width, width + 16), fl),
            jax.ShapeDtypeStruct((width, width + 16), fl),
            jax.ShapeDtypeStruct((hid, width + 16), fl),
            jax.ShapeDtypeStruct((hid, width), fl),
            jax.ShapeDtypeStruct((5 * width, 128), fl),
            jax.ShapeDtypeStruct((TOK, HEADS * 128), fl),
        ],
        scratch_shapes=[
            pltpu.VMEM((2, 2, 2, rows, width), bf),
            pltpu.VMEM((crops, 2, 2, rows, width), bf),
            pltpu.VMEM((crops, 2, rows, width), bf),
            pltpu.VMEM((crops, 2, rows, width), bf),
            pltpu.VMEM((crops, 2, rows, width), bf),
            pltpu.VMEM((crops, 2, rows, width), bf),
            pltpu.VMEM((2, 2, 4, rows, width), bf),
            sem((2, 2)),
            sem((crops, 2)),
            sem((crops, 2)),
            sem((crops,)),
            sem((crops,)),
            sem((crops,)),
            sem((crops,)),
            sem((2, 2)),
            sem((2, 2)),
            sem((crops, 2)),
        ],
        compiler_params=pltpu.CompilerParams(
            vmem_limit_bytes=60 * 2**20, collective_id=0, has_side_effects=True
        ),
        name="block",
    )(voxels, cotangent, *consts)


def make_tables(bias_table, planes, height, breadth):
    extent = (2 * WIN - 1) ** 3
    selector = (
        jnp.asarray(relative_index().T.reshape(-1), jnp.int32)[:, None]
        == jnp.arange(extent, dtype=jnp.int32)[None, :]
    ).astype(fl)
    pair_bias = jnp.einsum("hr,pr->hp", bias_table, selector, precision=lax.Precision.HIGHEST)
    pair_bias = pair_bias.reshape(HEADS, TOK, TOK)
    plane_labels = region_labels(
        planes, lax.axis_index("depth") * planes, planes * lax.axis_size("depth")
    )
    column_labels = region_labels(
        breadth, lax.axis_index("wide") * breadth, breadth * lax.axis_size("wide")
    )
    tables = []
    for place in (0, height - WIN):
        height_labels = region_labels(height, 0, height)[place : place + WIN]
        labels = (
            plane_labels[:, None, None] * 9
            + height_labels[None, :, None] * 3
            + column_labels[None, None, :]
        )
        labels = window_split(labels[None, :, :, :, None])[..., 0]
        masks = jnp.where(labels[:, :, None] == labels[:, None, :], 0.0, mask_fill).astype(fl)
        both = pair_bias[:, None] + masks[None]
        tables.append(both.transpose(2, 0, 1, 3).reshape(TOK, HEADS * 128))
    return jnp.stack(tables) * LOG2E, selector


def local(
    voxels,
    cotangent,
    project_in,
    project_out,
    expand,
    contract,
    bias_table,
    vectors,
    project_in_first,
    project_out_first,
    expand_first,
    contract_first,
    bias_table_first,
    vectors_first,
    project_in_second,
    project_out_second,
    expand_second,
    contract_second,
    bias_table_second,
    vectors_second,
):
    batches, planes, height, breadth, width = voxels.shape
    table, selector = make_tables(bias_table, planes, height, breadth)
    vec_wide = jnp.broadcast_to(vectors[:, None], (vectors.shape[0], 128))
    in_low = project_in.astype(bf)
    out_low = project_out.astype(bf)
    expand_low = expand.astype(bf)
    contract_low = contract.astype(bf)
    mats = [
        in_low.T, in_low, out_low.T, out_low,
        expand_low.T, expand_low, contract_low, contract_low.T,
    ]
    flat = (batches, planes, height * breadth, width)
    result, token_grad, d_in, d_out, d_exp, d_con, d_vec, d_tab = block_call(
        voxels.reshape(flat), cotangent.reshape(flat), table, vec_wide, mats
    )
    sums = jnp.sum(d_vec, -1).reshape(5, width)
    vector_grad = jnp.concatenate(
        [
            sums[0],
            sums[1],
            d_in[:width, width],
            d_in[2 * width :, width],
            d_out[:, width],
            sums[2],
            sums[3],
            sums[4],
            d_exp[:, width],
        ]
    )
    table_grad = d_tab.reshape(TOK, HEADS, 2, TOK).sum(2).transpose(1, 0, 2).reshape(HEADS, -1)
    table_grad = jnp.einsum("hp,pr->hr", table_grad, selector, precision=lax.Precision.HIGHEST)
    weights = [project_in, project_out, expand, contract, bias_table, vectors]
    firsts = [
        project_in_first,
        project_out_first,
        expand_first,
        contract_first,
        bias_table_first,
        vectors_first,
    ]
    seconds = [
        project_in_second,
        project_out_second,
        expand_second,
        contract_second,
        bias_table_second,
        vectors_second,
    ]
    rates = [rate_matrix] * 4 + [rate_vector] * 2
    decays = [weight_decay] * 4 + [0.0, 0.0]
    totals = list(
        lax.psum(
            (
                d_in[:, :width].T,
                d_out[:, :width].T,
                d_exp[:, :width].T,
                d_con,
                table_grad,
                vector_grad,
            ),
            ("dp", "depth", "wide"),
        )
    )
    outputs, norm_value = whole_update(totals, weights, firsts, seconds, rates, decays)
    flat_out = [result.reshape(voxels.shape), token_grad.reshape(voxels.shape)]
    for member in range(6):
        flat_out = flat_out + list(outputs[member])
    for member in range(4):
        flat_out = flat_out + [outputs[member][3].astype(bf)]
    flat_out = flat_out + [norm_value]
    return tuple(flat_out)


def solution(mesh):
    split = P("dp", "depth", None, "wide", None)
    return jax.shard_map(
        local,
        mesh=mesh,
        in_specs=(split,) * 2 + (P(),) * 18,
        out_specs=(split,) * 2 + (P(),) * 29,
        check_vma=False,
    )
```

time: 1570 us -> 685 us (0.44)
  matrix products: 465 us -> 7.3 us
  Pallas kernels: 0 us -> 430 us
  local copies, waits for them, and re-layouts: 422 us -> 85.2 us
  other arithmetic: 320 us -> 34.4 us
  waiting for transfers between devices: 223 us -> 65.4 us
  blocking collectives: 107 us -> 38.9 us
    dot_general x20 -> x2, matrix products: 465 us -> 7.3 us  [the longest x1 4.23 us: make_tables(): jnp.einsum('hr,pr->hp', bias_table, selector, precision=lax.Precision.HIG...]
    pallas_call x0 -> x1, Pallas kernels: none -> 430 us  [block_call(): pl.pallas_call(block_kernel, in_specs=[far, far] + [whole] * len(consts),...]
    ppermute x4 -> x0, waiting for transfers between devices: 214 us -> none  [from_behind(): lax.ppermute(value, axis, [(i, (i + by) % peers) for i in range(peers)])]
    reshape x12 -> x2, local copies, waits for them, and re-layouts: 200 us -> 1.94 us  [local(): d_tab.reshape(TOK, HEADS, 2, TOK).sum(2).transpose(1, 0, 2)]
    reduce_sum x8 -> x2, other arithmetic: 125 us -> 0.69 us  [the longest x1 0.49 us: local(): d_tab.reshape(TOK, HEADS, 2, TOK).sum(2).transpose(1, 0, 2)]
    convert_element_type x7 -> x1, local copies, waits for them, and re-layouts: 108 us -> 0.92 us  [local(): contract_low = contract.astype(bf)]
    convert_element_type x4, other arithmetic: 88.7 us -> 6.24 us  [the longest x1 1.81 us: local(): expand_low = expand.astype(bf)]
    psum x1, blocking collectives: 107 us -> 38.9 us  [local(): lax.psum((d_in[:, :width].T, d_out[:, :width].T, d_exp[:, :width].T, d_co...]
  transfers between devices with their start and end apart: 5 -> 1, of which waited for: 4 -> 1; matrix products, arithmetic and copies ran while one was open for 7% -> 4% of each run, Pallas kernels for 0% -> 0%
where the time goes in v1:
time: 685 us; the launch traced here: 681 us
  Pallas kernels  430 us (63%)
  local copies, waits for them, and re-layouts  85.2 us (12%)
  waiting for transfers between devices  65.4 us (10%)
  blocking collectives  38.9 us (6%)
  other arithmetic  34.4 us (5%)
  between operations  19.5 us (3%)
  matrix products  7.3 us (1%)
    pallas_call x1, Pallas kernels, block_call(): pl.pallas_call(block_kernel, in_specs=[far, far] + [whole] * len(consts),...  430 us
    unnamed x72, local copies, waits for them, and re-layouts  65.7 us
    psum x1, waiting for transfers between devices, local(): lax.psum((d_in[:, :width].T, d_out[:, :width].T, d_exp[:, :width].T, d_co...  65.3 us
    psum x1, blocking collectives, local(): lax.psum((d_in[:, :width].T, d_out[:, :width].T, d_exp[:, :width].T, d_co...  38.9 us
  transfers between devices with their start and end apart: 1, of which 1 were waited for; matrix products, arithmetic and copies ran while one was open for 4% of the time, Pallas kernels for 0%

profile of v1, /device:TPU:1, one launch (start us, length us, event | category | flops | bytes accessed | tf_op | source)
XLA Modules:
  0.0 680.9 jit_solution(5123795781969768528)
XLA Ops:
  19.0 4.2 fusion.2
  30.4 430.1 %block.1 = (bf16[8,4,512,192]{3,2,1,0:T(8,128)(2,1)}, bf16[8,4,512,192]{3,2,1,0:T(8,128)(2,1)}, f32[576,208]{1,0:T(8,128)}, f32[192,208]{1,0:T(8,128)}, f32[768,...) custom-call(bf16[8,4,512,192]{3,2,1,0:T(8,128)(2,1)} %bitcast.34, ...), custom_call_target="tpu_custom_call" | custom-call | tf_op jit(solution)/shard_map/block/pallas_call | solution.py:545
  464.3 2.1 slice_bitcast_fusion
  471.5 2.1 copy.194
  479.5 2.2 copy.204
  481.7 2.2 copy.203
  485.3 2.2 copy.208
  492.1 3.1 fusion
  495.1 38.9 %all-reduce = (f32[6,343]{1,0:T(8,128)S(1)}, f32[2304]{0:T(1024)S(1)}) all-reduce(f32[6,343]{1,0:T(8,128)S(1)} %fusion, f32[2304]{0:T(1024)S(1)} %concatenate.4), channel_id=1, replica_groups=mesh['dp'=2,'depth'=4,'wide'=4] {'dp','depth','wide'}, use_global_device_ids=true, to_apply=%region_9.10 | all-reduce | flops 4362 | bytes 34896 | tf_op jit(solution)/shard_map/psum | solution.py:687
  535.3 65.3 %all-reduce.4.cloned.1.call-done = (f32[192,576]{0,1:T(8,128)}, f32[192,192]{0,1:T(8,128)}, f32[192,768]{0,1:T(8,128)}, f32[768,192]{1,0:T(8,128)}) async-done(((f32[192,576]{0,1:T(8,128)}, f32[192,192]{0,1:T(8,128)}, f32[192,768]{0,1:T(8,128)}, f32[768,192]{1,0:T(8,128)}), (f32[192,576]{0,1:T(8,128)}, f32[192,192]{0,1:T(8,128)}, f32[192,768]{0,1:T(8,128)}, ...) | async-done | bytes 1769488 | tf_op jit(solution)/shard_map/psum | solution.py:687
  611.9 2.9 fusion.21
  614.8 2.1 copy.212
  616.9 2.1 copy.213
  628.3 3.4 fusion.17
  631.7 2.2 copy.220
  633.9 2.2 copy.221
  636.1 2.2 copy.222
  638.3 2.2 copy.223
  640.5 2.8 fusion.15
  643.4 2.2 copy.224
  645.6 2.2 copy.225
  647.8 2.2 copy.226
  657.6 7.7 %copy.238 = bf16[8,4,64,8,192]{4,3,2,1,0:T(8,128)(2,1)} copy(bf16[8,4,64,8,192]{4,3,2,1,0:T(8,128)(2,1)} %bitcast.37) | data formatting | bytes 12582912
  665.2 7.7 %copy.239 = bf16[8,4,64,8,192]{4,3,2,1,0:T(8,128)(2,1)} copy(bf16[8,4,64,8,192]{4,3,2,1,0:T(8,128)(2,1)} %bitcast.36) | data formatting | bytes 12582912
  (111 shorter events, 64.8 us)
Async XLA Ops:
  7.2 593.4 %all-reduce.4.cloned.1.call-start = ((), (), s32[]{:S(2)}) async-start(), calls=%async_computation | async-start | bytes 4718592 | tf_op jit(solution)/shard_map/psum | solution.py:687
  12.6 16.4 %copy-start.9 = (f32[2304]{0:T(1024)S(1)}, f32[2304]{0:T(1024)}, u32[]{:S(2)}) copy-start(f32[2304]{0:T(1024)} %param.32) | copy-start | bytes 27652
  30.4 435.9 %copy-start.2 = (f32[192,576]{1,0:T(8,128)S(1)}, f32[192,576]{1,0:T(8,128)}, u32[]{:S(2)}) copy-start(f32[192,576]{1,0:T(8,128)} %param.27) | copy-start | bytes 1327108
  460.6 6.0 copy-start.8
  460.6 7.4 %copy-start.6 = (f32[192,192]{1,0:T(8,128)S(1)}, f32[192,192]{1,0:T(8,128)}, u32[]{:S(2)}) copy-start(f32[192,192]{1,0:T(8,128)} %param.28) | copy-start | bytes 442372
  460.6 8.2 %copy-start = (f32[192,768]{1,0:T(8,128)S(1)}, f32[192,768]{1,0:T(8,128)}, u32[]{:S(2)}) copy-start(f32[192,768]{1,0:T(8,128)} %param.29) | copy-start | bytes 1769476
  460.6 9.3 %copy-start.1 = (f32[768,192]{0,1:T(8,128)S(1)}, f32[768,192]{0,1:T(8,128)}, u32[]{:S(2)}) copy-start(f32[768,192]{0,1:T(8,128)} %param.30) | copy-start | bytes 1769476
  469.9 21.0 %copy-start.5 = (f32[768,208]{1,0:T(8,128)S(1)}, f32[768,208]{1,0:T(8,128)}, u32[]{:S(2)}) copy-start(f32[768,208]{1,0:T(8,128)} %get-tuple-element.43) | copy-start | bytes 1916932
  534.0 77.8 %copy-start.10 = (f32[2304]{0:T(1024)}, f32[2304]{0:T(1024)S(1)}, u32[]{:S(2)}) copy-start(f32[2304]{0:T(1024)S(1)} %get-tuple-element.174) | copy-start | bytes 27652
  534.1 77.8 %copy-start.12 = (f32[6,343]{1,0:T(8,128)}, f32[6,343]{1,0:T(8,128)S(1)}, u32[]{:S(2)}) copy-start(f32[6,343]{1,0:T(8,128)S(1)} %get-tuple-element.173) | copy-start | bytes 24700
  611.9 16.4 %copy-start.4 = (f32[192,768]{0,1:T(8,128)S(1)}, f32[192,768]{0,1:T(8,128)}, u32[]{:S(2)}) copy-start(f32[192,768]{0,1:T(8,128)} %get-tuple-element.177) | copy-start | bytes 1769476
  627.5 13.0 %copy-start.3 = (f32[768,192]{1,0:T(8,128)S(1)}, f32[768,192]{1,0:T(8,128)}, u32[]{:S(2)}) copy-start(f32[768,192]{1,0:T(8,128)} %get-tuple-element.178) | copy-start | bytes 1769476
  643.3 12.1 %copy-start.7 = (bf16[768,192]{1,0:T(8,128)(2,1)S(1)}, bf16[768,192]{1,0:T(8,128)(2,1)}, u32[]{:S(2)}) copy-start(bf16[768,192]{1,0:T(8,128)(2,1)} %get-tuple-element.179) | copy-start | bytes 884740
  643.3 13.0 %copy-start.13 = (f32[6,343]{1,0:T(8,128)S(1)}, f32[6,343]{1,0:T(8,128)}, u32[]{:S(2)}) copy-start(f32[6,343]{1,0:T(8,128)} %copy-done.12) | copy-start | bytes 24700
  643.3 13.0 %copy-start.14 = (f32[6,343]{1,0:T(8,128)S(1)}, f32[6,343]{1,0:T(8,128)}, u32[]{:S(2)}) copy-start(f32[6,343]{1,0:T(8,128)} %param.31) | copy-start | bytes 24700
  643.3 13.0 %copy-start.15 = (f32[6,343]{1,0:T(8,128)S(1)}, f32[6,343]{1,0:T(8,128)}, u32[]{:S(2)}) copy-start(f32[6,343]{1,0:T(8,128)} %param.43) | copy-start | bytes 24700
  643.3 13.0 %copy-start.16 = (f32[6,343]{1,0:T(8,128)S(1)}, f32[6,343]{1,0:T(8,128)}, u32[]{:S(2)}) copy-start(f32[6,343]{1,0:T(8,128)} %param.37) | copy-start | bytes 24700
  643.3 13.6 %copy-start.11 = (f32[2304]{0:T(1024)S(1)}, f32[2304]{0:T(1024)}, u32[]{:S(2)}) copy-start(f32[2304]{0:T(1024)} %copy-done.10) | copy-start | bytes 27652
  643.4 13.6 %copy-start.17 = (f32[2304]{0:T(1024)S(1)}, f32[2304]{0:T(1024)}, u32[]{:S(2)}) copy-start(f32[2304]{0:T(1024)} %param.44) | copy-start | bytes 27652
  643.4 13.6 %copy-start.18 = (f32[2304]{0:T(1024)S(1)}, f32[2304]{0:T(1024)}, u32[]{:S(2)}) copy-start(f32[2304]{0:T(1024)} %param.38) | copy-start | bytes 27652
Sparse Core Ops, SparseCore 0:
  466.5 134.0 all-reduce.3

commit v2 on v1

--- a/solution.py
+++ b/solution.py
@@ -38,20 +38,6 @@
     return (offsets[..., 0] * extent + offsets[..., 1]) * extent + offsets[..., 2]
 
 
-def region_labels(count, start, length):
-    places = start + jnp.arange(count, dtype=jnp.int32)
-    return (places >= length - WIN).astype(jnp.int32) + (places >= length - SHIFT).astype(jnp.int32)
-
-
-def window_split(tensor):
-    batches, planes, height, breadth, feature = tensor.shape
-    tensor = tensor.reshape(
-        batches, planes // WIN, WIN, height // WIN, WIN, breadth // WIN, WIN, feature
-    )
-    tensor = tensor.transpose(0, 1, 3, 5, 2, 4, 6, 7)
-    return tensor.reshape(-1, WIN**3, feature)
-
-
 def adam_update(weight, first, second, gradient, rate, decay):
     first_new = beta_first * first + (1.0 - beta_first) * gradient
     second_new = beta_second * second + (1.0 - beta_second) * gradient * gradient
@@ -59,29 +45,6 @@
     second_hat = second_new / (1.0 - beta_second**STEP)
     weight_new = weight - rate * (first_hat / (jnp.sqrt(second_hat) + adam_eps) + decay * weight)
     return (first_new, second_new, weight_new)
-
-
-def whole_update(totals, weights, firsts, seconds, rates, decays):
-    squares = jnp.float32(0.0)
-    for member in totals:
-        squares = squares + jnp.sum(member * member)
-    norm_value = jnp.sqrt(squares)
-    factor = jnp.minimum(1.0, clip_bound / (norm_value + 1e-06))
-    outputs = []
-    for member in range(6):
-        clipped = totals[member] * factor
-        outputs.append(
-            (clipped,)
-            + adam_update(
-                weights[member],
-                firsts[member],
-                seconds[member],
-                clipped,
-                rates[member],
-                decays[member],
-            )
-        )
-    return (outputs, norm_value)
 
 
 fl = jnp.float32
@@ -188,6 +151,20 @@
 def block_kernel(
     vox,
     cot,
+    f_in,
+    f_out,
+    f_exp,
+    f_con,
+    bias_ref,
+    vectors_ref,
+    related,
+    take,
+    give,
+    pick,
+    fill,
+    out_res,
+    out_tok,
+    out_total,
     table_ref,
     vec_ref,
     w_in_t,
@@ -198,18 +175,17 @@
     w_exp,
     w_con,
     w_con_t,
-    take,
-    give,
-    pick,
-    fill,
-    out_res,
-    out_tok,
-    d_in,
-    d_out,
-    d_exp,
-    d_con,
+    acc_in,
+    acc_exp,
+    acc_con,
     d_vec,
     d_tab,
+    d_row,
+    bucket,
+    landed,
+    partial_sum,
+    landed_two,
+    total,
     own,
     halo_d,
     halo_w,
@@ -227,6 +203,14 @@
     o_sem,
     r_send,
     r_recv,
+    s1_send,
+    s1_recv,
+    s2_send,
+    s2_recv,
+    s3_send,
+    s3_recv,
+    s4_send,
+    s4_recv,
 ):
     crops = vox.shape[0]
     rows = vox.shape[2]
@@ -296,10 +280,23 @@
             device_id_type=mesh_id,
         )
 
+    crew = lax.axis_size("dp") * peers_d
+    place = lax.axis_index("dp") * peers_d + depth
+
+    def mate(step):
+        other = lax.rem(place + step, crew)
+        return other, {"dp": other // peers_d, "depth": lax.rem(other, peers_d)}
+
+    def across(step):
+        other = lax.rem(column + step, peers_w)
+        return other, {"wide": other}
+
     barrier = pltpu.get_barrier_semaphore()
-    for peer in (d_prev, d_next, w_prev, w_next):
-        pl.semaphore_signal(barrier, inc=1, device_id=peer, device_id_type=mesh_id)
-    pl.semaphore_wait(barrier, 4)
+    for step in range(1, crew):
+        pl.semaphore_signal(barrier, inc=1, device_id=mate(step)[1], device_id_type=mesh_id)
+    for step in range(1, peers_w):
+        pl.semaphore_signal(barrier, inc=1, device_id=across(step)[1], device_id_type=mesh_id)
+    pl.semaphore_wait(barrier, crew + peers_w - 2)
 
     for a in range(2):
         own_copy(0, a).start()
@@ -310,8 +307,68 @@
         return carry
 
     lax.fori_loop(0, crops, send_depth, 0)
-    for ref in (d_in, d_out, d_exp, d_con, d_vec, d_tab):
+    for ref in (acc_in, acc_exp, acc_con, d_vec, d_tab):
         ref[...] = jnp.zeros_like(ref)
+    for source, straight, turned in (
+        (f_in, w_in, w_in_t),
+        (f_out, w_out, w_out_t),
+        (f_exp, w_exp, w_exp_t),
+        (f_con, w_con_t, w_con),
+    ):
+        straight[...] = source[...].astype(bf)
+        turned[...] = source[...].T.astype(bf)
+    for tile in range(vectors_ref.shape[0]):
+        vec_ref[128 * tile : 128 * tile + 128, :] = jnp.broadcast_to(
+            vectors_ref[tile : tile + 1, :], (128, 128)
+        ).T
+
+    def chooser(places):
+        return (
+            lax.broadcasted_iota(jnp.int32, (384, 128), 0)
+            == jnp.broadcast_to(places, (384, 128))
+        ).astype(bf)
+
+    def eight(block):
+        return pl.ds(pl.multiple_of(8 * block, 8), 8)
+
+    def thirds(v):
+        high = v.astype(bf)
+        rest = v - high.astype(fl)
+        middle = rest.astype(bf)
+        return jnp.concatenate([high, middle, (rest - middle.astype(fl)).astype(bf)], axis=0)
+
+    def ends(v):
+        return v[:8] + v[8:16] + v[16:24]
+
+    def code(at, window, edge):
+        last_d = (depth == peers_d - 1).astype(jnp.int32)
+        last_w = (column == peers_w - 1).astype(jnp.int32)
+        d, h, w = at // 16, lax.rem(at // 4, 4), lax.rem(at, 4)
+        return (
+            last_d * (d >= SHIFT).astype(jnp.int32) * 4
+            + edge * (h >= SHIFT).astype(jnp.int32) * 2
+            + last_w * window * (w >= SHIFT).astype(jnp.int32)
+        )
+
+    bias_parts = thirds(bias_ref[...])
+
+    def table_rows(block, carry):
+        near = related[eight(block), :]
+        found = [ends(dot(bias_parts, chooser(near[k : k + 1]))) for k in range(8)]
+        lane = lax.broadcasted_iota(jnp.int32, (8, 128), 1)
+        j = lax.broadcasted_iota(jnp.int32, (8, 128), 0) + 8 * block
+        window, i = lane // TOK, lax.rem(lane, TOK)
+        for edge in range(2):
+            differ = code(i, window, edge) != code(j, window, edge)
+            mask = jnp.where(differ, mask_fill, 0.0)
+            for head in range(HEADS):
+                values = jnp.concatenate([row[head : head + 1, :] for row in found], axis=0)
+                table_ref[edge, eight(block), 128 * head : 128 * head + 128] = (
+                    values + mask
+                ) * LOG2E
+        return carry
+
+    lax.fori_loop(0, TOK // 8, table_rows, 0)
 
     def starts(u):
         first = pl.multiple_of(u * TOK + 16, 16)
@@ -470,10 +527,10 @@
         grad_one = dot(w_in[...], triple_low)
         token_grad = middle_grad + unit_back(grad_one, unit_one, inverse_one, vec(0))
         put(1, token_grad.astype(bf))
-        d_in[...] += dot_nt(triple_low, jnp.concatenate([entry_one, ones], axis=0))
-        d_out[...] += dot_nt(branch_low, jnp.concatenate([mixed, ones], axis=0))
-        d_exp[...] += dot_nt(hidden_low, jnp.concatenate([entry_two, ones], axis=0))
-        d_con[...] += dot_nt(active, up_low)
+        acc_in[: 3 * width, :] += dot_nt(triple_low, jnp.concatenate([entry_one, ones], axis=0))
+        acc_in[3 * width :, :] += dot_nt(branch_low, jnp.concatenate([mixed, ones], axis=0))
+        acc_exp[...] += dot_nt(hidden_low, jnp.concatenate([entry_two, ones], axis=0))
+        acc_con[...] += dot_nt(active, up_low)
         d_vec[0:width, :] += fold(grad_one * unit_one)
         d_vec[width : 2 * width, :] += fold(grad_one)
         d_vec[2 * width : 3 * width, :] += fold(grad_two * unit_two)
@@ -514,7 +571,151 @@
         return carry
 
     lax.fori_loop(0, crops, crop, 0)
+
+    extra = 18 * width
+    for tile in range(12):
+        acc, at = ((acc_in, 128 * tile), (acc_exp, 128 * (tile - 6)))[tile // 6]
+        turned = acc[at : at + 128, :].T
+        bucket[width * tile : width * tile + width, :] = turned[:width].astype(bf)
+        d_row[tile : tile + 1, :] = turned[width : width + 1]
+    for tile in range(6):
+        bucket[width * (12 + tile) : width * (13 + tile), :] = (
+            acc_con[128 * tile : 128 * tile + 128, :].T.astype(bf)
+        )
+    for tile in range(8):
+        size = min(128, 5 * width - 128 * tile)
+        d_row[12 + tile : 13 + tile, :size] = jnp.sum(
+            d_vec[128 * tile : 128 * tile + size, :].T, 0, keepdims=True
+        )
+    d_row[19:20, 64:] = jnp.zeros((1, 64), fl)
+
+    def table_sums(block, carry):
+        near = related[eight(block), :]
+        held = d_tab[eight(block), :]
+        for k in range(8):
+            rows_k = jnp.concatenate(
+                [held[k : k + 1, 128 * head : 128 * head + 128] for head in range(HEADS)]
+                + [jnp.zeros((2, 128), fl)],
+                axis=0,
+            )
+            carry = carry + dot_nt(thirds(rows_k), chooser(near[k : k + 1]))
+        return carry
+
+    sums = ends(lax.fori_loop(0, TOK // 8, table_sums, jnp.zeros((24, 384), fl)))
+    for tile in range(3):
+        d_row[24 + 8 * tile : 32 + 8 * tile, :] = sums[:, 128 * tile : 128 * tile + 128]
+    d_row[20:24, :] = jnp.zeros((4, 128), fl)
+    bucket[extra : extra + 48, :] = d_row[...].astype(bf)
+    length = bucket.shape[0]
+    if length > extra + 48:
+        bucket[extra + 48 :, :] = jnp.zeros((length - extra - 48, 128), bf)
+
+    share = length // crew
+    piece = share // peers_w
+
+    def span(start, size):
+        return pl.ds(pl.multiple_of(start, 16), size)
+
+    def first_copy(step):
+        other, peer = mate(step)
+        return pltpu.make_async_remote_copy(
+            src_ref=bucket.at[span(other * share, share)],
+            dst_ref=landed.at[step - 1],
+            send_sem=s1_send.at[step - 1],
+            recv_sem=s1_recv.at[step - 1],
+            device_id=peer,
+            device_id_type=mesh_id,
+        )
+
+    def second_copy(step):
+        other, peer = across(step)
+        return pltpu.make_async_remote_copy(
+            src_ref=partial_sum.at[span(other * piece, piece)],
+            dst_ref=landed_two.at[step - 1],
+            send_sem=s2_send.at[step - 1],
+            recv_sem=s2_recv.at[step - 1],
+            device_id=peer,
+            device_id_type=mesh_id,
+        )
+
+    def third_copy(step):
+        rows_mine = total.at[span(place * share + column * piece, piece)]
+        return pltpu.make_async_remote_copy(
+            src_ref=rows_mine,
+            dst_ref=rows_mine,
+            send_sem=s3_send.at[step - 1],
+            recv_sem=s3_recv.at[step - 1],
+            device_id=across(step)[1],
+            device_id_type=mesh_id,
+        )
+
+    def fourth_copy(step):
+        rows_mine = total.at[span(place * share, share)]
+        return pltpu.make_async_remote_copy(
+            src_ref=rows_mine,
+            dst_ref=rows_mine,
+            send_sem=s4_send.at[step - 1],
+            recv_sem=s4_recv.at[step - 1],
+            device_id=mate(step)[1],
+            device_id_type=mesh_id,
+        )
+
+    def third_arrival(step):
+        other = lax.rem(column + peers_w - step, peers_w)
+        rows_there = total.at[span(place * share + other * piece, piece)]
+        return pltpu.make_async_remote_copy(
+            src_ref=rows_there,
+            dst_ref=rows_there,
+            send_sem=s3_send.at[step - 1],
+            recv_sem=s3_recv.at[step - 1],
+            device_id=across(step)[1],
+            device_id_type=mesh_id,
+        )
+
+    def fourth_arrival(step):
+        other = lax.rem(place + crew - step, crew)
+        rows_there = total.at[span(other * share, share)]
+        return pltpu.make_async_remote_copy(
+            src_ref=rows_there,
+            dst_ref=rows_there,
+            send_sem=s4_send.at[step - 1],
+            recv_sem=s4_recv.at[step - 1],
+            device_id=mate(step)[1],
+            device_id_type=mesh_id,
+        )
+
+    for step in range(1, crew):
+        first_copy(step).start()
     merge(crops - 1)
+    for step in range(1, crew):
+        first_copy(step).wait_recv()
+    summed = bucket[span(place * share, share), :].astype(fl)
+    for step in range(1, crew):
+        summed = summed + landed[step - 1].astype(fl)
+    partial_sum[...] = summed.astype(bf)
+    for step in range(1, peers_w):
+        second_copy(step).start()
+    for step in range(1, peers_w):
+        second_copy(step).wait_recv()
+    summed = partial_sum[span(column * piece, piece), :].astype(fl)
+    for step in range(1, peers_w):
+        summed = summed + landed_two[step - 1].astype(fl)
+    total[span(place * share + column * piece, piece), :] = summed.astype(bf)
+    for step in range(1, peers_w):
+        third_copy(step).start()
+    for step in range(1, peers_w):
+        third_arrival(step).wait_recv()
+    for step in range(1, crew):
+        fourth_copy(step).start()
+    for step in range(1, crew):
+        fourth_arrival(step).wait_recv()
+    out_total[...] = total[...]
+    for step in range(1, crew):
+        first_copy(step).wait_send()
+        fourth_copy(step).wait_send()
+    for step in range(1, peers_w):
+        second_copy(step).wait_send()
+        third_copy(step).wait_send()
 
     def finish(c, carry):
         for a in range(2):
@@ -535,28 +736,52 @@
     lax.fori_loop(crops - 2, crops, close, 0)
 
 
-def block_call(voxels, cotangent, table, vec_wide, mats):
+def block_call(voxels, cotangent, matrices, bias_table, vectors):
     crops, planes, rows, width = voxels.shape
     hid = 4 * width
     whole = pl.BlockSpec(memory_space=pltpu.VMEM)
     far = pl.BlockSpec(memory_space=pl.ANY)
-    consts = [table, vec_wide] + mats + placement()
+    related = relative_index().T
+    related = jnp.asarray(np.concatenate([related, related], axis=1), jnp.int32)
+    consts = list(matrices) + [bias_table, vectors, related] + placement()
     sem = pltpu.SemaphoreType.DMA
+    crew = lax.axis_size("dp") * lax.axis_size("depth")
+    peers_w = lax.axis_size("wide")
+    unit_rows = 16 * crew * peers_w
+    length = -(-(18 * width + 48) // unit_rows) * unit_rows
+    share = length // crew
+    piece = share // peers_w
     return pl.pallas_call(
         block_kernel,
         in_specs=[far, far] + [whole] * len(consts),
-        out_specs=[far, far] + [whole] * 6,
+        out_specs=[far, far, whole],
         out_shape=[
             jax.ShapeDtypeStruct(voxels.shape, bf),
             jax.ShapeDtypeStruct(voxels.shape, bf),
-            jax.ShapeDtypeStruct((3 * width, width + 16), fl),
-            jax.ShapeDtypeStruct((width, width + 16), fl),
-            jax.ShapeDtypeStruct((hid, width + 16), fl),
-            jax.ShapeDtypeStruct((hid, width), fl),
-            jax.ShapeDtypeStruct((5 * width, 128), fl),
-            jax.ShapeDtypeStruct((TOK, HEADS * 128), fl),
+            jax.ShapeDtypeStruct((length, 128), bf),
         ],
         scratch_shapes=[
+            pltpu.VMEM((2, TOK, HEADS * 128), fl),
+            pltpu.VMEM((12 * width, 128), fl),
+            pltpu.VMEM((3 * width, width), bf),
+            pltpu.VMEM((width, 3 * width), bf),
+            pltpu.VMEM((width, width), bf),
+            pltpu.VMEM((width, width), bf),
+            pltpu.VMEM((hid, width), bf),
+            pltpu.VMEM((width, hid), bf),
+            pltpu.VMEM((hid, width), bf),
+            pltpu.VMEM((width, hid), bf),
+            pltpu.VMEM((4 * width, width + 16), fl),
+            pltpu.VMEM((hid, width + 16), fl),
+            pltpu.VMEM((hid, width), fl),
+            pltpu.VMEM((5 * width, 128), fl),
+            pltpu.VMEM((TOK, HEADS * 128), fl),
+            pltpu.VMEM((48, 128), fl),
+            pltpu.VMEM((length, 128), bf),
+            pltpu.VMEM((crew - 1, share, 128), bf),
+            pltpu.VMEM((share, 128), bf),
+            pltpu.VMEM((peers_w - 1, piece, 128), bf),
+            pltpu.VMEM((length, 128), bf),
             pltpu.VMEM((2, 2, 2, rows, width), bf),
             pltpu.VMEM((crops, 2, 2, rows, width), bf),
             pltpu.VMEM((crops, 2, rows, width), bf),
@@ -574,6 +799,14 @@
             sem((2, 2)),
             sem((2, 2)),
             sem((crops, 2)),
+            sem((crew - 1,)),
+            sem((crew - 1,)),
+            sem((peers_w - 1,)),
+            sem((peers_w - 1,)),
+            sem((peers_w - 1,)),
+            sem((peers_w - 1,)),
+            sem((crew - 1,)),
+            sem((crew - 1,)),
         ],
         compiler_params=pltpu.CompilerParams(
             vmem_limit_bytes=60 * 2**20, collective_id=0, has_side_effects=True
@@ -582,33 +815,108 @@
     )(voxels, cotangent, *consts)
 
 
-def make_tables(bias_table, planes, height, breadth):
-    extent = (2 * WIN - 1) ** 3
-    selector = (
-        jnp.asarray(relative_index().T.reshape(-1), jnp.int32)[:, None]
-        == jnp.arange(extent, dtype=jnp.int32)[None, :]
-    ).astype(fl)
-    pair_bias = jnp.einsum("hr,pr->hp", bias_table, selector, precision=lax.Precision.HIGHEST)
-    pair_bias = pair_bias.reshape(HEADS, TOK, TOK)
-    plane_labels = region_labels(
-        planes, lax.axis_index("depth") * planes, planes * lax.axis_size("depth")
+def update_kernel(*refs):
+    far_in, total, params, far_out, outs, norm_ref, held, in_sem, out_sem = (
+        refs[0:2], refs[2], refs[3:21], refs[21:23], refs[23:51], refs[51], refs[52],
+        refs[53], refs[54],
     )
-    column_labels = region_labels(
-        breadth, lax.axis_index("wide") * breadth, breadth * lax.axis_size("wide")
+    crops = far_in[0].shape[0]
+
+    def fetch(a, c):
+        return pltpu.make_async_copy(far_in[a].at[c], held.at[a, c], in_sem.at[a, c])
+
+    def store(a, c):
+        return pltpu.make_async_copy(held.at[a, c], far_out[a].at[c], out_sem.at[a, c])
+
+    for a in range(2):
+        for c in range(crops):
+            fetch(a, c).start()
+    for a in range(2):
+        for c in range(crops):
+            fetch(a, c).wait()
+            store(a, c).start()
+    width = 192
+
+    def slab(tile):
+        return total[width * tile : width * tile + width, :].astype(fl)
+
+    small = total[18 * width : 18 * width + 48, :].astype(fl)
+    low_half = slab(4)
+    grads = [
+        jnp.concatenate([slab(k) for k in range(4)] + [low_half[:, :64]], axis=1),
+        jnp.concatenate([low_half[:, 64:], slab(5)], axis=1),
+        jnp.concatenate([slab(k) for k in range(6, 12)], axis=1),
+        jnp.concatenate([slab(k) for k in range(12, 18)], axis=1),
+    ]
+    flat_bias = jnp.concatenate([small[k : k + 1] for k in range(12)], axis=1)
+    flat_sum = jnp.concatenate([small[k : k + 1] for k in range(12, 20)], axis=1)
+
+    def cut(flat, index):
+        return flat[:, width * index : width * index + width]
+
+    table = jnp.concatenate([small[24:32], small[32:40], small[40:48]], axis=1)
+    grads.append(table[:HEADS, : params[4].shape[1]])
+    grads.append(
+        jnp.concatenate(
+            [
+                cut(flat_sum, 0), cut(flat_sum, 1), cut(flat_bias, 0), cut(flat_bias, 2),
+                cut(flat_bias, 3), cut(flat_sum, 2), cut(flat_sum, 3), cut(flat_sum, 4),
+                flat_bias[:, 4 * width : 8 * width],
+            ],
+            axis=1,
+        )
     )
-    tables = []
-    for place in (0, height - WIN):
-        height_labels = region_labels(height, 0, height)[place : place + WIN]
-        labels = (
-            plane_labels[:, None, None] * 9
-            + height_labels[None, :, None] * 3
-            + column_labels[None, None, :]
-        )
-        labels = window_split(labels[None, :, :, :, None])[..., 0]
-        masks = jnp.where(labels[:, :, None] == labels[:, None, :], 0.0, mask_fill).astype(fl)
-        both = pair_bias[:, None] + masks[None]
-        tables.append(both.transpose(2, 0, 1, 3).reshape(TOK, HEADS * 128))
-    return jnp.stack(tables) * LOG2E, selector
+    squares = jnp.zeros((1, 1), fl)
+    for grad in grads:
+        squares = squares + jnp.sum(
+            jnp.sum(grad * grad, 0, keepdims=True), 1, keepdims=True
+        )
+    norm_value = jnp.sqrt(squares)
+    norm_ref[...] = norm_value
+    factor = jnp.minimum(1.0, clip_bound / (norm_value + 1e-06))
+    for member in range(6):
+        matrix = member < 4
+        clipped = grads[member] * factor
+        first, second, fresh = adam_update(
+            params[member][...],
+            params[6 + member][...],
+            params[12 + member][...],
+            clipped,
+            rate_matrix if matrix else rate_vector,
+            weight_decay if matrix else 0.0,
+        )
+        for place, value in enumerate((clipped, first, second, fresh)):
+            outs[4 * member + place][...] = value
+        if matrix:
+            outs[24 + member][...] = fresh.astype(bf)
+    for a in range(2):
+        for c in range(crops):
+            store(a, c).wait()
+
+
+def update_call(result, token_grad, total, params):
+    whole = pl.BlockSpec(memory_space=pltpu.VMEM)
+    far = pl.BlockSpec(memory_space=pl.ANY)
+    shapes = []
+    for member in range(6):
+        shapes = shapes + [jax.ShapeDtypeStruct(params[member].shape, fl)] * 4
+    for member in range(4):
+        shapes.append(jax.ShapeDtypeStruct(params[member].shape, bf))
+    shapes.append(jax.ShapeDtypeStruct((1, 1), fl))
+    big = jax.ShapeDtypeStruct(result.shape, bf)
+    return pl.pallas_call(
+        update_kernel,
+        in_specs=[far, far, whole] + [whole] * 18,
+        out_specs=[far, far] + [whole] * 29,
+        out_shape=[big, big] + shapes,
+        scratch_shapes=[
+            pltpu.VMEM((2,) + result.shape, bf),
+            pltpu.SemaphoreType.DMA((2, result.shape[0])),
+            pltpu.SemaphoreType.DMA((2, result.shape[0])),
+        ],
+        compiler_params=pltpu.CompilerParams(vmem_limit_bytes=56 * 2**20),
+        name="update",
+    )(result, token_grad, total, *params)
 
 
 def local(
@@ -634,76 +942,45 @@
     vectors_second,
 ):
     batches, planes, height, breadth, width = voxels.shape
-    table, selector = make_tables(bias_table, planes, height, breadth)
-    vec_wide = jnp.broadcast_to(vectors[:, None], (vectors.shape[0], 128))
-    in_low = project_in.astype(bf)
-    out_low = project_out.astype(bf)
-    expand_low = expand.astype(bf)
-    contract_low = contract.astype(bf)
-    mats = [
-        in_low.T, in_low, out_low.T, out_low,
-        expand_low.T, expand_low, contract_low, contract_low.T,
-    ]
     flat = (batches, planes, height * breadth, width)
-    result, token_grad, d_in, d_out, d_exp, d_con, d_vec, d_tab = block_call(
-        voxels.reshape(flat), cotangent.reshape(flat), table, vec_wide, mats
+    result, token_grad, total = block_call(
+        voxels.reshape(flat),
+        cotangent.reshape(flat),
+        (project_in, project_out, expand, contract.T),
+        jnp.pad(bias_table, ((0, 2), (0, 384 - bias_table.shape[1]))),
+        vectors.reshape(-1, 128),
     )
-    sums = jnp.sum(d_vec, -1).reshape(5, width)
-    vector_grad = jnp.concatenate(
-        [
-            sums[0],
-            sums[1],
-            d_in[:width, width],
-            d_in[2 * width :, width],
-            d_out[:, width],
-            sums[2],
-            sums[3],
-            sums[4],
-            d_exp[:, width],
-        ]
-    )
-    table_grad = d_tab.reshape(TOK, HEADS, 2, TOK).sum(2).transpose(1, 0, 2).reshape(HEADS, -1)
-    table_grad = jnp.einsum("hp,pr->hr", table_grad, selector, precision=lax.Precision.HIGHEST)
-    weights = [project_in, project_out, expand, contract, bias_table, vectors]
-    firsts = [
+    params = [
+        project_in,
+        project_out,
+        expand,
+        contract.T,
+        bias_table,
+        vectors.reshape(1, -1),
         project_in_first,
         project_out_first,
         expand_first,
-        contract_first,
+        contract_first.T,
         bias_table_first,
-        vectors_first,
-    ]
-    seconds = [
+        vectors_first.reshape(1, -1),
         project_in_second,
         project_out_second,
         expand_second,
-        contract_second,
+        contract_second.T,
         bias_table_second,
-        vectors_second,
+        vectors_second.reshape(1, -1),
     ]
-    rates = [rate_matrix] * 4 + [rate_vector] * 2
-    decays = [weight_decay] * 4 + [0.0, 0.0]
-    totals = list(
-        lax.psum(
-            (
-                d_in[:, :width].T,
-                d_out[:, :width].T,
-                d_exp[:, :width].T,
-                d_con,
-                table_grad,
-                vector_grad,
-            ),
-            ("dp", "depth", "wide"),
-        )
+    done = update_call(result, token_grad, total, params)
+    outs = list(done[2:30])
+    for place in range(20, 24):
+        outs[place] = outs[place].reshape(-1)
+    for place in (12, 13, 14, 15, 27):
+        outs[place] = outs[place].T
+    return (
+        (done[0].reshape(voxels.shape), done[1].reshape(voxels.shape))
+        + tuple(outs)
+        + (done[30].reshape(()),)
     )
-    outputs, norm_value = whole_update(totals, weights, firsts, seconds, rates, decays)
-    flat_out = [result.reshape(voxels.shape), token_grad.reshape(voxels.shape)]
-    for member in range(6):
-        flat_out = flat_out + list(outputs[member])
-    for member in range(4):
-        flat_out = flat_out + [outputs[member][3].astype(bf)]
-    flat_out = flat_out + [norm_value]
-    return tuple(flat_out)
 
 
 def solution(mesh):

time: 685 us -> 478 us (0.70)
  local copies, waits for them, and re-layouts: 85.2 us -> 5.24 us
  waiting for transfers between devices: 65.4 us -> 0 us
  blocking collectives: 38.9 us -> 0 us
  Pallas kernels: 430 us -> 466 us
  other arithmetic: 34.4 us -> 5.3 us
  between operations: 19.5 us -> 0.69 us
  matrix products: 7.3 us -> 0 us
    unnamed x72 -> x0, local copies, waits for them, and re-layouts: 65.7 us -> none
    psum x1 -> x0, waiting for transfers between devices: 65.3 us -> none  [local(): lax.psum((d_in[:, :width].T, d_out[:, :width].T, d_exp[:, :width].T, d_co...]
    psum x1 -> x0, blocking collectives: 38.9 us -> none  [local(): lax.psum((d_in[:, :width].T, d_out[:, :width].T, d_exp[:, :width].T, d_co...]
    pallas_call x0 -> x1, Pallas kernels: none -> 20.9 us  [update_call(): pl.pallas_call(update_kernel, in_specs=[far, far, whole] + [whole] * 18,...]
    convert_element_type x8 -> x0, other arithmetic: 17.4 us -> none  [the longest x4 11.2 us: local(): flat_out = flat_out + [outputs[member][3].astype(bf)]]
    pallas_call x1, Pallas kernels: 430 us -> 445 us  [block_call(): pl.pallas_call(block_kernel, in_specs=[far, far] + [whole] * len(consts),...]
    reduce_sum x8 -> x0, other arithmetic: 9.17 us -> none  [the longest x6 8.48 us: whole_update(): squares = squares + jnp.sum(member * member)]
    transpose x7 -> x0, local copies, waits for them, and re-layouts: 8.3 us -> none  [the longest x3 2.54 us: local(): mats = [in_low.T, in_low, out_low.T, out_low, expand_low.T, expand_low, c...]
  transfers between devices with their start and end apart: 1 -> 0, of which waited for: 1 -> 0; matrix products, arithmetic and copies ran while one was open for 4% -> 0% of each run, Pallas kernels for 0% -> 0%
where the time goes in v2:
time: 478 us; the launch traced here: 477 us
  Pallas kernels  466 us (97%)
  other arithmetic  5.3 us (1%)
  local copies, waits for them, and re-layouts  5.24 us (1%)
    pallas_call x1, Pallas kernels, block_call(): pl.pallas_call(block_kernel, in_specs=[far, far] + [whole] * len(consts),...  445 us
    pallas_call x1, Pallas kernels, update_call(): pl.pallas_call(update_kernel, in_specs=[far, far, whole] + [whole] * 18,...  20.9 us

profile of v2, /device:TPU:1, one launch (start us, length us, event | category | flops | bytes accessed | tf_op | source)
XLA Modules:
  0.0 476.9 jit_solution(8450455386118811824)
XLA Ops:
  0.7 1.3 reshape.105.refs_14_
  2.0 1.3 reshape.106.refs_20_
  3.3 1.3 reshape.104.refs_8_
  4.6 1.3 pad.4.bias_ref
  5.9 444.7 %block.1 = (bf16[8,4,512,192]{3,2,1,0:T(8,128)(2,1)}, bf16[8,4,512,192]{3,2,1,0:T(8,128)(2,1)}, bf16[3584,128]{1,0:T(8,128)(2,1)}) custom-call(bf16[8,4,512,192]{3,2,1,0:T(8,128)(2,1)} %bitcast.14, bf16[8,4,512,192]{3,2,1,0:T(8,128)(2,1)} %bitcast.15, f32[192,576]{1,0:T(8,128)} %refs_3_.1, f32[192,192]{1,0:T(8,128)} %refs_4_.1, f32[192,768]{1,0:T(8,128)} %refs_5_.1, ...), custom_call_target="tpu_custom_call" | custom-call | tf_op jit(solution)/shard_map/block/pallas_call | solution.py:754
  450.6 20.9 %update.1 = (bf16[8,4,512,192]{3,2,1,0:T(8,128)(2,1)}, bf16[8,4,512,192]{3,2,1,0:T(8,128)(2,1)}, f32[192,576]{1,0:T(8,128)}, f32[192,576]{1,0:T(8,128)}, f32[192...) custom-call(bf16[8,4,512,192]{3,2,1,0:T(8,128)(2,1)} %get-tuple-elem, ...), custom_call_target="tpu_custom_call" | custom-call | tf_op jit(solution)/shard_map/update/pallas_call | solution.py:907
  471.6 1.3 reduce
  472.9 1.3 reduce.1
  474.2 1.3 reduce.2
  475.5 1.3 reduce.3

commit v3 on v2

v3 whole, which is shorter than its diff:
```python
from functools import partial

import jax
import jax.numpy as jnp
import numpy as np
from jax import lax
from jax.experimental import pallas as pl
from jax.experimental.pallas import tpu as pltpu
from jax.sharding import PartitionSpec as P

HEADS = 6
WIN = 4
SHIFT = 2
STEP = 10
TOK = WIN**3
GROUP = 4
LANES = GROUP * TOK

norm_eps = 1e-05
mask_fill = -100.0
clip_bound = 1000.0
rate_matrix = 0.1
rate_vector = 0.6
weight_decay = 0.01
beta_first = 0.9
beta_second = 0.999
adam_eps = 1e-08
LOG2E = 1.4426950408889634
INV_SQRT2 = 0.7071067811865476
INV_SQRT2PI = 0.3989422804014327


def relative_index():
    extent = 2 * WIN - 1
    corner = np.arange(WIN)
    places = np.stack(np.meshgrid(corner, corner, corner, indexing="ij"), -1).reshape(-1, 3)
    offsets = places[:, None, :] - places[None, :, :] + WIN - 1
    return (offsets[..., 0] * extent + offsets[..., 1]) * extent + offsets[..., 2]


def adam_update(weight, first, second, gradient, rate, decay):
    first_new = beta_first * first + (1.0 - beta_first) * gradient
    second_new = beta_second * second + (1.0 - beta_second) * gradient * gradient
    first_hat = first_new / (1.0 - beta_first**STEP)
    second_hat = second_new / (1.0 - beta_second**STEP)
    weight_new = weight - rate * (first_hat / (jnp.sqrt(second_hat) + adam_eps) + decay * weight)
    return (first_new, second_new, weight_new)


fl = jnp.float32
bf = jnp.bfloat16


def dot(a, b):
    return jnp.dot(a, b, preferred_element_type=fl)


def dot_nt(a, b):
    return lax.dot_general(a, b, (((1,), (1,)), ((), ())), preferred_element_type=fl)


def wide(v, lanes):
    return jnp.concatenate([v] * (lanes // v.shape[1]), axis=1)


def unit_norm(v):
    width = v.shape[0]
    mean = jnp.sum(v, 0, keepdims=True) * (1.0 / width)
    centred = v - mean
    inverse = lax.rsqrt(jnp.sum(centred * centred, 0, keepdims=True) * (1.0 / width) + norm_eps)
    return centred * inverse, inverse


def unit_back(grad, unit, inverse, gain):
    width = grad.shape[0]
    scaled = grad * gain
    inner = jnp.sum(scaled, 0, keepdims=True) * (1.0 / width)
    along = jnp.sum(scaled * unit, 0, keepdims=True) * (1.0 / width)
    return inverse * (scaled - inner - unit * along)


def fold(v):
    total = v[:, :128]
    for lane in range(128, v.shape[1], 128):
        total = total + v[:, lane : lane + 128]
    return total


def two_windows(compact, first_half):
    zero = jnp.zeros_like(compact)
    return jnp.concatenate(
        [jnp.where(first_half, compact, zero), jnp.where(first_half, zero, compact)], axis=0
    )


def two_heads(ref, head_pair, lanes):
    at = 64 * head_pair
    zero = jnp.zeros((32, 128), bf)
    return jnp.concatenate(
        [
            jnp.concatenate([ref[at : at + 32, lanes], zero], axis=1),
            jnp.concatenate([zero, ref[at + 32 : at + 64, lanes]], axis=1),
        ],
        axis=0,
    )


def cross(token_major, low, first, head_pair, first_half):
    right = two_heads(low, head_pair, slice(first, first + 128))
    if head_pair == 1:
        right = jnp.concatenate([jnp.zeros((64, 256), bf), right], axis=0)
        left = token_major[first : first + 128, 0:128]
    else:
        at = 64 * head_pair
        left = token_major[first : first + 128, at : at + 64]
    full = dot(left, right)
    out = []
    for head in range(2):
        block = full[:, 128 * head : 128 * head + 128]
        out.append(jnp.where(first_half, block[:TOK], block[TOK:]))
    return out


def weave(one, other):
    whole_one = sum(weight for weight, _ in one) + 1e-9
    whole_other = sum(weight for weight, _ in other) + 1e-9
    merged, done_one, done_other = [], 0.0, 0.0
    one, other = list(one), list(other)
    while one or other:
        if not other or (
            one
            and (done_one + one[0][0] / 2) / whole_one
            <= (done_other + other[0][0] / 2) / whole_other
        ):
            merged.append(one.pop(0))
            done_one += merged[-1][0]
        else:
            merged.append(other.pop(0))
            done_other += merged[-1][0]
    return merged


def placement():
    take = np.zeros((LANES + TOK, LANES), np.float32)
    pick = np.zeros((TOK, LANES), np.float32)
    for hw in range(2):
        for ww in range(2):
            for d in range(WIN):
                for hh in range(WIN):
                    for wl in range(WIN):
                        t = ((hw * 2 + ww) * WIN + d) * 16 + hh * 4 + wl
                        h, w = 4 * hw + hh, 4 * ww + wl
                        if w < 2 * WIN - SHIFT:
                            row = d * 64 + h * 8 + w + SHIFT
                        else:
                            row = LANES + d * 16 + h * 2 + w - (2 * WIN - SHIFT)
                        take[row, t] = 1.0
    for d in range(WIN):
        for h in range(2 * WIN):
            for w in range(SHIFT):
                pick[d * 16 + h * 2 + w, d * 64 + h * 8 + w] = 1.0
    return [jnp.asarray(m, bf) for m in (take, take.T, pick, pick.T)]


WIDTH = 192
HID = 4 * WIDTH
SPAN = 2 * LANES
PAIRS = SPAN // 128
SUBS = SPAN // LANES
SLOTS = 3
BOTH = {
    "up": ((WIDTH, SPAN), fl),
    "up_low": ((WIDTH, SPAN), bf),
    "unit_one": ((WIDTH, SPAN), fl),
    "inverse_one": ((8, SPAN), fl),
    "entry_one": ((WIDTH + 16, SPAN), bf),
    "query": ((WIDTH, SPAN), bf),
    "keys": ((WIDTH, SPAN), bf),
    "values": ((WIDTH, SPAN), bf),
    "values_t": ((SPAN, WIDTH), bf),
    "probs": ((PAIRS, HEADS, TOK, 128), fl),
    "probs_wide": ((PAIRS, HEADS, 128, 128), bf),
    "mixed": ((WIDTH + 16, SPAN), bf),
    "unit_two": ((WIDTH, SPAN), fl),
    "inverse_two": ((8, SPAN), fl),
    "entry_two": ((WIDTH + 16, SPAN), bf),
    "slope": ((HID, SPAN), fl),
    "active": ((HID, SPAN), bf),
    "edge_res": ((SUBS, WIDTH, TOK), bf),
}
ONCE = {
    "x": ((WIDTH, SPAN), fl),
    "keys_t": ((SPAN, WIDTH), bf),
    "middle": ((WIDTH, SPAN), fl),
    "result": ((WIDTH, SPAN), bf),
    "hidden_low": ((HID, SPAN), bf),
    "grad_two": ((WIDTH, SPAN), fl),
    "middle_grad": ((WIDTH, SPAN), fl),
    "branch_low": ((WIDTH, SPAN), bf),
    "mixed_low": ((WIDTH, SPAN), bf),
    "triple_low": ((3 * WIDTH, SPAN), bf),
    "grad_one": ((WIDTH, SPAN), fl),
    "token_grad": ((WIDTH, SPAN), bf),
}
WEIGHTS = {
    "table": ((2, TOK, HEADS * 128), fl),
    "vec": ((5 * WIDTH, 128), fl),
    "w_in_t": ((3 * WIDTH, WIDTH + 16), bf),
    "w_in": ((WIDTH, 3 * WIDTH), bf),
    "w_out_t": ((WIDTH, WIDTH + 16), bf),
    "w_out": ((WIDTH, WIDTH), bf),
    "w_exp_t": ((HID, WIDTH + 16), bf),
    "w_exp": ((WIDTH, HID), bf),
    "w_con": ((HID, WIDTH), bf),
    "w_con_t": ((WIDTH, HID), bf),
    "acc_in": ((4 * WIDTH, WIDTH + 16), fl),
    "acc_exp": ((HID, WIDTH + 16), fl),
    "acc_con": ((HID, WIDTH), fl),
    "d_vec": ((5 * WIDTH, 128), fl),
    "d_tab": ((TOK, HEADS * 128), fl),
    "d_row": ((48, 128), fl),
}
GAIN_ONE, SHIFT_ONE, GAIN_TWO, SHIFT_TWO, CON_BIAS = (WIDTH * k for k in range(5))
scale = 32 ** (-0.5)


def forward_tasks(r, first_half, tokens_of, edge, put):
    tasks = []
    slots = [(k, hp) for k in range(PAIRS) for hp in range(3)]
    held = {}

    def vec(at, lanes=SPAN):
        return wide(r["vec"][at : at + WIDTH, :], lanes)

    def fetch():
        rows = []
        for s in range(SUBS):
            rows = rows + tokens_of(s)
        moved = dot(jnp.concatenate(rows, axis=0), r["take"][...])
        for s in range(SUBS):
            lanes = slice(LANES * s, LANES * s + LANES)
            at = 2 * WIDTH * s
            up = moved[at + WIDTH : at + 2 * WIDTH]
            r["x"][:, lanes] = moved[at : at + WIDTH]
            r["up"][:, lanes] = up
            r["up_low"][:, lanes] = up.astype(bf)

    def norm_one():
        unit_vals, inverse = unit_norm(r["x"][...])
        r["unit_one"][...] = unit_vals
        r["inverse_one"][...] = jnp.broadcast_to(inverse, (8, SPAN))
        r["entry_one"][:WIDTH] = (unit_vals * vec(GAIN_ONE) + vec(SHIFT_ONE)).astype(bf)

    def project():
        triple = dot(r["w_in_t"][...], r["entry_one"][...]).astype(bf)
        r["query"][...] = triple[:WIDTH]
        r["keys"][...] = triple[WIDTH : 2 * WIDTH]
        r["values"][...] = triple[2 * WIDTH :]

    def turn():
        r["keys_t"][...] = r["keys"][...].T
        r["values_t"][...] = r["values"][...].T

    def scores(t):
        k, hp = slots[t]
        held["s", t] = cross(r["keys_t"], r["query"], 128 * k, hp, first_half)

    def soft(t):
        k, hp = slots[t]
        pieces = held.pop(("s", t))
        wides = []
        for head in (2 * hp, 2 * hp + 1):
            which = edge if k == PAIRS - 1 else 0
            s = (
                pieces[head - 2 * hp] * (scale * LOG2E)
                + r["table"][which, :, 128 * head : 128 * head + 128]
            )
            e = jnp.exp2(s - jnp.max(s, 0, keepdims=True))
            p = e * (1.0 / jnp.sum(e, 0, keepdims=True))
            r["probs"][k, head] = p
            p_wide = two_windows(p.astype(bf), first_half)
            r["probs_wide"][k, head] = p_wide
            wides.append(p_wide)
        held["p", t] = wides

    def mix(t):
        k, hp = slots[t]
        lanes = slice(128 * k, 128 * k + 128)
        r["mixed"][64 * hp : 64 * hp + 64, lanes] = dot(
            two_heads(r["values"], hp, lanes), jnp.concatenate(held.pop(("p", t)), axis=0)
        ).astype(bf)

    def attend(t):
        def run():
            if t == 0:
                scores(0)
            if t + 1 < len(slots):
                scores(t + 1)
            if t < len(slots):
                soft(t)
            if t >= 1:
                mix(t - 1)

        return run

    def join():
        r["middle"][...] = r["x"][...] + dot(r["w_out_t"][...], r["mixed"][...])

    def norm_two():
        unit_vals, inverse = unit_norm(r["middle"][...])
        r["unit_two"][...] = unit_vals
        r["inverse_two"][...] = jnp.broadcast_to(inverse, (8, SPAN))
        r["entry_two"][:WIDTH] = (unit_vals * vec(GAIN_TWO) + vec(SHIFT_TWO)).astype(bf)

    def gelu(s, part):
        def run():
            lanes = slice(LANES * s, LANES * s + LANES)
            rows = slice(HID // 2 * part, HID // 2 * part + HID // 2)
            hidden = dot(r["w_exp_t"][rows], r["entry_two"][:, lanes])
            twice = 1.0 + lax.erf(hidden * INV_SQRT2)
            r["active"][rows, lanes] = (hidden * twice).astype(bf)
            r["slope"][rows, lanes] = twice + hidden * (
                (2.0 * INV_SQRT2PI) * jnp.exp2(hidden * hidden * (-0.5 * LOG2E))
            )

        return run

    def contracted(s):
        def run():
            lanes = slice(LANES * s, LANES * s + LANES)
            r["result"][:, lanes] = (
                r["middle"][:, lanes]
                + dot(r["w_con_t"][...], r["active"][:, lanes])
                + vec(CON_BIAS, LANES)
            ).astype(bf)

        return run

    tasks = tasks + [(340, fetch), (120, norm_one), (180, project), (80, turn)]
    tasks = tasks + [(80, attend(t)) for t in range(len(slots) + 1)]
    tasks = tasks + [(100, join), (150, norm_two)]
    tasks = tasks + [(270, gelu(s, part)) for s in range(SUBS) for part in range(2)]
    tasks = tasks + [(130, contracted(s)) for s in range(SUBS)]
    tasks = tasks + [(70, put(s)) for s in range(SUBS)]
    return tasks


def backward_tasks(r, first_half, put):
    slots = [(k, hp) for k in range(PAIRS) for hp in range(3)]
    held = {}

    def vec(at):
        return wide(r["vec"][at : at + WIDTH, :], SPAN)

    def hidden_back(s, part):
        def run():
            lanes = slice(LANES * s, LANES * s + LANES)
            rows = slice(HID // 2 * part, HID // 2 * part + HID // 2)
            r["hidden_low"][rows, lanes] = (
                dot(r["w_con"][rows], r["up_low"][:, lanes]) * r["slope"][rows, lanes]
            ).astype(bf)

        return run

    def expand_back(s):
        def run():
            lanes = slice(LANES * s, LANES * s + LANES)
            r["grad_two"][:, lanes] = dot(r["w_exp"][...], r["hidden_low"][:, lanes])

        return run

    def norm_two_back():
        grad = r["up"][...] + unit_back(
            r["grad_two"][...], r["unit_two"][...], r["inverse_two"][0:1, :], vec(GAIN_TWO)
        )
        r["middle_grad"][...] = grad
        r["branch_low"][...] = grad.astype(bf)

    def out_back():
        r["mixed_low"][...] = dot(r["w_out"][...], r["branch_low"][...]).astype(bf)

    def expand_sum(part):
        def run():
            rows = slice(HID // 2 * part, HID // 2 * part + HID // 2)
            r["acc_exp"][rows, :] += dot_nt(r["hidden_low"][rows, :], r["entry_two"][...])

        return run

    def contract_sum(part):
        def run():
            rows = slice(HID // 2 * part, HID // 2 * part + HID // 2)
            r["acc_con"][rows, :] += dot_nt(r["active"][rows, :], r["up_low"][...])

        return run

    def prob_back(t):
        k, hp = slots[t]
        held["g", t] = cross(r["values_t"], r["mixed_low"], 128 * k, hp, first_half)

    def score_back(t):
        k, hp = slots[t]
        pieces = held.pop(("g", t))
        wides = []
        for head in (2 * hp, 2 * hp + 1):
            p, g = r["probs"][k, head], pieces[head - 2 * hp]
            s = p * (g - jnp.sum(g * p, 0, keepdims=True))
            r["d_tab"][:, 128 * head : 128 * head + 128] += s
            wides.append(two_windows(s.astype(bf), first_half))
        held["s", t] = wides

    def triple_back(t):
        k, hp = slots[t]
        wides = held.pop(("s", t))
        lanes = slice(128 * k, 128 * k + 128)
        at = 64 * hp
        r["triple_low"][at : at + 64, lanes] = (
            dot(two_heads(r["keys"], hp, lanes), jnp.concatenate(wides, axis=0)) * scale
        ).astype(bf)
        r["triple_low"][WIDTH + at : WIDTH + at + 64, lanes] = (
            dot_nt(two_heads(r["query"], hp, lanes), jnp.concatenate(wides, axis=1)) * scale
        ).astype(bf)
        probs = jnp.concatenate([r["probs_wide"][k, 2 * hp], r["probs_wide"][k, 2 * hp + 1]], axis=1)
        r["triple_low"][2 * WIDTH + at : 2 * WIDTH + at + 64, lanes] = dot_nt(
            two_heads(r["mixed_low"], hp, lanes), probs
        ).astype(bf)

    def attend(t):
        def run():
            if t == 0:
                prob_back(0)
            if t + 1 < len(slots):
                prob_back(t + 1)
            if t < len(slots):
                score_back(t)
            if t >= 1:
                triple_back(t - 1)

        return run

    def entry_back(s):
        def run():
            lanes = slice(LANES * s, LANES * s + LANES)
            r["grad_one"][:, lanes] = dot(r["w_in"][...], r["triple_low"][:, lanes])

        return run

    def in_sum():
        r["acc_in"][: 3 * WIDTH, :] += dot_nt(r["triple_low"][...], r["entry_one"][...])

    def out_sum():
        r["acc_in"][3 * WIDTH :, :] += dot_nt(r["branch_low"][...], r["mixed"][...])

    def norm_one_back():
        r["token_grad"][...] = (
            r["middle_grad"][...]
            + unit_back(
                r["grad_one"][...], r["unit_one"][...], r["inverse_one"][0:1, :], vec(GAIN_ONE)
            )
        ).astype(bf)

    def vector_sum():
        one, two = r["grad_one"][...], r["grad_two"][...]
        for place, term in enumerate(
            (one * r["unit_one"][...], one, two * r["unit_two"][...], two, r["up"][...])
        ):
            r["d_vec"][WIDTH * place : WIDTH * place + WIDTH, :] += fold(term)

    tasks = [(80, hidden_back(s, part)) for s in range(SUBS) for part in range(2)]
    tasks = tasks + [(130, expand_back(s)) for s in range(SUBS)]
    tasks = tasks + [(200, norm_two_back), (100, out_back)]
    sums = [(130, expand_sum(part)) for part in range(2)]
    sums = sums + [(130, contract_sum(part)) for part in range(2)]
    tasks = tasks + weave([(130, attend(t)) for t in range(len(slots) + 1)], sums)
    tasks = tasks + [(110, entry_back(s)) for s in range(SUBS)]
    tasks = tasks + [(200, in_sum), (200, norm_one_back), (70, out_sum), (200, vector_sum)]
    tasks = tasks + [(70, put(s)) for s in range(SUBS)]
    return tasks


def block_kernel(*refs):
    names = (
        ["vox", "cot", "f_in", "f_out", "f_exp", "f_con", "bias", "vectors", "related"]
        + ["take", "give", "pick", "fill", "out_res", "out_tok", "out_total"]
        + list(WEIGHTS)
        + list(ONCE)
        + [name + "_0" for name in BOTH]
        + [name + "_1" for name in BOTH]
        + ["bucket", "landed", "partial_sum", "landed_two", "total"]
        + ["own", "halo_d", "halo_w", "send_w", "back_send", "back_recv", "grid_res", "grid_tok"]
        + ["own_sem", "d_send", "d_recv", "w_send", "w_recv", "b_send", "b_recv"]
        + ["o_sem", "r_send", "r_recv"]
        + ["s1_send", "s1_recv", "s2_send", "s2_recv", "s3_send", "s3_recv", "s4_send", "s4_recv"]
    )
    r = dict(zip(names, refs))
    states = []
    for parity in range(2):
        state = dict(r)
        for name in BOTH:
            state[name] = r[f"{name}_{parity}"]
        states.append(state)
    crops, _, rows, width = r["vox"].shape
    per_crop = rows // (2 * TOK)
    subs = rows // TOK
    steps = crops * per_crop
    half_rows = rows // 2
    depth, peers_d = lax.axis_index("depth"), lax.axis_size("depth")
    column, peers_w = lax.axis_index("wide"), lax.axis_size("wide")
    d_prev = {"depth": lax.rem(depth + peers_d - 1, peers_d)}
    d_next = {"depth": lax.rem(depth + 1, peers_d)}
    w_prev = {"wide": lax.rem(column + peers_w - 1, peers_w)}
    w_next = {"wide": lax.rem(column + 1, peers_w)}
    mesh_id = pl.DeviceIdType.MESH
    sources = (r["vox"], r["cot"])
    results = (r["out_res"], r["out_tok"])
    grids = (r["grid_res"], r["grid_tok"])
    own, halo_d, halo_w = r["own"], r["halo_d"], r["halo_w"]

    def own_copy(c, a):
        slot = lax.rem(c, SLOTS)
        return pltpu.make_async_copy(
            sources[a].at[c, pl.ds(SHIFT, 2)], own.at[slot, a], r["own_sem"].at[slot, a]
        )

    def depth_copy(c, a):
        return pltpu.make_async_remote_copy(
            src_ref=sources[a].at[c, pl.ds(0, SHIFT)],
            dst_ref=halo_d.at[c, a],
            send_sem=r["d_send"].at[c, a],
            recv_sem=r["d_recv"].at[c, a],
            device_id=d_prev,
            device_id_type=mesh_id,
        )

    def wide_copy(c, half):
        return pltpu.make_async_remote_copy(
            src_ref=r["send_w"].at[lax.rem(c, SLOTS), half],
            dst_ref=halo_w.at[c, half],
            send_sem=r["w_send"].at[c, half],
            recv_sem=r["w_recv"].at[c, half],
            device_id=w_prev,
            device_id_type=mesh_id,
        )

    def back_copy(c, half):
        return pltpu.make_async_remote_copy(
            src_ref=r["back_send"].at[lax.rem(c, SLOTS), half],
            dst_ref=r["back_recv"].at[c, half],
            send_sem=r["b_send"].at[c, half],
            recv_sem=r["b_recv"].at[c, half],
            device_id=w_next,
            device_id_type=mesh_id,
        )

    def keep_copy(c, a):
        slot = lax.rem(c, SLOTS)
        return pltpu.make_async_copy(
            grids[a].at[slot, pl.ds(0, 2)],
            results[a].at[c, pl.ds(SHIFT, 2)],
            r["o_sem"].at[slot, a],
        )

    def return_copy(c, a):
        slot = lax.rem(c, SLOTS)
        return pltpu.make_async_remote_copy(
            src_ref=grids[a].at[slot, pl.ds(2, 2)],
            dst_ref=results[a].at[c, pl.ds(0, SHIFT)],
            send_sem=r["r_send"].at[slot, a],
            recv_sem=r["r_recv"].at[c, a],
            device_id=d_next,
            device_id_type=mesh_id,
        )

    crew = lax.axis_size("dp") * peers_d
    place = lax.axis_index("dp") * peers_d + depth

    def mate(step):
        other = lax.rem(place + step, crew)
        return other, {"dp": other // peers_d, "depth": lax.rem(other, peers_d)}

    def across(step):
        other = lax.rem(column + step, peers_w)
        return other, {"wide": other}

    barrier = pltpu.get_barrier_semaphore()
    for step in range(1, crew):
        pl.semaphore_signal(barrier, inc=1, device_id=mate(step)[1], device_id_type=mesh_id)
    for step in range(1, peers_w):
        pl.semaphore_signal(barrier, inc=1, device_id=across(step)[1], device_id_type=mesh_id)
    pl.semaphore_wait(barrier, crew + peers_w - 2)

    for c in range(2):
        for a in range(2):
            own_copy(c, a).start()

    def send_depth(c, carry):
        for a in range(2):
            depth_copy(c, a).start()
        return carry

    lax.fori_loop(0, crops, send_depth, 0)

    for name in ("acc_in", "acc_exp", "acc_con", "d_vec", "d_tab"):
        r[name][...] = jnp.zeros_like(r[name])
    for parity in range(2):
        for name in ("entry_one", "entry_two", "mixed"):
            states[parity][name][WIDTH:, :] = jnp.ones((16, SPAN), bf)
    r["back_recv"][crops] = jnp.zeros(r["back_recv"].shape[1:], bf)
    for name in ("w_in_t", "w_out_t", "w_exp_t"):
        shape = r[name].shape
        r[name][:, WIDTH:] = jnp.zeros((shape[0], 16), bf)
    r["w_in"][...] = r["f_in"][...].astype(bf)
    r["w_in_t"][:, :WIDTH] = r["f_in"][...].T.astype(bf)
    r["w_out"][...] = r["f_out"][...].astype(bf)
    r["w_out_t"][:, :WIDTH] = r["f_out"][...].T.astype(bf)
    r["w_exp"][...] = (r["f_exp"][...].astype(bf).astype(fl) * 0.5).astype(bf)
    r["w_exp_t"][:, :WIDTH] = r["f_exp"][...].T.astype(bf)
    r["w_con_t"][...] = (r["f_con"][...].astype(bf).astype(fl) * 0.5).astype(bf)
    r["w_con"][...] = r["f_con"][...].T.astype(bf)
    lane16 = lax.broadcasted_iota(jnp.int32, (64, 16), 1)
    for tile in range(r["vectors"].shape[0]):
        spread = jnp.broadcast_to(r["vectors"][tile : tile + 1, :], (128, 128)).T
        for part in range(2):
            chunk = spread[64 * part : 64 * part + 64]
            member, at = divmod(128 * tile + 64 * part, WIDTH)
            narrow = chunk[:, :16]
            high = narrow.astype(bf).astype(fl)
            middle = (narrow - high).astype(bf).astype(fl)
            column_parts = jnp.where(
                lane16 == 0,
                high,
                jnp.where(
                    lane16 == 1, middle, jnp.where(lane16 == 2, narrow - high - middle, 0.0)
                ),
            ).astype(bf)
            if member in (0, 1, 5, 6, 7):
                base = {0: GAIN_ONE, 1: SHIFT_ONE, 5: GAIN_TWO, 6: SHIFT_TWO, 7: CON_BIAS}[member]
                r["vec"][base + at : base + at + 64, :] = chunk
            elif member == 2:
                r["w_in_t"][at : at + 64, WIDTH:] = column_parts
            elif member == 3:
                r["w_in_t"][2 * WIDTH + at : 2 * WIDTH + at + 64, WIDTH:] = column_parts
            elif member == 4:
                r["w_out_t"][at : at + 64, WIDTH:] = column_parts
            else:
                base = WIDTH * (member - 8)
                r["w_exp_t"][base + at : base + at + 64, WIDTH:] = column_parts

    related = r["related"]

    def chooser(places):
        return (
            lax.broadcasted_iota(jnp.int32, (384, 128), 0)
            == jnp.broadcast_to(places, (384, 128))
        ).astype(bf)

    def eight(block):
        return pl.ds(pl.multiple_of(8 * block, 8), 8)

    def thirds(v):
        high = v.astype(bf)
        rest = v - high.astype(fl)
        middle = rest.astype(bf)
        return jnp.concatenate([high, middle, (rest - middle.astype(fl)).astype(bf)], axis=0)

    def ends(v):
        return v[:8] + v[8:16] + v[16:24]

    def code(at, window, edge):
        last_d = (depth == peers_d - 1).astype(jnp.int32)
        last_w = (column == peers_w - 1).astype(jnp.int32)
        d, h, w = at // 16, lax.rem(at // 4, 4), lax.rem(at, 4)
        return (
            last_d * (d >= SHIFT).astype(jnp.int32) * 4
            + edge * (h >= SHIFT).astype(jnp.int32) * 2
            + last_w * window * (w >= SHIFT).astype(jnp.int32)
        )

    bias_parts = thirds(r["bias"][...])

    def table_rows(block, carry):
        near = related[eight(block), :]
        found = [ends(dot(bias_parts, chooser(near[k : k + 1]))) for k in range(8)]
        lane = lax.broadcasted_iota(jnp.int32, (8, 128), 1)
        j = lax.broadcasted_iota(jnp.int32, (8, 128), 0) + 8 * block
        window, i = lane // TOK, lax.rem(lane, TOK)
        for edge in range(2):
            differ = code(i, window, edge) != code(j, window, edge)
            mask = jnp.where(differ, mask_fill, 0.0)
            for head in range(HEADS):
                values = jnp.concatenate([row[head : head + 1, :] for row in found], axis=0)
                r["table"][edge, eight(block), 128 * head : 128 * head + 128] = (
                    values + mask
                ) * LOG2E
        return carry

    lax.fori_loop(0, TOK // 8, table_rows, 0)
    first_half = lax.broadcasted_iota(jnp.int32, (TOK, 128), 1) < TOK

    def starts(b):
        first = pl.multiple_of(b * TOK + 16, 16)
        second = pl.multiple_of(lax.rem(b * TOK + TOK, rows), 16)
        return first, second

    def natural(c, a, b):
        first, second = starts(b)
        slot = lax.rem(c, SLOTS)
        parts = []
        for d in range(2):
            parts.append(own[slot, a, d, pl.ds(first, 48), :])
            parts.append(own[slot, a, d, pl.ds(second, 16), :])
        for d in range(2):
            parts.append(halo_d[c, a, d, pl.ds(first, 48), :])
            parts.append(halo_d[c, a, d, pl.ds(second, 16), :])
        return jnp.concatenate(parts, axis=0)

    def edge_rows(b):
        half = b // (subs // 2)
        return half, pl.ds(pl.multiple_of(lax.rem(b, subs // 2) * TOK, TOK), TOK)

    def pack(c, b):
        half, there = edge_rows(b)
        source = jnp.minimum(c, crops - 1)
        r["send_w"][lax.rem(c, SLOTS), half, there, :] = jnp.concatenate(
            [dot(r["pick"][...], natural(source, a, b)) for a in range(2)], axis=1
        ).astype(bf)

    def merge(c, b):
        first, second = starts(b)
        half, there = edge_rows(b)
        slot = lax.rem(c + SLOTS, SLOTS)
        arrived = r["back_recv"][lax.rem(c + crops + 1, crops + 1), half, there, :]
        for a in range(2):
            extra = dot(r["fill"][...], arrived[:, WIDTH * a : WIDTH * a + WIDTH]).astype(bf)
            for d in range(WIN):
                for start, size, at in ((first, 48, 64 * d), (second, 16, 64 * d + 48)):
                    place_rows = pl.ds(start, size)
                    grids[a][slot, d, place_rows, :] = (
                        grids[a][slot, d, place_rows, :] + extra[at : at + size]
                    )

    def put_grid(a, c, b, low):
        first, second = starts(b)
        slot = lax.rem(c, SLOTS)
        placed = low.T
        for d in range(WIN):
            grids[a][slot, d, pl.ds(first, 48), :] = placed[64 * d : 64 * d + 48]
            grids[a][slot, d, pl.ds(second, 16), :] = placed[64 * d + 48 : 64 * d + 64]

    def forward_of(g, state):
        c, u = g // per_crop, lax.rem(g, per_crop)

        def tokens_of(s):
            b = 2 * u + s
            half, there = edge_rows(b)
            edges = halo_w[c, half, there, :].T
            return [
                jnp.concatenate(
                    [natural(c, a, b).T, edges[WIDTH * a : WIDTH * a + WIDTH]], axis=1
                )
                for a in range(2)
            ]

        def put(s):
            def run():
                moved = dot(
                    state["result"][:, LANES * s : LANES * s + LANES], state["give"][...]
                ).astype(bf)
                state["edge_res"][s] = moved[:, LANES:]
                put_grid(0, c, 2 * u + s, moved[:, :LANES])

            return run

        def ready(s):
            return lambda: pack(c + 1, 2 * u + s)

        edge = (u == per_crop - 1).astype(jnp.int32)
        tasks = forward_tasks(state, first_half, tokens_of, edge, put)
        return weave(tasks, [(80, ready(s)) for s in range(SUBS)])

    def backward_of(g, state):
        c, u = g // per_crop, lax.rem(g, per_crop)

        def put(s):
            def run():
                b = 2 * u + s
                moved = dot(
                    state["token_grad"][:, LANES * s : LANES * s + LANES], state["give"][...]
                ).astype(bf)
                put_grid(1, c, b, moved[:, :LANES])
                half, there = edge_rows(b)
                r["back_send"][lax.rem(c, SLOTS), half, there, :] = jnp.concatenate(
                    [state["edge_res"][s], moved[:, LANES:]], axis=0
                ).T

            return run

        def mended(s):
            return lambda: merge(c - 1, 2 * u + s)

        tasks = backward_tasks(state, first_half, put)
        return weave(tasks, [(120, mended(s)) for s in range(SUBS)])

    def before(f, b):
        if f is not None:
            c, u = f // per_crop, lax.rem(f, per_crop)

            @pl.when(u == 0)
            def _():
                wide_copy(c, 0).wait_recv()

                @pl.when(c + 2 < crops)
                def _():
                    for a in range(2):
                        own_copy(c + 2, a).start()

                @pl.when(c + 1 < crops)
                def _():
                    for a in range(2):
                        own_copy(c + 1, a).wait()
                        depth_copy(c + 1, a).wait_recv()

                @pl.when(c >= SLOTS - 1)
                def _():
                    for half in range(2):
                        wide_copy(c + 1 - SLOTS, half).wait_send()

                @pl.when(c >= SLOTS)
                def _():
                    for a in range(2):
                        keep_copy(c - SLOTS, a).wait()
                        return_copy(c - SLOTS, a).wait_send()

            @pl.when(u == per_crop // 2)
            def _():
                wide_copy(c, 1).wait_recv()

        if b is not None:
            c_b, u_b = b // per_crop, lax.rem(b, per_crop)

            @pl.when((u_b == 0) & (c_b >= SLOTS))
            def _():
                for half in range(2):
                    back_copy(c_b - SLOTS, half).wait_send()

            @pl.when((u_b == 0) & (c_b >= 1))
            def _():
                back_copy(c_b - 1, 0).wait_recv()

            @pl.when((u_b == per_crop // 2) & (c_b >= 1))
            def _():
                back_copy(c_b - 1, 1).wait_recv()

    def after(f, b):
        if f is not None:
            c, u = f // per_crop, lax.rem(f, per_crop)

            @pl.when((u == per_crop // 2 - 1) & (c + 1 < crops))
            def _():
                wide_copy(c + 1, 0).start()

            @pl.when((u == per_crop - 1) & (c + 1 < crops))
            def _():
                wide_copy(c + 1, 1).start()

        if b is not None:
            c_b, u_b = b // per_crop, lax.rem(b, per_crop)

            @pl.when(u_b == per_crop // 2 - 1)
            def _():
                back_copy(c_b, 0).start()

            @pl.when(u_b == per_crop - 1)
            def _():
                back_copy(c_b, 1).start()

                @pl.when(c_b >= 1)
                def _():
                    for a in range(2):
                        keep_copy(c_b - 1, a).start()
                        return_copy(c_b - 1, a).start()

    def half_step(f, b, forward_state, backward_state):
        before(f, b)
        ahead = [] if f is None else forward_of(f, forward_state)
        behind = [] if b is None else backward_of(b, backward_state)
        for _, task in weave(behind, ahead):
            task()
        after(f, b)

    for a in range(2):
        own_copy(0, a).wait()
        depth_copy(0, a).wait_recv()
    for half in range(2):

        def first_pack(b, carry):
            pack(0, b)
            return carry

        lax.fori_loop(half * (subs // 2), (half + 1) * (subs // 2), first_pack, 0)
        wide_copy(0, half).start()
    half_step(jnp.int32(0), None, states[0], None)

    def two_steps(i, carry):
        half_step(2 * i + 1, 2 * i, states[1], states[0])
        half_step(2 * i + 2, 2 * i + 1, states[0], states[1])
        return carry

    lax.fori_loop(0, steps // 2 - 1, two_steps, 0)
    half_step(jnp.int32(steps - 1), jnp.int32(steps - 2), states[1], states[0])
    half_step(None, jnp.int32(steps - 1), None, states[1])

    bucket, landed, total, d_row = r["bucket"], r["landed"], r["total"], r["d_row"]
    partial_sum, landed_two = r["partial_sum"], r["landed_two"]
    extra = 18 * width
    for tile in range(12):
        acc, at = ((r["acc_in"], 128 * tile), (r["acc_exp"], 128 * (tile - 6)))[tile // 6]
        turned = acc[at : at + 128, :].T * (1.0, 0.5)[tile // 6]
        bucket[width * tile : width * tile + width, :] = turned[:width].astype(bf)
        d_row[tile : tile + 1, :] = turned[width : width + 1]
    for tile in range(6):
        bucket[width * (12 + tile) : width * (13 + tile), :] = (
            r["acc_con"][128 * tile : 128 * tile + 128, :].T * 0.5
        ).astype(bf)
    for tile in range(8):
        size = min(128, 5 * width - 128 * tile)
        d_row[12 + tile : 13 + tile, :size] = jnp.sum(
            r["d_vec"][128 * tile : 128 * tile + size, :].T, 0, keepdims=True
        )
    d_row[19:20, 64:] = jnp.zeros((1, 64), fl)

    def table_sums(block, carry):
        near = related[eight(block), :]
        held = r["d_tab"][eight(block), :]
        for k in range(8):
            rows_k = jnp.concatenate(
                [held[k : k + 1, 128 * head : 128 * head + 128] for head in range(HEADS)]
                + [jnp.zeros((2, 128), fl)],
                axis=0,
            )
            carry = carry + dot_nt(thirds(rows_k), chooser(near[k : k + 1]))
        return carry

    sums = ends(lax.fori_loop(0, TOK // 8, table_sums, jnp.zeros((24, 384), fl)))
    for tile in range(3):
        d_row[24 + 8 * tile : 32 + 8 * tile, :] = sums[:, 128 * tile : 128 * tile + 128]
    d_row[20:24, :] = jnp.zeros((4, 128), fl)
    bucket[extra : extra + 48, :] = d_row[...].astype(bf)
    length = bucket.shape[0]
    if length > extra + 48:
        bucket[extra + 48 :, :] = jnp.zeros((length - extra - 48, 128), bf)

    share = length // crew
    piece = share // peers_w

    def span(start, size):
        return pl.ds(pl.multiple_of(start, 16), size)

    def first_copy(step):
        other, peer = mate(step)
        return pltpu.make_async_remote_copy(
            src_ref=bucket.at[span(other * share, share)],
            dst_ref=landed.at[step - 1],
            send_sem=r["s1_send"].at[step - 1],
            recv_sem=r["s1_recv"].at[step - 1],
            device_id=peer,
            device_id_type=mesh_id,
        )

    def second_copy(step):
        other, peer = across(step)
        return pltpu.make_async_remote_copy(
            src_ref=partial_sum.at[span(other * piece, piece)],
            dst_ref=landed_two.at[step - 1],
            send_sem=r["s2_send"].at[step - 1],
            recv_sem=r["s2_recv"].at[step - 1],
            device_id=peer,
            device_id_type=mesh_id,
        )

    def third_copy(step):
        rows_mine = total.at[span(place * share + column * piece, piece)]
        return pltpu.make_async_remote_copy(
            src_ref=rows_mine,
            dst_ref=rows_mine,
            send_sem=r["s3_send"].at[step - 1],
            recv_sem=r["s3_recv"].at[step - 1],
            device_id=across(step)[1],
            device_id_type=mesh_id,
        )

    def fourth_copy(step):
        rows_mine = total.at[span(place * share, share)]
        return pltpu.make_async_remote_copy(
            src_ref=rows_mine,
            dst_ref=rows_mine,
            send_sem=r["s4_send"].at[step - 1],
            recv_sem=r["s4_recv"].at[step - 1],
            device_id=mate(step)[1],
            device_id_type=mesh_id,
        )

    def third_arrival(step):
        other = lax.rem(column + peers_w - step, peers_w)
        rows_there = total.at[span(place * share + other * piece, piece)]
        return pltpu.make_async_remote_copy(
            src_ref=rows_there,
            dst_ref=rows_there,
            send_sem=r["s3_send"].at[step - 1],
            recv_sem=r["s3_recv"].at[step - 1],
            device_id=across(step)[1],
            device_id_type=mesh_id,
        )

    def fourth_arrival(step):
        other = lax.rem(place + crew - step, crew)
        rows_there = total.at[span(other * share, share)]
        return pltpu.make_async_remote_copy(
            src_ref=rows_there,
            dst_ref=rows_there,
            send_sem=r["s4_send"].at[step - 1],
            recv_sem=r["s4_recv"].at[step - 1],
            device_id=mate(step)[1],
            device_id_type=mesh_id,
        )

    for step in range(1, crew):
        first_copy(step).start()
    for half in range(2):
        back_copy(crops - 1, half).wait_recv()

        def last_merge(b, carry):
            merge(jnp.int32(crops - 1), b)
            return carry

        lax.fori_loop(half * (subs // 2), (half + 1) * (subs // 2), last_merge, 0)
    for a in range(2):
        keep_copy(crops - 1, a).start()
        return_copy(crops - 1, a).start()
    for step in range(1, crew):
        first_copy(step).wait_recv()
    summed = bucket[span(place * share, share), :].astype(fl)
    for step in range(1, crew):
        summed = summed + landed[step - 1].astype(fl)
    partial_sum[...] = summed.astype(bf)
    for step in range(1, peers_w):
        second_copy(step).start()
    for step in range(1, peers_w):
        second_copy(step).wait_recv()
    summed = partial_sum[span(column * piece, piece), :].astype(fl)
    for step in range(1, peers_w):
        summed = summed + landed_two[step - 1].astype(fl)
    total[span(place * share + column * piece, piece), :] = summed.astype(bf)
    for step in range(1, peers_w):
        third_copy(step).start()
    for step in range(1, peers_w):
        third_arrival(step).wait_recv()
    for step in range(1, crew):
        fourth_copy(step).start()
    for step in range(1, crew):
        fourth_arrival(step).wait_recv()
    r["out_total"][...] = total[...]
    for step in range(1, crew):
        first_copy(step).wait_send()
        fourth_copy(step).wait_send()
    for step in range(1, peers_w):
        second_copy(step).wait_send()
        third_copy(step).wait_send()

    def finish(c, carry):
        for a in range(2):
            depth_copy(c, a).wait_send()
            return_copy(c, a).wait_recv()
        return carry

    lax.fori_loop(0, crops, finish, 0)

    def close(c, carry):
        for a in range(2):
            keep_copy(c, a).wait()
            return_copy(c, a).wait_send()
        for half in range(2):
            back_copy(c, half).wait_send()
        return carry

    lax.fori_loop(crops - SLOTS, crops, close, 0)

    def close_wide(c, carry):
        for half in range(2):
            wide_copy(c, half).wait_send()
        return carry

    lax.fori_loop(crops + 1 - SLOTS, crops, close_wide, 0)


def block_call(voxels, cotangent, matrices, bias_table, vectors):
    crops, planes, rows, width = voxels.shape
    whole = pl.BlockSpec(memory_space=pltpu.VMEM)
    far = pl.BlockSpec(memory_space=pl.ANY)
    related = relative_index().T
    related = jnp.asarray(np.concatenate([related, related], axis=1), jnp.int32)
    consts = list(matrices) + [bias_table, vectors, related] + placement()
    sem = pltpu.SemaphoreType.DMA
    crew = lax.axis_size("dp") * lax.axis_size("depth")
    peers_w = lax.axis_size("wide")
    unit_rows = 16 * crew * peers_w
    length = -(-(18 * width + 48) // unit_rows) * unit_rows
    share = length // crew
    piece = share // peers_w
    return pl.pallas_call(
        block_kernel,
        in_specs=[far, far] + [whole] * len(consts),
        out_specs=[far, far, whole],
        out_shape=[
            jax.ShapeDtypeStruct(voxels.shape, bf),
            jax.ShapeDtypeStruct(voxels.shape, bf),
            jax.ShapeDtypeStruct((length, 128), bf),
        ],
        scratch_shapes=[
            pltpu.VMEM(*spec)
            for spec in list(WEIGHTS.values()) + list(ONCE.values()) + list(BOTH.values()) * 2
        ]
        + [
            pltpu.VMEM((length, 128), bf),
            pltpu.VMEM((crew - 1, share, 128), bf),
            pltpu.VMEM((share, 128), bf),
            pltpu.VMEM((peers_w - 1, piece, 128), bf),
            pltpu.VMEM((length, 128), bf),
            pltpu.VMEM((SLOTS, 2, 2, rows, width), bf),
            pltpu.VMEM((crops, 2, 2, rows, width), bf),
            pltpu.VMEM((crops, 2, rows // 2, 2 * width), bf),
            pltpu.VMEM((SLOTS, 2, rows // 2, 2 * width), bf),
            pltpu.VMEM((SLOTS, 2, rows // 2, 2 * width), bf),
            pltpu.VMEM((crops + 1, 2, rows // 2, 2 * width), bf),
            pltpu.VMEM((SLOTS, 4, rows, width), bf),
            pltpu.VMEM((SLOTS, 4, rows, width), bf),
            sem((SLOTS, 2)),
            sem((crops, 2)),
            sem((crops, 2)),
            sem((crops, 2)),
            sem((crops, 2)),
            sem((crops, 2)),
            sem((crops, 2)),
            sem((SLOTS, 2)),
            sem((SLOTS, 2)),
            sem((crops, 2)),
            sem((crew - 1,)),
            sem((crew - 1,)),
            sem((peers_w - 1,)),
            sem((peers_w - 1,)),
            sem((peers_w - 1,)),
            sem((peers_w - 1,)),
            sem((crew - 1,)),
            sem((crew - 1,)),
        ],
        compiler_params=pltpu.CompilerParams(
            vmem_limit_bytes=60 * 2**20, collective_id=0, has_side_effects=True
        ),
        name="block",
    )(voxels, cotangent, *consts)


def update_kernel(*refs):
    far_in, total, params, far_out, outs, norm_ref, held, in_sem, out_sem = (
        refs[0:2], refs[2], refs[3:21], refs[21:23], refs[23:51], refs[51], refs[52],
        refs[53], refs[54],
    )
    crops = far_in[0].shape[0]

    def fetch(a, c):
        return pltpu.make_async_copy(far_in[a].at[c], held.at[a, c], in_sem.at[a, c])

    def store(a, c):
        return pltpu.make_async_copy(held.at[a, c], far_out[a].at[c], out_sem.at[a, c])

    for a in range(2):
        for c in range(crops):
            fetch(a, c).start()
    for a in range(2):
        for c in range(crops):
            fetch(a, c).wait()
            store(a, c).start()
    width = 192

    def slab(tile):
        return total[width * tile : width * tile + width, :].astype(fl)

    small = total[18 * width : 18 * width + 48, :].astype(fl)
    low_half = slab(4)
    grads = [
        jnp.concatenate([slab(k) for k in range(4)] + [low_half[:, :64]], axis=1),
        jnp.concatenate([low_half[:, 64:], slab(5)], axis=1),
        jnp.concatenate([slab(k) for k in range(6, 12)], axis=1),
        jnp.concatenate([slab(k) for k in range(12, 18)], axis=1),
    ]
    flat_bias = jnp.concatenate([small[k : k + 1] for k in range(12)], axis=1)
    flat_sum = jnp.concatenate([small[k : k + 1] for k in range(12, 20)], axis=1)

    def cut(flat, index):
        return flat[:, width * index : width * index + width]

    table = jnp.concatenate([small[24:32], small[32:40], small[40:48]], axis=1)
    grads.append(table[:HEADS, : params[4].shape[1]])
    grads.append(
        jnp.concatenate(
            [
                cut(flat_sum, 0), cut(flat_sum, 1), cut(flat_bias, 0), cut(flat_bias, 2),
                cut(flat_bias, 3), cut(flat_sum, 2), cut(flat_sum, 3), cut(flat_sum, 4),
                flat_bias[:, 4 * width : 8 * width],
            ],
            axis=1,
        )
    )
    squares = jnp.zeros((1, 1), fl)
    for grad in grads:
        squares = squares + jnp.sum(
            jnp.sum(grad * grad, 0, keepdims=True), 1, keepdims=True
        )
    norm_value = jnp.sqrt(squares)
    norm_ref[...] = norm_value
    factor = jnp.minimum(1.0, clip_bound / (norm_value + 1e-06))
    for member in range(6):
        matrix = member < 4
        clipped = grads[member] * factor
        first, second, fresh = adam_update(
            params[member][...],
            params[6 + member][...],
            params[12 + member][...],
            clipped,
            rate_matrix if matrix else rate_vector,
            weight_decay if matrix else 0.0,
        )
        for place, value in enumerate((clipped, first, second, fresh)):
            outs[4 * member + place][...] = value
        if matrix:
            outs[24 + member][...] = fresh.astype(bf)
    for a in range(2):
        for c in range(crops):
            store(a, c).wait()


def update_call(result, token_grad, total, params):
    whole = pl.BlockSpec(memory_space=pltpu.VMEM)
    far = pl.BlockSpec(memory_space=pl.ANY)
    shapes = []
    for member in range(6):
        shapes = shapes + [jax.ShapeDtypeStruct(params[member].shape, fl)] * 4
    for member in range(4):
        shapes.append(jax.ShapeDtypeStruct(params[member].shape, bf))
    shapes.append(jax.ShapeDtypeStruct((1, 1), fl))
    big = jax.ShapeDtypeStruct(result.shape, bf)
    return pl.pallas_call(
        update_kernel,
        in_specs=[far, far, whole] + [whole] * 18,
        out_specs=[far, far] + [whole] * 29,
        out_shape=[big, big] + shapes,
        scratch_shapes=[
            pltpu.VMEM((2,) + result.shape, bf),
            pltpu.SemaphoreType.DMA((2, result.shape[0])),
            pltpu.SemaphoreType.DMA((2, result.shape[0])),
        ],
        compiler_params=pltpu.CompilerParams(vmem_limit_bytes=56 * 2**20),
        name="update",
    )(result, token_grad, total, *params)


def local(
    voxels,
    cotangent,
    project_in,
    project_out,
    expand,
    contract,
    bias_table,
    vectors,
    project_in_first,
    project_out_first,
    expand_first,
    contract_first,
    bias_table_first,
    vectors_first,
    project_in_second,
    project_out_second,
    expand_second,
    contract_second,
    bias_table_second,
    vectors_second,
):
    batches, planes, height, breadth, width = voxels.shape
    flat = (batches, planes, height * breadth, width)
    result, token_grad, total = block_call(
        voxels.reshape(flat),
        cotangent.reshape(flat),
        (project_in, project_out, expand, contract.T),
        jnp.pad(bias_table, ((0, 2), (0, 384 - bias_table.shape[1]))),
        vectors.reshape(-1, 128),
    )
    params = [
        project_in,
        project_out,
        expand,
        contract.T,
        bias_table,
        vectors.reshape(1, -1),
        project_in_first,
        project_out_first,
        expand_first,
        contract_first.T,
        bias_table_first,
        vectors_first.reshape(1, -1),
        project_in_second,
        project_out_second,
        expand_second,
        contract_second.T,
        bias_table_second,
        vectors_second.reshape(1, -1),
    ]
    done = update_call(result, token_grad, total, params)
    outs = list(done[2:30])
    for place in range(20, 24):
        outs[place] = outs[place].reshape(-1)
    for place in (12, 13, 14, 15, 27):
        outs[place] = outs[place].T
    return (
        (done[0].reshape(voxels.shape), done[1].reshape(voxels.shape))
        + tuple(outs)
        + (done[30].reshape(()),)
    )


def solution(mesh):
    split = P("dp", "depth", None, "wide", None)
    return jax.shard_map(
        local,
        mesh=mesh,
        in_specs=(split,) * 2 + (P(),) * 18,
        out_specs=(split,) * 2 + (P(),) * 29,
        check_vma=False,
    )
```

time: 478 us -> 275 us (0.58)
  Pallas kernels: 466 us -> 263 us
    pallas_call x1, Pallas kernels: 445 us -> 242 us  [block_call(): pl.pallas_call(block_kernel, in_specs=[far, far] + [whole] * len(consts),...]
where the time goes in v3:
time: 275 us; the launch traced here: 274 us
  Pallas kernels  263 us (96%)
  other arithmetic  5.3 us (2%)
  local copies, waits for them, and re-layouts  5.24 us (2%)
    pallas_call x1, Pallas kernels, block_call(): pl.pallas_call(block_kernel, in_specs=[far, far] + [whole] * len(consts),...  242 us
    pallas_call x1, Pallas kernels, update_call(): pl.pallas_call(update_kernel, in_specs=[far, far, whole] + [whole] * 18,...  20.9 us

profile of v3, /device:TPU:1, one launch (start us, length us, event | category | flops | bytes accessed | tf_op | source)
XLA Modules:
  0.0 273.8 jit_solution(4075541387327992982)
XLA Ops:
  0.7 1.3 reshape.105.refs_14_
  2.0 1.3 reshape.106.refs_20_
  3.3 1.3 reshape.104.refs_8_
  4.6 1.3 pad.4.refs_6_
  5.9 241.6 %block.1 = (bf16[8,4,512,192]{3,2,1,0:T(8,128)(2,1)}, bf16[8,4,512,192]{3,2,1,0:T(8,128)(2,1)}, bf16[3584,128]{1,0:T(8,128)(2,1)}) custom-call(bf16[8,4,512,192]{3,2,1,0:T(8,128)(2,1)} %bitcast.14, bf16[8,4,512,192]{3,2,1,0:T(8,128)(2,1)} %bitcast.15, f32[192,576]{1,0:T(8,128)} %refs_3_.3, f32[192,192]{1,0:T(8,128)} %refs_4_.3, f32[192,768]{1,0:T(8,128)} %refs_5_.1, ...), custom_call_target="tpu_custom_call" | custom-call | tf_op jit(solution)/shard_map/block/pallas_call | solution.py:1109
  247.6 20.9 %update.1 = (bf16[8,4,512,192]{3,2,1,0:T(8,128)(2,1)}, bf16[8,4,512,192]{3,2,1,0:T(8,128)(2,1)}, f32[192,576]{1,0:T(8,128)}, f32[192,576]{1,0:T(8,128)}, f32[192...) custom-call(bf16[8,4,512,192]{3,2,1,0:T(8,128)(2,1)} %get-tuple-elem, ...), custom_call_target="tpu_custom_call" | custom-call | tf_op jit(solution)/shard_map/update/pallas_call | solution.py:1251
  268.5 1.3 reduce
  269.8 1.3 reduce.1
  271.1 1.3 reduce.2
  272.5 1.3 reduce.3

commit v4 on v3

v4 whole, which is shorter than its diff:
```python
from types import SimpleNamespace

import jax
import jax.numpy as jnp
import numpy as np
from jax import lax
from jax.experimental import pallas as pl
from jax.experimental.pallas import tpu as pltpu
from jax.sharding import PartitionSpec as P

HEADS = 6
WIN = 4
SHIFT = 2
STEP = 10
TOK = WIN**3
GROUP = 4
LANES = GROUP * TOK

norm_eps = 1e-05
mask_fill = -100.0
clip_bound = 1000.0
rate_matrix = 0.1
rate_vector = 0.6
weight_decay = 0.01
beta_first = 0.9
beta_second = 0.999
adam_eps = 1e-08
LOG2E = 1.4426950408889634
INV_SQRT2 = 0.7071067811865476
INV_SQRT2PI = 0.3989422804014327


def relative_index():
    extent = 2 * WIN - 1
    corner = np.arange(WIN)
    places = np.stack(np.meshgrid(corner, corner, corner, indexing="ij"), -1).reshape(-1, 3)
    offsets = places[:, None, :] - places[None, :, :] + WIN - 1
    return (offsets[..., 0] * extent + offsets[..., 1]) * extent + offsets[..., 2]


def adam_update(weight, first, second, gradient, rate, decay):
    first_new = beta_first * first + (1.0 - beta_first) * gradient
    second_new = beta_second * second + (1.0 - beta_second) * gradient * gradient
    first_hat = first_new / (1.0 - beta_first**STEP)
    second_hat = second_new / (1.0 - beta_second**STEP)
    weight_new = weight - rate * (first_hat / (jnp.sqrt(second_hat) + adam_eps) + decay * weight)
    return (first_new, second_new, weight_new)


fl = jnp.float32
bf = jnp.bfloat16


def dot(a, b):
    return jnp.dot(a, b, preferred_element_type=fl)


def dot_nt(a, b):
    return lax.dot_general(a, b, (((1,), (1,)), ((), ())), preferred_element_type=fl)


def wide(v, lanes):
    return jnp.concatenate([v] * (lanes // v.shape[1]), axis=1)


def unit_norm(v):
    width = v.shape[0]
    mean = jnp.sum(v, 0, keepdims=True) * (1.0 / width)
    centred = v - mean
    inverse = lax.rsqrt(jnp.sum(centred * centred, 0, keepdims=True) * (1.0 / width) + norm_eps)
    return centred * inverse, inverse


def unit_back(grad, unit, inverse, gain):
    width = grad.shape[0]
    scaled = grad * gain
    inner = jnp.sum(scaled, 0, keepdims=True) * (1.0 / width)
    along = jnp.sum(scaled * unit, 0, keepdims=True) * (1.0 / width)
    return inverse * (scaled - inner - unit * along)


def fold(v):
    total = v[:, :128]
    for lane in range(128, v.shape[1], 128):
        total = total + v[:, lane : lane + 128]
    return total


def two_windows(compact, first_half):
    zero = jnp.zeros_like(compact)
    return jnp.concatenate(
        [jnp.where(first_half, compact, zero), jnp.where(first_half, zero, compact)], axis=0
    )


def two_heads(ref, head_pair, lanes):
    at = 64 * head_pair
    zero = jnp.zeros((32, 128), bf)
    return jnp.concatenate(
        [
            jnp.concatenate([ref[at : at + 32, lanes], zero], axis=1),
            jnp.concatenate([zero, ref[at + 32 : at + 64, lanes]], axis=1),
        ],
        axis=0,
    )


def cross(token_major, low, first, head_pair, first_half):
    right = two_heads(low, head_pair, slice(first, first + 128))
    if head_pair == 1:
        right = jnp.concatenate([jnp.zeros((64, 256), bf), right], axis=0)
        left = token_major[first : first + 128, 0:128]
    else:
        at = 64 * head_pair
        left = token_major[first : first + 128, at : at + 64]
    full = dot(left, right)
    out = []
    for head in range(2):
        block = full[:, 128 * head : 128 * head + 128]
        out.append(jnp.where(first_half, block[:TOK], block[TOK:]))
    return out


def weave(one, other):
    whole_one = sum(weight for weight, _ in one) + 1e-9
    whole_other = sum(weight for weight, _ in other) + 1e-9
    merged, done_one, done_other = [], 0.0, 0.0
    one, other = list(one), list(other)
    while one or other:
        if not other or (
            one
            and (done_one + one[0][0] / 2) / whole_one
            <= (done_other + other[0][0] / 2) / whole_other
        ):
            merged.append(one.pop(0))
            done_one += merged[-1][0]
        else:
            merged.append(other.pop(0))
            done_other += merged[-1][0]
    return merged


def placement():
    take = np.zeros((LANES + TOK, LANES), np.float32)
    pick = np.zeros((TOK, LANES), np.float32)
    for hw in range(2):
        for ww in range(2):
            for d in range(WIN):
                for hh in range(WIN):
                    for wl in range(WIN):
                        t = ((hw * 2 + ww) * WIN + d) * 16 + hh * 4 + wl
                        h, w = 4 * hw + hh, 4 * ww + wl
                        if w < 2 * WIN - SHIFT:
                            row = d * 64 + h * 8 + w + SHIFT
                        else:
                            row = LANES + d * 16 + h * 2 + w - (2 * WIN - SHIFT)
                        take[row, t] = 1.0
    for d in range(WIN):
        for h in range(2 * WIN):
            for w in range(SHIFT):
                pick[d * 16 + h * 2 + w, d * 64 + h * 8 + w] = 1.0
    pick = pick[:32, :128]
    return [jnp.asarray(m, bf) for m in (take, take.T, pick, pick.T)]


WIDTH = 192
HID = 4 * WIDTH
SPAN = 2 * LANES
PAIRS = SPAN // 128
SUBS = SPAN // LANES
SLOTS = 3
DEPTH_SLOTS = 5
RETURN_SLOTS = 3
MERGE_LAG = 5
UNPACK_LAG = 9
BOTH = dict(
    up=((WIDTH, SPAN), fl),
    up_low=((WIDTH, SPAN), bf),
    unit_one=((WIDTH, SPAN), fl),
    inverse_one=((8, SPAN), fl),
    entry_one=((WIDTH + 16, SPAN), bf),
    query=((WIDTH, SPAN), bf),
    keys=((WIDTH, SPAN), bf),
    values=((WIDTH, SPAN), bf),
    values_t=((SPAN, WIDTH), bf),
    probs=((PAIRS, HEADS, TOK, 128), fl),
    probs_low=((PAIRS, HEADS, TOK, 128), bf),
    mixed=((WIDTH + 16, SPAN), bf),
    unit_two=((WIDTH, SPAN), fl),
    inverse_two=((8, SPAN), fl),
    entry_two=((WIDTH + 16, SPAN), bf),
    slope=((HID, SPAN), fl),
    active=((HID, SPAN), bf),
    edge_res=((SUBS, WIDTH, 3 * TOK), bf),
)
ONCE = dict(
    x=((WIDTH, SPAN), fl),
    keys_t=((SPAN, WIDTH), bf),
    result=((WIDTH, SPAN), bf),
    hidden_low=((HID, SPAN), bf),
    grad_two=((WIDTH, SPAN), fl),
    middle_grad=((WIDTH, SPAN), fl),
    branch_low=((WIDTH, SPAN), bf),
    mixed_low=((WIDTH, SPAN), bf),
    triple_low=((3 * WIDTH, SPAN), bf),
    grad_one=((WIDTH, SPAN), fl),
    token_grad=((WIDTH, SPAN), bf),
)
WEIGHTS = dict(
    table=((2, TOK, HEADS * 128), fl),
    vec=((5 * WIDTH, 128), fl),
    w_in_t=((3 * WIDTH, WIDTH + 16), bf),
    w_in=((WIDTH, 3 * WIDTH), bf),
    w_out_t=((WIDTH, WIDTH + 16), bf),
    w_out=((WIDTH, WIDTH), bf),
    w_exp_t=((HID, WIDTH + 16), bf),
    w_exp=((WIDTH, HID), bf),
    w_con=((HID, WIDTH), bf),
    w_con_t=((WIDTH, HID), bf),
    acc_in=((4 * WIDTH, WIDTH + 16), fl),
    acc_exp=((HID, WIDTH + 16), fl),
    acc_con=((HID, WIDTH), fl),
    d_vec=((5 * WIDTH, 128), fl),
    d_tab=((TOK, HEADS * 128), fl),
    d_row=((48, 128), fl),
    bias_pad=((8, 384), fl),
)
GAIN_ONE, SHIFT_ONE, GAIN_TWO, SHIFT_TWO, CON_BIAS = (WIDTH * k for k in range(5))
ENDS = dict(
    vox=0, cot=0, f_in=0, f_out=0, f_exp=0, f_con=0, bias=0, vectors=0, related=0,
    take=0, give=0, pick=0, fill=0, out_res=0, out_tok=0, out_total=0,
)
SIGNALS = dict(
    own_sem=0, raw_sem=0, d_send=0, d_recv=0, w_send=0, w_recv=0, b_send=0, b_recv=0,
    o_sem=0, q_sem=0, r_send=0, r_recv=0, d_free=0, r_free=0, s1_send=0, s1_recv=0, s2_send=0, s2_recv=0,
    s3_send=0, s3_recv=0, s4_send=0, s4_recv=0, s0_send=0, s0_recv=0, s5_send=0, s5_recv=0,
    t_sem=0,
)
scale = 32 ** (-0.5)


def moves(crops, rows, length, share, peers_w):
    half = length // 2
    crew = half // share
    piece = share // peers_w
    part = 2 * TOK
    parts = rows // part
    return dict(
        bucket=((length, 128), bf),
        landed_zero=((half, 128), bf),
        half_sum=((half, 128), bf),
        landed=((crew - 1, share, 128), bf),
        partial_sum=((share, 128), bf),
        landed_two=((peers_w - 1, piece, 128), bf),
        total=((length, 128), bf),
        own=((SLOTS, 2, 2, rows, WIDTH), bf),
        raw=((2, 2, 2, rows, WIDTH), bf),
        send_d=((SLOTS, parts, 2, part, 2 * WIDTH), bf),
        halo_d=((DEPTH_SLOTS, parts, 2, part, 2 * WIDTH), bf),
        halo_w=((crops, parts, part, 2 * WIDTH), bf),
        send_w=((SLOTS, parts, part, 2 * WIDTH), bf),
        back_send=((SLOTS, parts, part, 2 * WIDTH), bf),
        back_recv=((crops + 1, parts, part, 2 * WIDTH), bf),
        keep_res=((SLOTS, 2, rows, WIDTH), bf),
        keep_tok=((SLOTS, 2, rows, WIDTH), bf),
        grid_ret=((SLOTS, parts, 2, part, 2 * WIDTH), bf),
        ret_recv=((RETURN_SLOTS + 1, parts, 2, part, 2 * WIDTH), bf),
        stage=((2, 2, 2, rows, WIDTH), bf),
    )


MOVES = moves(1, 2 * TOK, 32, 16, 1)


def forward_tasks(r, first_half, tokens_of, edge):
    tasks = []
    slots = [(k, hp) for k in range(PAIRS) for hp in range(3)]
    held = {}

    def vec(at, lanes=SPAN):
        return wide(r.vec[at : at + WIDTH, :], lanes)

    def fetch():
        rows = []
        for s in range(SUBS):
            rows = rows + tokens_of(s)
        moved = dot(jnp.concatenate(rows, axis=0), r.take[...])
        for s in range(SUBS):
            lanes = slice(LANES * s, LANES * s + LANES)
            at = 2 * WIDTH * s
            up = moved[at + WIDTH : at + 2 * WIDTH]
            r.x[:, lanes] = moved[at : at + WIDTH]
            r.up[:, lanes] = up
            r.up_low[:, lanes] = up.astype(bf)

    def norm_one():
        unit_vals, inverse = unit_norm(r.x[...])
        r.unit_one[...] = unit_vals
        r.inverse_one[...] = jnp.broadcast_to(inverse, (8, SPAN))
        r.entry_one[:WIDTH] = (unit_vals * vec(GAIN_ONE) + vec(SHIFT_ONE)).astype(bf)

    def project():
        triple = dot(r.w_in_t[...], r.entry_one[...]).astype(bf)
        r.query[...] = triple[:WIDTH]
        r.keys[...] = triple[WIDTH : 2 * WIDTH]
        r.values[...] = triple[2 * WIDTH :]

    def turn():
        r.keys_t[...] = r.keys[...].T
        r.values_t[...] = r.values[...].T

    def scores(t):
        k, hp = slots[t]
        held["s", t] = cross(r.keys_t, r.query, 128 * k, hp, first_half)

    def soft(t):
        k, hp = slots[t]
        pieces = held.pop(("s", t))
        wides = []
        for head in (2 * hp, 2 * hp + 1):
            which = edge if k == PAIRS - 1 else 0
            s = (
                pieces[head - 2 * hp] * (scale * LOG2E)
                + r.table[which, :, 128 * head : 128 * head + 128]
            )
            e = jnp.exp2(s - jnp.max(s, 0, keepdims=True))
            p = e * (1.0 / jnp.sum(e, 0, keepdims=True))
            r.probs[k, head] = p
            p_low = p.astype(bf)
            r.probs_low[k, head] = p_low
            wides.append(two_windows(p_low, first_half))
        held["p", t] = wides

    def mix(t):
        k, hp = slots[t]
        lanes = slice(128 * k, 128 * k + 128)
        r.mixed[64 * hp : 64 * hp + 64, lanes] = dot(
            two_heads(r.values, hp, lanes), jnp.concatenate(held.pop(("p", t)), axis=0)
        ).astype(bf)

    def join():
        r.x[...] = r.x[...] + dot(r.w_out_t[...], r.mixed[...])

    def norm_two():
        unit_vals, inverse = unit_norm(r.x[...])
        r.unit_two[...] = unit_vals
        r.inverse_two[...] = jnp.broadcast_to(inverse, (8, SPAN))
        r.entry_two[:WIDTH] = (unit_vals * vec(GAIN_TWO) + vec(SHIFT_TWO)).astype(bf)

    def gelu(s, part):
        def run():
            lanes = slice(LANES * s, LANES * s + LANES)
            rows = slice(HID // 2 * part, HID // 2 * part + HID // 2)
            hidden = dot(r.w_exp_t[rows], r.entry_two[:, lanes])
            twice = 1.0 + lax.erf(hidden * INV_SQRT2)
            r.active[rows, lanes] = (hidden * twice).astype(bf)
            r.slope[rows, lanes] = twice + hidden * (
                (2.0 * INV_SQRT2PI) * jnp.exp2(hidden * hidden * (-0.5 * LOG2E))
            )

        return run

    def contracted(s):
        def run():
            lanes = slice(LANES * s, LANES * s + LANES)
            r.result[:, lanes] = (
                r.x[:, lanes]
                + dot(r.w_con_t[...], r.active[:, lanes])
                + vec(CON_BIAS, LANES)
            ).astype(bf)

        return run

    tasks = tasks + [(340, fetch), (120, norm_one), (180, project), (80, turn)]
    for t in range(len(slots) + 1):
        if t == 0:
            tasks.append((30, lambda: scores(0)))
        if t + 1 < len(slots):
            tasks.append((30, lambda t=t: scores(t + 1)))
        if t < len(slots):
            tasks.append((40, lambda t=t: soft(t)))
        if t >= 1:
            tasks.append((30, lambda t=t: mix(t - 1)))

    tasks = tasks + [(100, join), (150, norm_two)]
    tasks = tasks + [(270, gelu(s, part)) for s in range(SUBS) for part in range(2)]
    tasks = tasks + [(130, contracted(s)) for s in range(SUBS)]
    return tasks


def backward_tasks(r, first_half):
    slots = [(k, hp) for k in range(PAIRS) for hp in range(3)]
    held = {}

    def vec(at):
        return wide(r.vec[at : at + WIDTH, :], SPAN)

    def hidden_back(s, part):
        def run():
            lanes = slice(LANES * s, LANES * s + LANES)
            rows = slice(HID // 2 * part, HID // 2 * part + HID // 2)
            r.hidden_low[rows, lanes] = (
                dot(r.w_con[rows], r.up_low[:, lanes]) * r.slope[rows, lanes]
            ).astype(bf)

        return run

    def expand_back(s):
        def run():
            lanes = slice(LANES * s, LANES * s + LANES)
            r.grad_two[:, lanes] = dot(r.w_exp[...], r.hidden_low[:, lanes])

        return run

    def norm_two_back():
        grad = r.up[...] + unit_back(
            r.grad_two[...], r.unit_two[...], r.inverse_two[0:1, :], vec(GAIN_TWO)
        )
        r.middle_grad[...] = grad
        r.branch_low[...] = grad.astype(bf)

    def out_back():
        r.mixed_low[...] = dot(r.w_out[...], r.branch_low[...]).astype(bf)

    def expand_sum(part):
        def run():
            rows = slice(HID // 2 * part, HID // 2 * part + HID // 2)
            r.acc_exp[rows, :] += dot_nt(r.hidden_low[rows, :], r.entry_two[...])

        return run

    def contract_sum(part):
        def run():
            rows = slice(HID // 2 * part, HID // 2 * part + HID // 2)
            r.acc_con[rows, :] += dot_nt(r.active[rows, :], r.up_low[...])

        return run

    def prob_back(t):
        k, hp = slots[t]
        held["g", t] = cross(r.values_t, r.mixed_low, 128 * k, hp, first_half)

    def score_back(t):
        k, hp = slots[t]
        pieces = held.pop(("g", t))
        wides = []
        for head in (2 * hp, 2 * hp + 1):
            p, g = r.probs[k, head], pieces[head - 2 * hp]
            s = p * (g - jnp.sum(g * p, 0, keepdims=True))
            r.d_tab[:, 128 * head : 128 * head + 128] += s
            wides.append(two_windows(s.astype(bf), first_half))
        held["s", t] = wides

    def query_back(t):
        k, hp = slots[t]
        lanes = slice(128 * k, 128 * k + 128)
        at = 64 * hp
        r.triple_low[at : at + 64, lanes] = (
            dot(two_heads(r.keys, hp, lanes), jnp.concatenate(held["s", t], axis=0)) * scale
        ).astype(bf)

    def keys_back(t):
        k, hp = slots[t]
        lanes = slice(128 * k, 128 * k + 128)
        at = WIDTH + 64 * hp
        wides = held.pop(("s", t))
        r.triple_low[at : at + 64, lanes] = (
            dot_nt(two_heads(r.query, hp, lanes), jnp.concatenate(wides, axis=1)) * scale
        ).astype(bf)

    def values_back(t):
        k, hp = slots[t]
        lanes = slice(128 * k, 128 * k + 128)
        at = 2 * WIDTH + 64 * hp
        probs = jnp.concatenate(
            [two_windows(r.probs_low[k, head], first_half) for head in (2 * hp, 2 * hp + 1)], axis=1
        )
        r.triple_low[at : at + 64, lanes] = dot_nt(
            two_heads(r.mixed_low, hp, lanes), probs
        ).astype(bf)

    def entry_back(s):
        def run():
            lanes = slice(LANES * s, LANES * s + LANES)
            r.grad_one[:, lanes] = dot(r.w_in[...], r.triple_low[:, lanes])

        return run

    def in_sum():
        r.acc_in[: 3 * WIDTH, :] += dot_nt(r.triple_low[...], r.entry_one[...])

    def out_sum():
        r.acc_in[3 * WIDTH :, :] += dot_nt(r.branch_low[...], r.mixed[...])

    def norm_one_back():
        r.token_grad[...] = (
            r.middle_grad[...]
            + unit_back(
                r.grad_one[...], r.unit_one[...], r.inverse_one[0:1, :], vec(GAIN_ONE)
            )
        ).astype(bf)

    def vector_sum():
        one, two = r.grad_one[...], r.grad_two[...]
        for place, term in enumerate(
            (one * r.unit_one[...], one, two * r.unit_two[...], two, r.up[...])
        ):
            r.d_vec[WIDTH * place : WIDTH * place + WIDTH, :] += fold(term)

    tasks = [(80, hidden_back(s, part)) for s in range(SUBS) for part in range(2)]
    tasks = tasks + [(130, expand_back(s)) for s in range(SUBS)]
    tasks = tasks + [(200, norm_two_back), (100, out_back)]
    sums = [(130, expand_sum(part)) for part in range(2)]
    sums = sums + [(130, contract_sum(part)) for part in range(2)]
    fine = []
    for t in range(len(slots) + 1):
        if t == 0:
            fine.append((30, lambda: prob_back(0)))
        if t + 1 < len(slots):
            fine.append((30, lambda t=t: prob_back(t + 1)))
        if t < len(slots):
            fine.append((20, lambda t=t: values_back(t)))
            fine.append((40, lambda t=t: score_back(t)))
        if t >= 1:
            fine.append((20, lambda t=t: query_back(t - 1)))
            fine.append((20, lambda t=t: keys_back(t - 1)))
    tasks = tasks + weave(fine, sums)
    tasks = tasks + [(110, entry_back(s)) for s in range(SUBS)]
    tasks = tasks + [(200, in_sum), (200, norm_one_back), (70, out_sum), (200, vector_sum)]
    return tasks


def block_kernel(*refs):
    r = SimpleNamespace()
    place = 0
    for group in (ENDS, WEIGHTS, ONCE, MOVES, SIGNALS):
        for name in group:
            setattr(r, name, refs[place])
            place += 1
    states = []
    for _ in range(2):
        state = SimpleNamespace(**vars(r))
        for name in BOTH:
            setattr(state, name, refs[place])
            place += 1
        states.append(state)
    crops, _, rows, width = r.vox.shape
    per_crop = rows // (2 * TOK)
    subs = rows // TOK
    steps = crops * per_crop
    depth, peers_d = lax.axis_index("depth"), lax.axis_size("depth")
    column, peers_w = lax.axis_index("wide"), lax.axis_size("wide")
    d_prev = {"depth": lax.rem(depth + peers_d - 1, peers_d)}
    d_next = {"depth": lax.rem(depth + 1, peers_d)}
    w_prev = {"wide": lax.rem(column + peers_w - 1, peers_w)}
    w_next = {"wide": lax.rem(column + 1, peers_w)}
    mesh_id = pl.DeviceIdType.MESH
    sources = (r.vox, r.cot)
    results = (r.out_res, r.out_tok)
    keeps = (r.keep_res, r.keep_tok)
    own, halo_d, halo_w = r.own, r.halo_d, r.halo_w

    def own_copy(c, a):
        slot = lax.rem(c, SLOTS)
        return pltpu.make_async_copy(
            sources[a].at[c, pl.ds(SHIFT, 2)], own.at[slot, a], r.own_sem.at[slot, a]
        )

    def raw_copy(c, a):
        slot = lax.rem(c, 2)
        return pltpu.make_async_copy(
            sources[a].at[c, pl.ds(0, SHIFT)], r.raw.at[slot, a], r.raw_sem.at[slot, a]
        )

    def depth_copy(c, u):
        slot = lax.rem(c, SLOTS)
        return pltpu.make_async_remote_copy(
            src_ref=r.send_d.at[slot, u],
            dst_ref=halo_d.at[lax.rem(c, DEPTH_SLOTS), u],
            send_sem=r.d_send.at[slot, u],
            recv_sem=r.d_recv.at[c, u],
            device_id=d_prev,
            device_id_type=mesh_id,
        )

    def pack_depth(c, u):
        slot = lax.rem(c, 2)
        for start, size, at in parts_of(u):
            for d in range(SHIFT):
                r.send_d[lax.rem(c, SLOTS), u, d, at : at + size, :] = jnp.concatenate(
                    [r.raw[slot, a, d, pl.ds(start, size), :] for a in range(2)], axis=1
                )

    def parts_of(u):
        first = pl.multiple_of(u * 2 * TOK + 16, 16)
        second = pl.multiple_of(lax.rem(u * 2 * TOK + 2 * TOK, rows), 16)
        return (first, 2 * TOK - 16, 0), (second, 16, 2 * TOK - 16)

    def pack_depth_whole(c):
        def one(u, carry):
            pack_depth(c, u)
            depth_copy(c, u).start()
            return carry

        for a in range(2):
            raw_copy(c, a).wait()
        lax.fori_loop(0, per_crop, one, 0)

    def wide_copy(c, u):
        slot = lax.rem(c, SLOTS)
        return pltpu.make_async_remote_copy(
            src_ref=r.send_w.at[slot, u],
            dst_ref=halo_w.at[c, u],
            send_sem=r.w_send.at[slot, u],
            recv_sem=r.w_recv.at[c, u],
            device_id=w_prev,
            device_id_type=mesh_id,
        )

    def back_copy(c, u):
        slot = lax.rem(c, SLOTS)
        return pltpu.make_async_remote_copy(
            src_ref=r.back_send.at[slot, u],
            dst_ref=r.back_recv.at[c, u],
            send_sem=r.b_send.at[slot, u],
            recv_sem=r.b_recv.at[c, u],
            device_id=w_next,
            device_id_type=mesh_id,
        )

    def return_copy(c, u):
        slot = lax.rem(c, SLOTS)
        return pltpu.make_async_remote_copy(
            src_ref=r.grid_ret.at[slot, u],
            dst_ref=r.ret_recv.at[lax.rem(c, RETURN_SLOTS), u],
            send_sem=r.r_send.at[slot, u],
            recv_sem=r.r_recv.at[c, u],
            device_id=d_next,
            device_id_type=mesh_id,
        )

    def keep_copy(c, a):
        slot = lax.rem(c, SLOTS)
        return pltpu.make_async_copy(
            keeps[a].at[slot], results[a].at[c, pl.ds(SHIFT, 2)], r.o_sem.at[slot, a]
        )

    def out_copy(c, a):
        slot = lax.rem(c, 2)
        return pltpu.make_async_copy(
            r.stage.at[slot, a], results[a].at[c, pl.ds(0, SHIFT)], r.q_sem.at[slot, a]
        )

    chips_d = peers_d // 2
    crew = lax.axis_size("dp") * chips_d
    core = lax.rem(depth, 2)
    place = lax.axis_index("dp") * chips_d + depth // 2
    twin = {"depth": depth + 1 - 2 * core}

    def mate(step):
        other = lax.rem(place + step, crew)
        return other, {"dp": other // chips_d, "depth": lax.rem(other, chips_d) * 2 + core}

    def across(step):
        other = lax.rem(column + step, peers_w)
        return other, {"wide": other}

    barrier = pltpu.get_barrier_semaphore()
    peers = [mate(step)[1] for step in range(1, crew)]
    peers = peers + [across(step)[1] for step in range(1, peers_w)]
    for peer in peers + [d_prev, d_next]:
        pl.semaphore_signal(barrier, inc=1, device_id=peer, device_id_type=mesh_id)
    pl.semaphore_wait(barrier, crew + peers_w)

    for c in range(2):
        for a in range(2):
            raw_copy(c, a).start()
    for c in range(SLOTS):
        for a in range(2):
            own_copy(c, a).start()
    pack_depth_whole(jnp.int32(0))
    for a in range(2):
        raw_copy(2, a).start()
    pack_depth_whole(jnp.int32(1))
    for a in range(2):
        raw_copy(3, a).start()

    for ref in (r.acc_in, r.acc_exp, r.acc_con, r.d_vec, r.d_tab, r.bias_pad):
        ref[...] = jnp.zeros_like(ref)
    for state in states:
        for ref in (state.entry_one, state.entry_two, state.mixed):
            ref[WIDTH:, :] = jnp.ones((16, SPAN), bf)
    r.back_recv[crops] = jnp.zeros(r.back_recv.shape[1:], bf)
    for ref in (r.w_in_t, r.w_out_t, r.w_exp_t):
        ref[:, WIDTH:] = jnp.zeros((ref.shape[0], 16), bf)
    r.w_in[...] = r.f_in[...].astype(bf)
    r.w_in_t[:, :WIDTH] = r.f_in[...].T.astype(bf)
    r.w_out[...] = r.f_out[...].astype(bf)
    r.w_out_t[:, :WIDTH] = r.f_out[...].T.astype(bf)
    r.w_exp[...] = (r.f_exp[...].astype(bf).astype(fl) * 0.5).astype(bf)
    r.w_exp_t[:, :WIDTH] = r.f_exp[...].T.astype(bf)
    r.w_con_t[...] = (r.f_con[...].astype(bf).astype(fl) * 0.5).astype(bf)
    r.w_con[...] = r.f_con[...].T.astype(bf)
    lane16 = lax.broadcasted_iota(jnp.int32, (64, 16), 1)
    for tile in range(r.vectors.shape[0]):
        spread = jnp.broadcast_to(r.vectors[tile : tile + 1, :], (128, 128)).T
        for part in range(2):
            chunk = spread[64 * part : 64 * part + 64]
            member, at = divmod(128 * tile + 64 * part, WIDTH)
            narrow = chunk[:, :16]
            high = narrow.astype(bf).astype(fl)
            middle = (narrow - high).astype(bf).astype(fl)
            column_parts = jnp.where(
                lane16 == 0,
                high,
                jnp.where(
                    lane16 == 1, middle, jnp.where(lane16 == 2, narrow - high - middle, 0.0)
                ),
            ).astype(bf)
            if member in (0, 1, 5, 6, 7):
                base = {0: GAIN_ONE, 1: SHIFT_ONE, 5: GAIN_TWO, 6: SHIFT_TWO, 7: CON_BIAS}[member]
                r.vec[base + at : base + at + 64, :] = chunk
            elif member == 2:
                r.w_in_t[at : at + 64, WIDTH:] = column_parts
            elif member == 3:
                r.w_in_t[2 * WIDTH + at : 2 * WIDTH + at + 64, WIDTH:] = column_parts
            elif member == 4:
                r.w_out_t[at : at + 64, WIDTH:] = column_parts
            else:
                base = WIDTH * (member - 8)
                r.w_exp_t[base + at : base + at + 64, WIDTH:] = column_parts

    related = r.related

    def chooser(places):
        return (
            lax.broadcasted_iota(jnp.int32, (384, 128), 0)
            == jnp.broadcast_to(places, (384, 128))
        ).astype(bf)

    def eight(block):
        return pl.ds(pl.multiple_of(8 * block, 8), 8)

    def thirds(v):
        high = v.astype(bf)
        rest = v - high.astype(fl)
        middle = rest.astype(bf)
        return jnp.concatenate([high, middle, (rest - middle.astype(fl)).astype(bf)], axis=0)

    def ends(v):
        return v[:8] + v[8:16] + v[16:24]

    def code(at, window, edge):
        last_d = (depth == peers_d - 1).astype(jnp.int32)
        last_w = (column == peers_w - 1).astype(jnp.int32)
        d, h, w = at // 16, lax.rem(at // 4, 4), lax.rem(at, 4)
        return (
            last_d * (d >= SHIFT).astype(jnp.int32) * 4
            + edge * (h >= SHIFT).astype(jnp.int32) * 2
            + last_w * window * (w >= SHIFT).astype(jnp.int32)
        )

    r.bias_pad[: r.bias.shape[0], : r.bias.shape[1]] = r.bias[...]
    bias_parts = thirds(r.bias_pad[...])

    def table_rows(block, carry):
        near = related[eight(block), :]
        found = [ends(dot(bias_parts, chooser(near[k : k + 1]))) for k in range(8)]
        lane = lax.broadcasted_iota(jnp.int32, (8, 128), 1)
        j = lax.broadcasted_iota(jnp.int32, (8, 128), 0) + 8 * block
        window, i = lane // TOK, lax.rem(lane, TOK)
        for edge in range(2):
            differ = code(i, window, edge) != code(j, window, edge)
            mask = jnp.where(differ, mask_fill, 0.0)
            for head in range(HEADS):
                values = jnp.concatenate([row[head : head + 1, :] for row in found], axis=0)
                r.table[edge, eight(block), 128 * head : 128 * head + 128] = (
                    values + mask
                ) * LOG2E
        return carry

    lax.fori_loop(0, TOK // 8, table_rows, 0)
    first_half = lax.broadcasted_iota(jnp.int32, (TOK, 128), 1) < TOK

    def starts(b):
        first = pl.multiple_of(b * TOK + 16, 16)
        second = pl.multiple_of(lax.rem(b * TOK + TOK, rows), 16)
        return first, second

    def kept(c, a, b):
        first, second = starts(b)
        slot = lax.rem(c, SLOTS)
        parts = []
        for d in range(2):
            parts.append(own[slot, a, d, pl.ds(first, 48), :])
            parts.append(own[slot, a, d, pl.ds(second, 16), :])
        return jnp.concatenate(parts, axis=0)

    def brought(c, b):
        u, there = edge_rows(b)
        slot = lax.rem(c, DEPTH_SLOTS)
        return jnp.concatenate([halo_d[slot, u, d, there, :] for d in range(2)], axis=0)

    def edge_rows(b):
        return b // 2, pl.ds(pl.multiple_of(lax.rem(b, 2) * TOK, TOK), TOK)

    def pack(c, b):
        u, there = edge_rows(b)
        source = jnp.minimum(c, crops - 1)
        near = jnp.concatenate(
            [dot(r.pick[...], kept(source, a, b)) for a in range(2)], axis=1
        )
        far = dot(r.pick[...], brought(source, b))
        r.send_w[lax.rem(c, SLOTS), u, there, :] = jnp.concatenate([near, far], axis=0).astype(
            bf
        )

    ahead_units = SLOTS * 2 * per_crop

    def place_of(g):
        g = g + ahead_units
        return g // per_crop - 2 * SLOTS, lax.rem(g, per_crop)

    def merge(g, s):
        c, u = place_of(g)
        b = SUBS * u + s
        first, second = starts(b)
        _, there = edge_rows(b)
        slot = lax.rem(c + 2 * SLOTS, SLOTS)
        arrived = r.back_recv[jnp.where(c >= 0, c, crops), u, there, :]
        for a in range(2):
            extra = dot(r.fill[...], arrived[:TOK // 2, WIDTH * a : WIDTH * a + WIDTH]).astype(bf)
            for d in range(2):
                for start, size, at in ((first, 48, 64 * d), (second, 16, 64 * d + 48)):
                    keeps[a][slot, d, pl.ds(start, size), :] = (
                        keeps[a][slot, d, pl.ds(start, size), :] + extra[at : at + size]
                    )
        extra = dot(r.fill[...], arrived[TOK // 2 :, :]).astype(bf)
        for d in range(2):
            r.grid_ret[slot, u, d, there, :] = (
                r.grid_ret[slot, u, d, there, :] + extra[TOK * d : TOK * d + TOK]
            )

    def unpack(g):
        c, u = place_of(g)
        slot = jnp.where(c >= 0, lax.rem(c + 2 * RETURN_SLOTS, RETURN_SLOTS), RETURN_SLOTS)
        to = lax.rem(c + 2 * SLOTS, 2)
        for start, size, at in parts_of(u):
            for d in range(SHIFT):
                both = r.ret_recv[slot, u, d, at : at + size, :]
                for a in range(2):
                    r.stage[to, a, d, pl.ds(start, size), :] = both[
                        :, WIDTH * a : WIDTH * a + WIDTH
                    ]

    def put_keep(a, c, b, low):
        first, second = starts(b)
        slot = lax.rem(c, SLOTS)
        placed = low.T
        for d in range(2):
            keeps[a][slot, d, pl.ds(first, 48), :] = placed[64 * d : 64 * d + 48]
            keeps[a][slot, d, pl.ds(second, 16), :] = placed[64 * d + 48 : 64 * d + 64]

    def moved_out(ref, give):
        rows_of = jnp.concatenate(
            [ref[:, LANES * s : LANES * s + LANES] for s in range(SUBS)], axis=0
        )
        return dot(rows_of, give[...]).astype(bf)

    def put_result(g, state):
        c, u = g // per_crop, lax.rem(g, per_crop)

        def run():
            moved = moved_out(state.result, state.give)
            for s in range(SUBS):
                mine = moved[WIDTH * s : WIDTH * s + WIDTH]
                state.edge_res[s] = mine[:, 2 * TOK :]
                put_keep(0, c, 2 * u + s, mine[:, : 2 * TOK])

        return run

    def put_gradient(g, state):
        g = g + SLOTS * per_crop
        c, u = g // per_crop, lax.rem(g, per_crop)

        def run():
            moved = moved_out(state.token_grad, state.give)
            slot = lax.rem(c, SLOTS)
            for s in range(SUBS):
                b = 2 * u + s
                mine = moved[WIDTH * s : WIDTH * s + WIDTH]
                put_keep(1, c, b, mine[:, : 2 * TOK])
                both = jnp.concatenate([state.edge_res[s], mine[:, 2 * TOK :]], axis=0).T
                there = slice(TOK * s, TOK * s + TOK)
                for d in range(2):
                    r.grid_ret[slot, u, d, there, :] = both[TOK * d : TOK * d + TOK]
                r.back_send[slot, u, there, :] = both[2 * TOK :]

        return run

    def forward_of(g, state):
        c, u = g // per_crop, lax.rem(g, per_crop)

        def tokens_of(s):
            b = 2 * u + s
            part, there = edge_rows(b)
            edges = halo_w[c, part, there, :].T
            others = brought(c, b).T
            return [
                jnp.concatenate(
                    [
                        kept(c, a, b).T,
                        others[WIDTH * a : WIDTH * a + WIDTH],
                        edges[WIDTH * a : WIDTH * a + WIDTH],
                    ],
                    axis=1,
                )
                for a in range(2)
            ]

        def ready(s):
            return lambda: pack(c + 1, 2 * u + s)

        def depth_ready():
            pack_depth(c + SLOTS, u)

        edge = (u == per_crop - 1).astype(jnp.int32)
        tasks = forward_tasks(state, first_half, tokens_of, edge)
        return tasks, [(80, ready(0)), (40, depth_ready), (80, ready(1))]

    def backward_of(g, state):
        def mended(s):
            return lambda: merge(g - MERGE_LAG, s)

        def returned():
            unpack(g - UNPACK_LAG)

        tasks = backward_tasks(state, first_half)
        return tasks, [(120, mended(0)), (60, returned), (120, mended(1))]

    def before(f, b):
        if f is not None:
            c, u = f // per_crop, lax.rem(f, per_crop)

            @pl.when(u == 0)
            def _():
                @pl.when(c + 1 < crops)
                def _():
                    for a in range(2):
                        own_copy(c + 1, a).wait()

                @pl.when(c + SLOTS < crops)
                def _():
                    for a in range(2):
                        raw_copy(c + SLOTS, a).wait()

            wide_copy(c, u).wait_recv()
            depth_copy(c, u).wait_send()

            @pl.when(c + 1 < crops)
            def _():
                depth_copy(c + 1, u).wait_recv()

            @pl.when(c >= SLOTS - 1)
            def _():
                wide_copy(c + 1 - SLOTS, u).wait_send()

        if b is not None:
            c_b, u_b = place_of(b)

            @pl.when((u_b == 0) & (c_b >= SLOTS))
            def _():
                for a in range(2):
                    keep_copy(c_b - SLOTS, a).wait()

            ready_to_merge(b - MERGE_LAG)
            ready_to_unpack(b - UNPACK_LAG)
            c_p, u_p = place_of(b - 1)

            @pl.when(c_p >= SLOTS)
            def _():
                back_copy(c_p - SLOTS, u_p).wait_send()
                return_copy(c_p - SLOTS, u_p).wait_send()

    def ready_to_merge(g):
        @pl.when(g >= 0)
        def _():
            back_copy(*place_of(g)).wait_recv()

    def ready_to_unpack(g):
        c, u = place_of(g)

        @pl.when(g >= 0)
        def _():
            return_copy(c, u).wait_recv()

        @pl.when((u == 0) & (c >= 2))
        def _():
            for a in range(2):
                out_copy(c - 2, a).wait()

    def after_merge(g):
        c, u = place_of(g)

        @pl.when(g >= 0)
        def _():
            send_return(c, u)

            @pl.when(u == per_crop - 1)
            def _():
                for a in range(2):
                    keep_copy(c, a).start()

    def after_unpack(g):
        c, u = place_of(g)

        @pl.when((g >= 0) & (u == per_crop - 1))
        def _():
            for a in range(2):
                out_copy(c, a).start()

            @pl.when(c + RETURN_SLOTS < crops)
            def _():
                pl.semaphore_signal(r.r_free, inc=1, device_id=d_prev, device_id_type=mesh_id)

    def send_return(c, u):
        @pl.when((u == 0) & (c >= RETURN_SLOTS))
        def _():
            pl.semaphore_wait(r.r_free, 1)

        return_copy(c, u).start()

    def after(f, b):
        if f is not None:
            c, u = f // per_crop, lax.rem(f, per_crop)

            @pl.when(c + 1 < crops)
            def _():
                wide_copy(c + 1, u).start()

            @pl.when(c + SLOTS < crops)
            def _():
                @pl.when((u == 0) & (c + SLOTS >= DEPTH_SLOTS))
                def _():
                    pl.semaphore_wait(r.d_free, 1)

                depth_copy(c + SLOTS, u).start()

            @pl.when((u == per_crop - 1) & (c + SLOTS < crops))
            def _():
                for a in range(2):
                    own_copy(c + SLOTS, a).start()

            @pl.when((u == per_crop - 1) & (c + SLOTS + 2 < crops))
            def _():
                for a in range(2):
                    raw_copy(c + SLOTS + 2, a).start()

            @pl.when((u == per_crop - 1) & (c + DEPTH_SLOTS < crops))
            def _():
                pl.semaphore_signal(r.d_free, inc=1, device_id=d_next, device_id_type=mesh_id)

        if b is not None:
            @pl.when(b >= 1)
            def _():
                back_copy((b - 1) // per_crop, lax.rem(b - 1, per_crop)).start()

            after_merge(b - MERGE_LAG)
            after_unpack(b - UNPACK_LAG)

    def tasks_of(f, b, forward_state, backward_state):
        ahead, behind, extras = [], [], []
        if f is not None:
            ahead, more = forward_of(f, forward_state)
            extras = extras + more
        if b is not None:
            behind, more = backward_of(b, backward_state)
            extras = weave(extras, more)
            puts = [
                (140, put_result(b, backward_state)),
                (200, put_gradient(b - 1, forward_state)),
            ]
            extras = weave(extras, puts)
        return weave(weave(behind, ahead), extras)

    def half_step(f, b, forward_state, backward_state):
        before(f, b)
        for _, task in tasks_of(f, b, forward_state, backward_state):
            task()
        after(f, b)

    for a in range(2):
        own_copy(0, a).wait()

    def first_pack(u, carry):
        depth_copy(0, u).wait_recv()
        for s in range(SUBS):
            pack(0, SUBS * u + s)
        wide_copy(0, u).start()
        return carry

    lax.fori_loop(0, per_crop, first_pack, 0)
    pack_depth_whole(jnp.int32(2))
    for a in range(2):
        raw_copy(4, a).start()
    half_step(jnp.int32(0), None, states[0], None)

    def two_steps(i, carry):
        pair = ((2 * i + 1, 2 * i), (2 * i + 2, 2 * i + 1))
        for f, b in pair:
            before(f, b)
        tasks = tasks_of(*pair[0], states[1], states[0])
        tasks = tasks + tasks_of(*pair[1], states[0], states[1])
        for _, task in tasks:
            task()
        for f, b in pair:
            after(f, b)
        return carry

    lax.fori_loop(0, steps // 2 - 1, two_steps, 0)
    half_step(jnp.int32(steps - 1), jnp.int32(steps - 2), states[1], states[0])
    half_step(None, jnp.int32(steps - 1), states[0], states[1])
    back_copy(crops - 1 - SLOTS, per_crop - 1).wait_send()
    return_copy(crops - 1 - SLOTS, per_crop - 1).wait_send()
    put_gradient(jnp.int32(steps - 1), states[1])()
    back_copy(crops - 1, per_crop - 1).start()

    bucket, landed, total, d_row = r.bucket, r.landed, r.total, r.d_row
    partial_sum, landed_two = r.partial_sum, r.landed_two
    extra = 18 * width
    for tile in range(12):
        acc, at = ((r.acc_in, 128 * tile), (r.acc_exp, 128 * (tile - 6)))[tile // 6]
        turned = acc[at : at + 128, :].T * (1.0, 0.5)[tile // 6]
        bucket[width * tile : width * tile + width, :] = turned[:width].astype(bf)
        d_row[tile : tile + 1, :] = turned[width : width + 1]
    for tile in range(6):
        bucket[width * (12 + tile) : width * (13 + tile), :] = (
            r.acc_con[128 * tile : 128 * tile + 128, :].T * 0.5
        ).astype(bf)
    for tile in range(8):
        size = min(128, 5 * width - 128 * tile)
        d_row[12 + tile : 13 + tile, :size] = jnp.sum(
            r.d_vec[128 * tile : 128 * tile + size, :].T, 0, keepdims=True
        )
    d_row[19:20, 64:] = jnp.zeros((1, 64), fl)

    def table_sums(block, carry):
        near = related[eight(block), :]
        held = r.d_tab[eight(block), :]
        for k in range(8):
            rows_k = jnp.concatenate(
                [held[k : k + 1, 128 * head : 128 * head + 128] for head in range(HEADS)]
                + [jnp.zeros((2, 128), fl)],
                axis=0,
            )
            carry = carry + dot_nt(thirds(rows_k), chooser(near[k : k + 1]))
        return carry

    sums = ends(lax.fori_loop(0, TOK // 8, table_sums, jnp.zeros((24, 384), fl)))
    for tile in range(3):
        d_row[24 + 8 * tile : 32 + 8 * tile, :] = sums[:, 128 * tile : 128 * tile + 128]
    d_row[20:24, :] = jnp.zeros((4, 128), fl)
    bucket[extra : extra + 48, :] = d_row[...].astype(bf)
    length = bucket.shape[0]
    if length > extra + 48:
        bucket[extra + 48 :, :] = jnp.zeros((length - extra - 48, 128), bf)

    half = length // 2
    share = half // crew
    piece = share // peers_w

    def span(start, size):
        return pl.ds(pl.multiple_of(start, 16), size)

    base = core * half

    def zero_copy():
        return pltpu.make_async_remote_copy(
            src_ref=bucket.at[span((1 - core) * half, half)],
            dst_ref=r.landed_zero,
            send_sem=r.s0_send,
            recv_sem=r.s0_recv,
            device_id=twin,
            device_id_type=mesh_id,
        )

    def first_copy(step):
        other, peer = mate(step)
        return pltpu.make_async_remote_copy(
            src_ref=r.half_sum.at[span(other * share, share)],
            dst_ref=landed.at[step - 1],
            send_sem=r.s1_send.at[step - 1],
            recv_sem=r.s1_recv.at[step - 1],
            device_id=peer,
            device_id_type=mesh_id,
        )

    def second_copy(step):
        other, peer = across(step)
        return pltpu.make_async_remote_copy(
            src_ref=partial_sum.at[span(other * piece, piece)],
            dst_ref=landed_two.at[step - 1],
            send_sem=r.s2_send.at[step - 1],
            recv_sem=r.s2_recv.at[step - 1],
            device_id=peer,
            device_id_type=mesh_id,
        )

    def spread(start, size, send, recv, peer):
        there = total.at[span(start, size)]
        return pltpu.make_async_remote_copy(
            src_ref=there,
            dst_ref=there,
            send_sem=send,
            recv_sem=recv,
            device_id=peer,
            device_id_type=mesh_id,
        )

    def third_copy(step, owner=None):
        owner = column if owner is None else owner
        return spread(
            base + place * share + owner * piece,
            piece,
            r.s3_send.at[step - 1],
            r.s3_recv.at[step - 1],
            across(step)[1],
        )

    def fourth_copy(step, owner=None):
        owner = place if owner is None else owner
        return spread(
            base + owner * share,
            share,
            r.s4_send.at[step - 1],
            r.s4_recv.at[step - 1],
            mate(step)[1],
        )

    def fifth_copy(owner):
        return spread(owner * half, half, r.s5_send, r.s5_recv, twin)

    def third_arrival(step):
        return third_copy(step, lax.rem(column + peers_w - step, peers_w))

    def fourth_arrival(step):
        return fourth_copy(step, lax.rem(place + crew - step, crew))

    zero_copy().start()
    last = crops - 1

    def last_merge(g, carry):
        ready_to_merge(g)
        for s in range(SUBS):
            merge(g, s)
        after_merge(g)
        return carry

    def last_unpack(g, carry):
        ready_to_unpack(g)
        unpack(g)
        after_unpack(g)
        return carry

    zero_copy().wait_recv()
    r.half_sum[...] = (
        bucket[span(base, half), :].astype(fl) + r.landed_zero[...].astype(fl)
    ).astype(bf)
    for step in range(1, crew):
        first_copy(step).start()
    lax.fori_loop(steps - MERGE_LAG, steps, last_merge, 0)
    lax.fori_loop(steps - UNPACK_LAG, steps - per_crop, last_unpack, 0)
    for step in range(1, crew):
        first_copy(step).wait_recv()
    summed = r.half_sum[span(place * share, share), :].astype(fl)
    for step in range(1, crew):
        summed = summed + landed[step - 1].astype(fl)
    partial_sum[...] = summed.astype(bf)
    for step in range(1, peers_w):
        second_copy(step).start()
    for step in range(1, peers_w):
        second_copy(step).wait_recv()
    summed = partial_sum[span(column * piece, piece), :].astype(fl)
    for step in range(1, peers_w):
        summed = summed + landed_two[step - 1].astype(fl)
    total[span(base + place * share + column * piece, piece), :] = summed.astype(bf)
    for step in range(1, peers_w):
        third_copy(step).start()
    lax.fori_loop(steps - per_crop, steps, last_unpack, 0)
    for step in range(1, peers_w):
        third_arrival(step).wait_recv()
    for step in range(1, crew):
        fourth_copy(step).start()
    for step in range(1, crew):
        fourth_arrival(step).wait_recv()
    fifth_copy(core).start()
    fifth_copy(1 - core).wait_recv()
    leave = pltpu.make_async_copy(total, r.out_total, r.t_sem)
    leave.start()
    leave.wait()
    zero_copy().wait_send()
    fifth_copy(core).wait_send()
    for step in range(1, crew):
        first_copy(step).wait_send()
        fourth_copy(step).wait_send()
    for step in range(1, peers_w):
        second_copy(step).wait_send()
        third_copy(step).wait_send()

    def close(c, carry):
        for a in range(2):
            keep_copy(c, a).wait()
        for u in range(per_crop):
            back_copy(c, u).wait_send()
            return_copy(c, u).wait_send()
        return carry

    lax.fori_loop(crops - SLOTS, crops, close, 0)

    def close_wide(c, carry):
        for u in range(per_crop):
            wide_copy(c, u).wait_send()
        return carry

    lax.fori_loop(crops + 1 - SLOTS, crops, close_wide, 0)
    for c in (last - 1, last):
        for a in range(2):
            out_copy(c, a).wait()


def block_call(voxels, cotangent, matrices, bias_table, vectors):
    crops, planes, rows, width = voxels.shape
    whole = pl.BlockSpec(memory_space=pltpu.VMEM)
    far = pl.BlockSpec(memory_space=pl.ANY)
    related = relative_index().T
    related = jnp.asarray(np.concatenate([related, related], axis=1), jnp.int32)
    consts = list(matrices) + [bias_table, vectors, related] + placement()
    sem = pltpu.SemaphoreType.DMA
    parts = rows // (2 * TOK)
    crew = lax.axis_size("dp") * lax.axis_size("depth") // 2
    peers_w = lax.axis_size("wide")
    unit_rows = 32 * crew * peers_w
    length = -(-(18 * width + 48) // unit_rows) * unit_rows
    share = length // (2 * crew)
    return pl.pallas_call(
        block_kernel,
        in_specs=[far, far] + [whole] * len(consts),
        out_specs=[far, far, far],
        out_shape=[
            jax.ShapeDtypeStruct(voxels.shape, bf),
            jax.ShapeDtypeStruct(voxels.shape, bf),
            jax.ShapeDtypeStruct((length, 128), bf),
        ],
        scratch_shapes=[
            pltpu.VMEM(*spec)
            for spec in list(WEIGHTS.values())
            + list(ONCE.values())
            + list(moves(crops, rows, length, share, peers_w).values())
        ]
        + [
            sem((SLOTS, 2)),
            sem((2, 2)),
            sem((SLOTS, parts)),
            sem((crops, parts)),
            sem((SLOTS, parts)),
            sem((crops, parts)),
            sem((SLOTS, parts)),
            sem((crops, parts)),
            sem((SLOTS, 2)),
            sem((2, 2)),
            sem((SLOTS, parts)),
            sem((crops, parts)),
            pltpu.SemaphoreType.REGULAR,
            pltpu.SemaphoreType.REGULAR,
            sem((crew - 1,)),
            sem((crew - 1,)),
            sem((peers_w - 1,)),
            sem((peers_w - 1,)),
            sem((peers_w - 1,)),
            sem((peers_w - 1,)),
            sem((crew - 1,)),
            sem((crew - 1,)),
            sem(()),
            sem(()),
            sem(()),
            sem(()),
            sem(()),
        ]
        + [pltpu.VMEM(*spec) for spec in list(BOTH.values()) * 2],
        compiler_params=pltpu.CompilerParams(
            vmem_limit_bytes=63 * 2**20, collective_id=0, has_side_effects=True
        ),
        name="block",
    )(voxels, cotangent, *consts)


def update_kernel(*refs):
    far_in, total_in, far_params, far_out, far_new = (
        refs[0:2], refs[2], refs[3:21], refs[21:23], refs[23:51],
    )
    norm_ref, held, total = refs[51], refs[52], refs[53]
    params, grads_kept, copies = refs[54:72], refs[72:78], refs[78:82]
    in_sem, out_sem, load_sem, total_sem, save_sem = refs[82:87]
    crops = far_in[0].shape[0]

    def fetch(a, c):
        return pltpu.make_async_copy(far_in[a].at[c], held.at[a, c], in_sem.at[a, c])

    def store(a, c):
        return pltpu.make_async_copy(held.at[a, c], far_out[a].at[c], out_sem.at[a, c])

    def load(k):
        return pltpu.make_async_copy(far_params[k], params[k], load_sem.at[k])

    def save(k, ref):
        return pltpu.make_async_copy(ref, far_new[k], save_sem.at[k])

    whole = pltpu.make_async_copy(total_in, total, total_sem)
    whole.start()
    for k in range(18):
        load(k).start()
    for c in range(crops):
        for a in range(2):
            fetch(a, c).start()
    width = WIDTH
    whole.wait()

    def slab(tile):
        return total[width * tile : width * tile + width, :].astype(fl)

    small = total[18 * width : 18 * width + 48, :].astype(fl)
    low_half = slab(4)
    grads = [
        jnp.concatenate([slab(k) for k in range(4)] + [low_half[:, :64]], axis=1),
        jnp.concatenate([low_half[:, 64:], slab(5)], axis=1),
        jnp.concatenate([slab(k) for k in range(6, 12)], axis=1),
        jnp.concatenate([slab(k) for k in range(12, 18)], axis=1),
    ]
    flat_bias = jnp.concatenate([small[k : k + 1] for k in range(12)], axis=1)
    flat_sum = jnp.concatenate([small[k : k + 1] for k in range(12, 20)], axis=1)

    def cut(flat, index):
        return flat[:, width * index : width * index + width]

    table = jnp.concatenate([small[24:32], small[32:40], small[40:48]], axis=1)
    grads.append(table[:HEADS, : params[4].shape[1]])
    flat = jnp.concatenate(
        [
            cut(flat_sum, 0), cut(flat_sum, 1), cut(flat_bias, 0), cut(flat_bias, 2),
            cut(flat_bias, 3), cut(flat_sum, 2), cut(flat_sum, 3), cut(flat_sum, 4),
            flat_bias[:, 4 * width : 8 * width],
        ],
        axis=1,
    )
    grads.append(
        jnp.concatenate([flat[:, 128 * k : 128 * k + 128] for k in range(18)], axis=0)
    )
    squares = jnp.zeros((1, 1), fl)
    for grad in grads:
        squares = squares + jnp.sum(
            jnp.sum(grad * grad, 0, keepdims=True), 1, keepdims=True
        )
    norm_value = jnp.sqrt(squares)
    norm_ref[...] = norm_value
    factor = jnp.minimum(1.0, clip_bound / (norm_value + 1e-06))
    for member in (2, 3, 0, 1, 4, 5):
        matrix = member < 4
        for k in range(3):
            load(6 * k + member).wait()
        clipped = grads[member] * factor
        first, second, fresh = adam_update(
            params[member][...],
            params[6 + member][...],
            params[12 + member][...],
            clipped,
            rate_matrix if matrix else rate_vector,
            weight_decay if matrix else 0.0,
        )
        grads_kept[member][...] = clipped
        params[6 + member][...] = first
        params[12 + member][...] = second
        params[member][...] = fresh
        if matrix:
            copies[member][...] = fresh.astype(bf)
            save(24 + member, copies[member]).start()
        for place, ref in enumerate(
            (grads_kept[member], params[6 + member], params[12 + member], params[member])
        ):
            save(4 * member + place, ref).start()
        for c in range(member * crops // 6, (member + 1) * crops // 6):
            for a in range(2):
                fetch(a, c).wait()
                store(a, c).start()
    for member in range(6):
        for place, ref in enumerate(
            (grads_kept[member], params[6 + member], params[12 + member], params[member])
        ):
            save(4 * member + place, ref).wait()
        if member < 4:
            save(24 + member, copies[member]).wait()
    for a in range(2):
        for c in range(crops):
            store(a, c).wait()


def update_call(result, token_grad, total, params):
    whole = pl.BlockSpec(memory_space=pltpu.VMEM)
    far = pl.BlockSpec(memory_space=pl.ANY)
    shapes = []
    for member in range(6):
        shapes = shapes + [jax.ShapeDtypeStruct(params[member].shape, fl)] * 4
    for member in range(4):
        shapes.append(jax.ShapeDtypeStruct(params[member].shape, bf))
    shapes.append(jax.ShapeDtypeStruct((1, 1), fl))
    big = jax.ShapeDtypeStruct(result.shape, bf)
    sem = pltpu.SemaphoreType.DMA
    return pl.pallas_call(
        update_kernel,
        in_specs=[far] * 21,
        out_specs=[far] * 30 + [whole],
        out_shape=[big, big] + shapes,
        scratch_shapes=[pltpu.VMEM((2,) + result.shape, bf), pltpu.VMEM(total.shape, bf)]
        + [pltpu.VMEM(p.shape, fl) for p in params]
        + [pltpu.VMEM(p.shape, fl) for p in params[:6]]
        + [pltpu.VMEM(p.shape, bf) for p in params[:4]]
        + [sem((2, result.shape[0]))] * 2
        + [sem((18,)), sem(()), sem((28,))],
        compiler_params=pltpu.CompilerParams(vmem_limit_bytes=56 * 2**20),
        name="update",
    )(result, token_grad, total, *params)


def local(
    voxels,
    cotangent,
    project_in,
    project_out,
    expand,
    contract,
    bias_table,
    vectors,
    project_in_first,
    project_out_first,
    expand_first,
    contract_first,
    bias_table_first,
    vectors_first,
    project_in_second,
    project_out_second,
    expand_second,
    contract_second,
    bias_table_second,
    vectors_second,
):
    batches, planes, height, breadth, width = voxels.shape
    flat = (batches, planes, height * breadth, width)
    result, token_grad, total = block_call(
        voxels.reshape(flat),
        cotangent.reshape(flat),
        (project_in, project_out, expand, contract.T),
        bias_table,
        vectors.reshape(-1, 128),
    )
    params = [
        project_in,
        project_out,
        expand,
        contract.T,
        bias_table,
        vectors.reshape(-1, 128),
        project_in_first,
        project_out_first,
        expand_first,
        contract_first.T,
        bias_table_first,
        vectors_first.reshape(-1, 128),
        project_in_second,
        project_out_second,
        expand_second,
        contract_second.T,
        bias_table_second,
        vectors_second.reshape(-1, 128),
    ]
    done = update_call(result, token_grad, total, params)
    outs = list(done[2:30])
    for place in range(20, 24):
        outs[place] = outs[place].reshape(-1)
    for place in (12, 13, 14, 15, 27):
        outs[place] = outs[place].T
    return (
        (done[0].reshape(voxels.shape), done[1].reshape(voxels.shape))
        + tuple(outs)
        + (done[30].reshape(()),)
    )


def solution(mesh):
    split = P("dp", "depth", None, "wide", None)
    return jax.shard_map(
        local,
        mesh=mesh,
        in_specs=(split,) * 2 + (P(),) * 18,
        out_specs=(split,) * 2 + (P(),) * 29,
        check_vma=False,
    )
```

time: 275 us -> 226 us (0.82)
  Pallas kernels: 263 us -> 225 us
  other arithmetic: 5.3 us -> 0 us
  local copies, waits for them, and re-layouts: 5.24 us -> 0 us
    pallas_call x1, Pallas kernels: 242 us -> 207 us  [block_call(): pl.pallas_call(block_kernel, in_specs=[far, far] + [whole] * len(consts),...]
    pallas_call x4 -> x0, other arithmetic: 5.3 us -> none  [update_call(): pl.pallas_call(update_kernel, in_specs=[far, far, whole] + [whole] * 18,...]
    reshape x3 -> x0, local copies, waits for them, and re-layouts: 3.93 us -> none  [the longest x1 1.31 us: local(): vectors_first.reshape(1, -1)]
    pallas_call x1, Pallas kernels: 20.9 us -> 18 us  [update_call(): pl.pallas_call(update_kernel, in_specs=[far] * 21, out_specs=[far] * 30 +...]
where the time goes in v4:
time: 226 us
  Pallas kernels  225 us (100%)
    pallas_call x1, Pallas kernels, block_call(): pl.pallas_call(block_kernel, in_specs=[far, far] + [whole] * len(consts),...  207 us
    pallas_call x1, Pallas kernels, update_call(): pl.pallas_call(update_kernel, in_specs=[far] * 21, out_specs=[far] * 30 +...  18 us

profile of v4, /device:TPU:1, one launch (start us, length us, event | category | flops | bytes accessed | tf_op | source)
XLA Modules:
  0.0 225.7 jit_solution(14587968144468178726)
XLA Ops:
  0.7 206.9 %block.1 = (bf16[8,4,512,192]{3,2,1,0:T(8,128)(2,1)}, bf16[8,4,512,192]{3,2,1,0:T(8,128)(2,1)}, bf16[3584,128]{1,0:T(8,128)(2,1)}) custom-call(bf16[8,4,512,192]{3,2,1,0:T(8,128)(2,1)} %bitcast.20, bf16[8,4,512,192]{3,2,1,0:T(8,128)(2,1)} %bitcast.21, f32[192,576]{1,0:T(8,128)} %refs_3_.3, f32[192,192]{1,0:T(8,128)} %refs_4_.3, f32[192,768]{1,0:T(8,128)} %refs_5_.1, ...), custom_call_target="tpu_custom_call" | custom-call | tf_op jit(solution)/shard_map/block/pallas_call | solution.py:1345
  207.5 18.0 %update.1 = (bf16[8,4,512,192]{3,2,1,0:T(8,128)(2,1)}, bf16[8,4,512,192]{3,2,1,0:T(8,128)(2,1)}, f32[192,576]{1,0:T(8,128)}, f32[192,576]{1,0:T(8,128)}, f32[192...) custom-call(bf16[8,4,512,192]{3,2,1,0:T(8,128)(2,1)} %get-tuple-elem, ...), custom_call_target="tpu_custom_call" | custom-call | tf_op jit(solution)/shard_map/update/pallas_call | solution.py:1517

commit v5 on v4

--- a/solution.py
+++ b/solution.py
@@ -171,8 +171,8 @@
 SLOTS = 3
 DEPTH_SLOTS = 5
 RETURN_SLOTS = 3
-MERGE_LAG = 5
-UNPACK_LAG = 9
+MERGE_LAG = 4
+UNPACK_LAG = 8
 BOTH = dict(
     up=((WIDTH, SPAN), fl),
     up_low=((WIDTH, SPAN), bf),
@@ -371,20 +371,20 @@
 
         return run
 
-    tasks = tasks + [(340, fetch), (120, norm_one), (180, project), (80, turn)]
+    tasks = tasks + [(360, fetch), (97, norm_one), (443, project), (106, turn)]
     for t in range(len(slots) + 1):
         if t == 0:
-            tasks.append((30, lambda: scores(0)))
+            tasks.append((31, lambda: scores(0)))
         if t + 1 < len(slots):
-            tasks.append((30, lambda t=t: scores(t + 1)))
+            tasks.append((131, lambda t=t: scores(t + 1)))
         if t < len(slots):
-            tasks.append((40, lambda t=t: soft(t)))
+            tasks.append((61, lambda t=t: soft(t)))
         if t >= 1:
-            tasks.append((30, lambda t=t: mix(t - 1)))
-
-    tasks = tasks + [(100, join), (150, norm_two)]
-    tasks = tasks + [(270, gelu(s, part)) for s in range(SUBS) for part in range(2)]
-    tasks = tasks + [(130, contracted(s)) for s in range(SUBS)]
+            tasks.append((47, lambda t=t: mix(t - 1)))
+
+    tasks = tasks + [(264, join), (93, norm_two)]
+    tasks = tasks + [(206, gelu(s, part)) for s in range(SUBS) for part in range(2)]
+    tasks = tasks + [(207, contracted(s)) for s in range(SUBS)]
     return tasks
 
 
@@ -507,26 +507,26 @@
         ):
             r.d_vec[WIDTH * place : WIDTH * place + WIDTH, :] += fold(term)
 
-    tasks = [(80, hidden_back(s, part)) for s in range(SUBS) for part in range(2)]
-    tasks = tasks + [(130, expand_back(s)) for s in range(SUBS)]
-    tasks = tasks + [(200, norm_two_back), (100, out_back)]
-    sums = [(130, expand_sum(part)) for part in range(2)]
-    sums = sums + [(130, contract_sum(part)) for part in range(2)]
+    tasks = [(96, hidden_back(s, part)) for s in range(SUBS) for part in range(2)]
+    tasks = tasks + [(117, expand_back(s)) for s in range(SUBS)]
+    tasks = tasks + [(738, norm_two_back), (76, out_back)]
+    sums = [(132, expand_sum(part)) for part in range(2)]
+    sums = sums + [(134, contract_sum(part)) for part in range(2)]
     fine = []
     for t in range(len(slots) + 1):
         if t == 0:
-            fine.append((30, lambda: prob_back(0)))
+            fine.append((27, lambda: prob_back(0)))
         if t + 1 < len(slots):
-            fine.append((30, lambda t=t: prob_back(t + 1)))
+            fine.append((89, lambda t=t: prob_back(t + 1)))
         if t < len(slots):
-            fine.append((20, lambda t=t: values_back(t)))
-            fine.append((40, lambda t=t: score_back(t)))
+            fine.append((17, lambda t=t: values_back(t)))
+            fine.append((52, lambda t=t: score_back(t)))
         if t >= 1:
-            fine.append((20, lambda t=t: query_back(t - 1)))
-            fine.append((20, lambda t=t: keys_back(t - 1)))
+            fine.append((12, lambda t=t: query_back(t - 1)))
+            fine.append((21, lambda t=t: keys_back(t - 1)))
     tasks = tasks + weave(fine, sums)
-    tasks = tasks + [(110, entry_back(s)) for s in range(SUBS)]
-    tasks = tasks + [(200, in_sum), (200, norm_one_back), (70, out_sum), (200, vector_sum)]
+    tasks = tasks + [(99, entry_back(s)) for s in range(SUBS)]
+    tasks = tasks + [(136, in_sum), (170, norm_one_back), (44, out_sum), (502, vector_sum)]
     return tasks
 
 
@@ -681,9 +681,6 @@
     pack_depth_whole(jnp.int32(0))
     for a in range(2):
         raw_copy(2, a).start()
-    pack_depth_whole(jnp.int32(1))
-    for a in range(2):
-        raw_copy(3, a).start()
 
     for ref in (r.acc_in, r.acc_exp, r.acc_con, r.d_vec, r.d_tab, r.bias_pad):
         ref[...] = jnp.zeros_like(ref)
@@ -779,7 +776,6 @@
                 ) * LOG2E
         return carry
 
-    lax.fori_loop(0, TOK // 8, table_rows, 0)
     first_half = lax.broadcasted_iota(jnp.int32, (TOK, 128), 1) < TOK
 
     def starts(b):
@@ -926,7 +922,7 @@
 
         edge = (u == per_crop - 1).astype(jnp.int32)
         tasks = forward_tasks(state, first_half, tokens_of, edge)
-        return tasks, [(80, ready(0)), (40, depth_ready), (80, ready(1))]
+        return tasks, [(88, ready(0)), (17, depth_ready), (61, ready(1))]
 
     def backward_of(g, state):
         def mended(s):
@@ -936,7 +932,7 @@
             unpack(g - UNPACK_LAG)
 
         tasks = backward_tasks(state, first_half)
-        return tasks, [(120, mended(0)), (60, returned), (120, mended(1))]
+        return tasks, [(363, mended(0)), (21, returned), (153, mended(1))]
 
     def before(f, b):
         if f is not None:
@@ -1077,8 +1073,8 @@
             behind, more = backward_of(b, backward_state)
             extras = weave(extras, more)
             puts = [
-                (140, put_result(b, backward_state)),
-                (200, put_gradient(b - 1, forward_state)),
+                (128, put_result(b, backward_state)),
+                (105, put_gradient(b - 1, forward_state)),
             ]
             extras = weave(extras, puts)
         return weave(weave(behind, ahead), extras)
@@ -1100,43 +1096,86 @@
         return carry
 
     lax.fori_loop(0, per_crop, first_pack, 0)
+    pack_depth_whole(jnp.int32(1))
+    for a in range(2):
+        raw_copy(3, a).start()
+    lax.fori_loop(0, TOK // 8, table_rows, 0)
     pack_depth_whole(jnp.int32(2))
     for a in range(2):
         raw_copy(4, a).start()
     half_step(jnp.int32(0), None, states[0], None)
 
     def two_steps(i, carry):
-        pair = ((2 * i + 1, 2 * i), (2 * i + 2, 2 * i + 1))
-        for f, b in pair:
-            before(f, b)
-        tasks = tasks_of(*pair[0], states[1], states[0])
-        tasks = tasks + tasks_of(*pair[1], states[0], states[1])
-        for _, task in tasks:
-            task()
-        for f, b in pair:
-            after(f, b)
+        half_step(2 * i + 1, 2 * i, states[1], states[0])
+        half_step(2 * i + 2, 2 * i + 1, states[0], states[1])
         return carry
 
     lax.fori_loop(0, steps // 2 - 1, two_steps, 0)
     half_step(jnp.int32(steps - 1), jnp.int32(steps - 2), states[1], states[0])
-    half_step(None, jnp.int32(steps - 1), states[0], states[1])
+    bucket, d_row = r.bucket, r.d_row
+
+    def expand_rows(tile):
+        def run():
+            turned = r.acc_exp[128 * tile : 128 * tile + 128, :].T * 0.5
+            bucket[width * (6 + tile) : width * (7 + tile), :] = turned[:width].astype(bf)
+            d_row[6 + tile : 7 + tile, :] = turned[width : width + 1]
+
+        return run
+
+    def contract_rows(tile):
+        def run():
+            bucket[width * (12 + tile) : width * (13 + tile), :] = (
+                r.acc_con[128 * tile : 128 * tile + 128, :].T * 0.5
+            ).astype(bf)
+
+        return run
+
+    table_total = [jnp.zeros((24, 384), fl)]
+
+    def table_sums(block):
+        def run():
+            near = related[8 * block : 8 * block + 8, :]
+            held = r.d_tab[8 * block : 8 * block + 8, :]
+            for k in range(8):
+                rows_k = jnp.concatenate(
+                    [held[k : k + 1, 128 * head : 128 * head + 128] for head in range(HEADS)]
+                    + [jnp.zeros((2, 128), fl)],
+                    axis=0,
+                )
+                table_total[0] = table_total[0] + dot_nt(
+                    thirds(rows_k), chooser(near[k : k + 1])
+                )
+
+        return run
+
+    closing = [(300, table_sums(block)) for block in range(TOK // 8)]
+    closing = weave(
+        closing,
+        [(40, expand_rows(tile)) for tile in range(6)]
+        + [(40, contract_rows(tile)) for tile in range(6)],
+    )
+    last_unit = jnp.int32(steps - 1)
+    before(None, last_unit)
+    behind, more = backward_of(last_unit, states[1])
+    more = weave(
+        more, [(140, put_result(last_unit, states[1])), (200, put_gradient(last_unit - 1, states[0]))]
+    )
+    tail = 6
+    for _, task in weave(behind[:-tail], more) + weave(behind[-tail:], closing):
+        task()
+    after(None, last_unit)
     back_copy(crops - 1 - SLOTS, per_crop - 1).wait_send()
     return_copy(crops - 1 - SLOTS, per_crop - 1).wait_send()
     put_gradient(jnp.int32(steps - 1), states[1])()
     back_copy(crops - 1, per_crop - 1).start()
 
-    bucket, landed, total, d_row = r.bucket, r.landed, r.total, r.d_row
+    landed, total = r.landed, r.total
     partial_sum, landed_two = r.partial_sum, r.landed_two
     extra = 18 * width
-    for tile in range(12):
-        acc, at = ((r.acc_in, 128 * tile), (r.acc_exp, 128 * (tile - 6)))[tile // 6]
-        turned = acc[at : at + 128, :].T * (1.0, 0.5)[tile // 6]
+    for tile in range(6):
+        turned = r.acc_in[128 * tile : 128 * tile + 128, :].T
         bucket[width * tile : width * tile + width, :] = turned[:width].astype(bf)
         d_row[tile : tile + 1, :] = turned[width : width + 1]
-    for tile in range(6):
-        bucket[width * (12 + tile) : width * (13 + tile), :] = (
-            r.acc_con[128 * tile : 128 * tile + 128, :].T * 0.5
-        ).astype(bf)
     for tile in range(8):
         size = min(128, 5 * width - 128 * tile)
         d_row[12 + tile : 13 + tile, :size] = jnp.sum(
@@ -1144,19 +1183,7 @@
         )
     d_row[19:20, 64:] = jnp.zeros((1, 64), fl)
 
-    def table_sums(block, carry):
-        near = related[eight(block), :]
-        held = r.d_tab[eight(block), :]
-        for k in range(8):
-            rows_k = jnp.concatenate(
-                [held[k : k + 1, 128 * head : 128 * head + 128] for head in range(HEADS)]
-                + [jnp.zeros((2, 128), fl)],
-                axis=0,
-            )
-            carry = carry + dot_nt(thirds(rows_k), chooser(near[k : k + 1]))
-        return carry
-
-    sums = ends(lax.fori_loop(0, TOK // 8, table_sums, jnp.zeros((24, 384), fl)))
+    sums = ends(table_total[0])
     for tile in range(3):
         d_row[24 + 8 * tile : 32 + 8 * tile, :] = sums[:, 128 * tile : 128 * tile + 128]
     d_row[20:24, :] = jnp.zeros((4, 128), fl)

time: 226 us -> 217 us (0.960)
  Pallas kernels: 225 us -> 216 us
    pallas_call x1, Pallas kernels: 207 us -> 198 us  [block_call(): pl.pallas_call(block_kernel, in_specs=[far, far] + [whole] * len(consts),...]
where the time goes in v5:
time: 217 us
  Pallas kernels  216 us (100%)
    pallas_call x1, Pallas kernels, block_call(): pl.pallas_call(block_kernel, in_specs=[far, far] + [whole] * len(consts),...  198 us
    pallas_call x1, Pallas kernels, update_call(): pl.pallas_call(update_kernel, in_specs=[far] * 21, out_specs=[far] * 30 +...  18 us

profile of v5, /device:TPU:1, one launch (start us, length us, event | category | flops | bytes accessed | tf_op | source)
XLA Modules:
  0.0 216.8 jit_solution(12061833594528925320)
XLA Ops:
  0.7 197.9 %block.1 = (bf16[8,4,512,192]{3,2,1,0:T(8,128)(2,1)}, bf16[8,4,512,192]{3,2,1,0:T(8,128)(2,1)}, bf16[3584,128]{1,0:T(8,128)(2,1)}) custom-call(bf16[8,4,512,192]{3,2,1,0:T(8,128)(2,1)} %bitcast.20, bf16[8,4,512,192]{3,2,1,0:T(8,128)(2,1)} %bitcast.21, f32[192,576]{1,0:T(8,128)} %refs_3_.3, f32[192,192]{1,0:T(8,128)} %refs_4_.3, f32[192,768]{1,0:T(8,128)} %refs_5_.1, ...), custom_call_target="tpu_custom_call" | custom-call | tf_op jit(solution)/shard_map/block/pallas_call | solution.py:1372
  198.6 18.0 %update.1 = (bf16[8,4,512,192]{3,2,1,0:T(8,128)(2,1)}, bf16[8,4,512,192]{3,2,1,0:T(8,128)(2,1)}, f32[192,576]{1,0:T(8,128)}, f32[192,576]{1,0:T(8,128)}, f32[192...) custom-call(bf16[8,4,512,192]{3,2,1,0:T(8,128)(2,1)} %get-tuple-elem, ...), custom_call_target="tpu_custom_call" | custom-call | tf_op jit(solution)/shard_map/update/pallas_call | solution.py:1544
